TPU v7x, 32 devices: a whole 2x2x4 slice. The times are simulated.
32 devices in a mesh: dp: 2 (over x), label: 16 (over z, y, core).
Axes of the slice: x: 2, y: 2, z: 4, core: 2. Of those that a mesh axis runs over, the one named last changes fastest.
Arguments:
- embed: bfloat16 [2048, 768], P('dp'), may hold values from -6 to 6
- weight: bfloat16 [16384, 768], P('label'), may hold values from -0.21875 to 0.21875
- bias: bfloat16 [16384], P('label'), may hold values from -4 to 4
- beam: int32 [16, 38], P('dp'), may hold values from 0 to 127, as said below
- positives: int32 [2048, 8], P('dp'), may hold values from 0 to 16383, as said below
Outputs:
- row_grads: bfloat16 [2048, 768], P(('dp', 'label'))
- label_grads: bfloat16 [16384, 768], P(('label', 'dp'))
Inputs may be any that keep to these rules, and one draw needn't show every extreme that they name: `beam`: the label device of cluster c is c // 8. A block's 38 clusters are distinct. For the 8 blocks of one data shard, one label device holds exactly 8 of every block's clusters, and every other label device holds exactly 2 clusters of every block. `positives`: each is a label of one of the beam clusters of the instance's own block; repeats may occur.
All inputs are finite; a program needn't handle non-finite values.
Results may differ from a plain program's by a relative error of at most 0.015.
Values may be sent and summed in bfloat16 or wider, within the bound.
No kernel may reach another device: no remote copies, remote signals or barrier semaphores. Data moves between devices by JAX's collectives and lax.ppermute only.
A program may use at most 64 MiB of HBM per device.

v0:
```python
import jax
import jax.numpy as jnp
from jax import lax
from jax.sharding import PartitionSpec as P

INST_BLOCK = 128
CLUSTER = 128
HOT = 8


grad_scale = 0.125


def on_device(embed, weight, bias, beam, positives):
    position = lax.axis_index("label")
    blk_dev = beam.shape[0]
    row_count = embed.shape[0]
    features = embed.shape[1]
    pos_count = positives.shape[1]
    cl_dev = weight.shape[0] // CLUSTER
    blocks = embed.reshape(blk_dev, INST_BLOCK, features)
    cluster_slabs = weight.reshape(cl_dev, CLUSTER, features)
    biases = bias.reshape(cl_dev, CLUSTER)
    owned = beam // cl_dev == position
    slot_rank = jnp.cumsum(owned.astype(jnp.int32), axis=1) - 1
    slot_numbers = jnp.arange(HOT, dtype=jnp.int32)
    picked = owned[:, None, :] & (slot_rank[:, None, :] == slot_numbers[None, :, None])
    usable = jnp.any(picked, axis=2)
    local_ids = jnp.sum(jnp.where(picked, beam[:, None, :] % cl_dev, 0), axis=2)
    gathered = cluster_slabs[local_ids]
    bias_rows = biases[local_ids].astype(jnp.float32)
    scores = (
        jnp.einsum("bnd,bjkd->bnjk", blocks, gathered, preferred_element_type=jnp.float32)
        + bias_rows[:, None, :, :]
    )
    cluster_ids = position * cl_dev + local_ids
    wanted = positives.reshape(blk_dev, INST_BLOCK, pos_count)
    hits_cluster = (wanted[:, :, :, None] // CLUSTER == cluster_ids[:, None, None, :]).astype(
        jnp.float32
    )
    hits_label = (
        wanted[:, :, :, None] % CLUSTER == jnp.arange(CLUSTER, dtype=jnp.int32)[None, None, None, :]
    ).astype(jnp.float32)
    target = jnp.minimum(jnp.einsum("bnpj,bnpk->bnjk", hits_cluster, hits_label), 1.0)
    slopes = jnp.where(
        usable[:, None, :, None], (jax.nn.sigmoid(scores) - target) * grad_scale, 0.0
    ).astype(jnp.bfloat16)
    placing = (
        (local_ids[:, :, None] == jnp.arange(cl_dev, dtype=jnp.int32)[None, None, :])
        & usable[:, :, None]
    ).astype(jnp.bfloat16)
    spread = jnp.einsum(
        "bjc,bnjk->bnck", placing, slopes, preferred_element_type=jnp.float32
    ).astype(jnp.bfloat16)
    spread = spread.reshape(row_count, cl_dev * CLUSTER)
    row_part = jnp.dot(spread, weight, preferred_element_type=jnp.float32)
    label_part = lax.dot_general(
        spread, embed, (((0,), (0,)), ((), ())), preferred_element_type=jnp.float32
    )
    row_sums = lax.psum_scatter(row_part, "label", scatter_dimension=0, tiled=True)
    label_sums = lax.psum_scatter(
        label_part.astype(jnp.bfloat16), "dp", scatter_dimension=0, tiled=True
    )
    return (row_sums.astype(jnp.bfloat16), label_sums)


def solution(mesh):
    in_specs = (P("dp", None), P("label", None), P("label"), P("dp", None), P("dp", None))
    out_specs = (P(("dp", "label"), None), P(("label", "dp"), None))
    return jax.shard_map(
        on_device, mesh=mesh, in_specs=in_specs, out_specs=out_specs, check_vma=False
    )
```

profile of v0, /device:TPU:0, one launch (start us, length us, event | category | flops | bytes accessed | tf_op | source)
XLA Modules:
  0.0 148.9 jit_solution(9437653930580948089)
XLA Ops:
  7.2 0.0 copy-start
  7.2 0.0 reduce-scatter.3.cloned.1.call-start
  7.2 0.8 fusion.35
  8.0 0.2 reduce_window_sum.11
  8.2 0.7 add_select_fusion.2
  8.9 0.2 fusion.21
  9.1 0.2 select_reduce_fusion
  9.4 0.1 reshape.146
  9.5 0.0 copy-done
  9.5 0.0 copy-start.3
  9.5 7.0 %gather_fusion = bf16[64,128,768]{2,1,0:T(8,128)(2,1)} fusion(bf16[8,128,768]{2,1,0:T(8,128)(2,1)S(1)} %bitcast.72, s32[1024]{0:T(1024)S(1)} %pad_clamp_fusion), kind=kCustom, calls=%fused_computation | custom fusion | bytes 25166080 | tf_op jit(solution)/shard_map/gather | solution.py:30
  16.5 0.0 copy-done.3
  16.5 9.9 %fusion.37 = f32[8,8,128,128]{3,2,1,0:T(8,128)} fusion(bf16[8,8,128,768]{3,2,1,0:T(8,128)(2,1)} %bitcast.73, bf16[8,128,768,1]{2,1,3,0:T(8,128)(2,1)S(1)} %bitcast.75), kind=kOutput, calls=%fused_computation.56 | convolution fusion | flops 1610612736 | bytes 18350080 | tf_op jit(solution)/shard_map/bnd,bjkd->bnjk/dot_general | solution.py:33
  26.4 0.0 copy-start.1
  26.4 0.0 copy-start.2
  26.4 5.4 %copy.11 = f32[8,8,128,128]{2,1,3,0:T(8,128)} copy(f32[8,8,128,128]{3,2,1,0:T(8,128)} %fusion.37) | data formatting | bytes 8388608 | tf_op jit(solution)/shard_map/bnd,bjkd->bnjk/dot_general | solution.py:33
  31.8 0.0 copy-done.1
  31.8 0.6 gather_fusion.1
  32.5 0.0 copy-done.2
  32.5 0.1 broadcast_compare_fusion
  32.6 1.6 %copy.12 = pred[8,128,8,8]{2,3,1,0:T(8,128)(4,1)S(1)} copy(pred[8,128,8,8]{1,3,2,0:T(8,128)(4,1)S(1)} %broadcast_compare_fusion) | data formatting | bytes 131072 | tf_op jit(solution)/shard_map/eq | solution.py:38
  34.2 0.2 copy.9
  34.4 5.4 %fusion.11 = bf16[8,128,128,8]{2,3,1,0:T(8,128)(2,1)} fusion(f32[8,8,128,128]{2,1,3,0:T(8,128)} %copy.11, f32[8,8,128]{2,1,0:T(8,128)S(1)} %bitcast_convert_fusion, pred[8,8]{1,0:T(8,128)(4,1)S(1)} %fusion.21, pred[8,128,8,8]{2,3,1,0:T(8,128)(4,1)S(1)} %copy.12, s32[8,128,8]{2,1,0:T(8,128)S(1)} %copy.9, s32[8,8]{1,0:T(8,128)S(1)} %select_reduce_fusion), kind=kOutput, calls=%fused_computation.14 | convolution fusion | flops 45089792 | bytes 6422848 | tf_op jit(solution)/shard_map/bjc,bnjk->bnck/dot_general | solution.py:52
  39.9 0.0 copy-start.4
  39.9 5.2 %fusion.6 = f32[1024,768]{1,0:T(8,128)} fusion(bf16[1024,768]{1,0:T(8,128)(2,1)S(1)} %copy-done, bf16[128,8,8,128]{3,2,1,0:T(8,128)(2,1)} %bitcast.76), kind=kOutput, calls=%fused_computation.10 | convolution fusion | flops 1610612736 | bytes 6815744 | tf_op jit(solution)/shard_map/dot_general | solution.py:56
  45.1 0.0 reduce-scatter.3.cloned.1.call-update
  45.1 0.0 reduce-scatter.5.cloned.1.call-start
  45.1 0.0 copy-done.4
  45.1 4.6 %fusion.16 = bf16[1024,768]{1,0:T(8,128)(2,1)} fusion(bf16[1024,768]{1,0:T(8,128)(2,1)S(1)} %copy-done.4, bf16[128,8,8,128]{3,2,1,0:T(8,128)(2,1)} %bitcast.77), kind=kOutput, calls=%fused_computation.17 | convolution fusion | flops 1611399168 | bytes 5242880 | tf_op jit(solution)/shard_map/dot_general | solution.py:57
  49.8 0.0 reduce-scatter.5.cloned.1.call-update
  49.8 64.3 %reduce-scatter.3.cloned.1.call-done = f32[64,768]{1,0:T(8,128)} async-done(((f32[1024,768]{1,0:T(8,128)}), f32[64,768]{1,0:T(8,128)}) %reduce-scatter.3.cloned.1.call-update) | async-done | bytes 196624 | tf_op jit(solution)/shard_map/reduce_scatter | solution.py:60
  114.1 1.6 %convert_element_type.33 = bf16[64,768]{1,0:T(8,128)(2,1)} convert(f32[64,768]{1,0:T(8,128)} %reduce-scatter.3.cloned.1.call-done) | non-fusion elementwise | flops 49152 | bytes 294912 | tf_op jit(solution)/shard_map/convert_element_type | solution.py:64
  115.7 26.3 %reduce-scatter.5.cloned.1.call-done = bf16[512,768]{1,0:T(8,128)(2,1)} async-done(((bf16[1024,768]{1,0:T(8,128)(2,1)}), bf16[512,768]{1,0:T(8,128)(2,1)}) %reduce-scatter.5.cloned.1.call-update) | async-done | bytes 786448 | tf_op jit(solution)/shard_map/reduce_scatter | solution.py:61
  (5 shorter events, 0.1 us)
Async XLA Ops:
  7.2 2.3 %copy-start = (bf16[1024,768]{1,0:T(8,128)(2,1)S(1)}, bf16[1024,768]{1,0:T(8,128)(2,1)}, u32[]{:S(2)}) copy-start(bf16[1024,768]{1,0:T(8,128)(2,1)} %param.6) | copy-start | bytes 4718596
  7.2 107.0 %reduce-scatter.3.cloned.1.call-start = ((), (), s32[]{:S(2)}) async-start(), calls=%async_computation.2 | async-start | bytes 3342336 | tf_op jit(solution)/shard_map/reduce_scatter | solution.py:60
  9.5 7.0 %copy-start.3 = (bf16[1024,768]{1,0:T(8,128)(2,1)S(1)}, bf16[1024,768]{1,0:T(8,128)(2,1)}, u32[]{:S(2)}) copy-start(bf16[1024,768]{1,0:T(8,128)(2,1)} %param.5) | copy-start | bytes 4718596
  26.4 5.4 %copy-start.1 = (bf16[1024]{0:T(1024)(128)(2,1)S(1)}, bf16[1024]{0:T(1024)(128)(2,1)}, u32[]{:S(2)}) copy-start(bf16[1024]{0:T(1024)(128)(2,1)} %param.7) | copy-start | bytes 6148
  26.4 6.0 %copy-start.2 = (s32[1024,8]{0,1:T(8,128)S(1)}, s32[1024,8]{0,1:T(8,128)}, u32[]{:S(2)}) copy-start(s32[1024,8]{0,1:T(8,128)} %param.9) | copy-start | bytes 98308
  39.9 5.2 %copy-start.4 = (bf16[1024,768]{1,0:T(8,128)(2,1)S(1)}, bf16[1024,768]{1,0:T(8,128)(2,1)}, u32[]{:S(2)}) copy-start(bf16[1024,768]{1,0:T(8,128)(2,1)} %param.5) | copy-start | bytes 4718596
  45.1 96.9 %reduce-scatter.5.cloned.1.call-start = ((), (), s32[]{:S(2)}) async-start(), calls=%async_computation.3 | async-start | bytes 2359296 | tf_op jit(solution)/shard_map/reduce_scatter | solution.py:61
Sparse Core Ops, SparseCore 0:
  45.2 68.8 reduce-scatter.2
  116.9 25.0 reduce-scatter.4
where the time goes:
time: 149 us
  waiting for transfers between devices  90.7 us (61%)
  matrix products  25.2 us (17%)
  local copies, waits for them, and re-layouts  14.9 us (10%)
  between operations  14.1 us (9%)
  other arithmetic  3.87 us (3%)
    reduce_scatter x1, waiting for transfers between devices, on_device(): lax.psum_scatter(row_part, 'label', scatter_dimension=0, tiled=True)  64.3 us
    reduce_scatter x1, waiting for transfers between devices, on_device(): lax.psum_scatter(label_part.astype(jnp.bfloat16), 'dp', scatter_dimension...  26.3 us
    dot_general x1, matrix products, on_device(): jnp.einsum('bnd,bjkd->bnjk', blocks, gathered, preferred_element_type=jnp...  9.95 us
    gather x1, local copies, waits for them, and re-layouts, on_device(): gathered = cluster_slabs[local_ids]  6.99 us
    dot_general x1, matrix products, on_device(): jnp.einsum('bjc,bnjk->bnck', placing, slopes, preferred_element_type=jnp....  5.45 us
    dot_general x1, local copies, waits for them, and re-layouts, on_device(): jnp.einsum('bnd,bjkd->bnjk', blocks, gathered, preferred_element_type=jnp...  5.37 us
    dot_general x1, matrix products, on_device(): row_part = jnp.dot(spread, weight, preferred_element_type=jnp.float32)  5.17 us
    dot_general x1, matrix products, on_device(): lax.dot_general(spread, embed, (((0,), (0,)), ((), ())), preferred_elemen...  4.61 us
  transfers between devices with their start and end apart: 2, of which 2 were waited for; matrix products, arithmetic and copies ran while one was open for 4% of the time, Pallas kernels for 0%

commit v1 on v0

v1 whole, which is shorter than its diff:
```python
import functools

import jax
import jax.numpy as jnp
from jax import lax
from jax.experimental import pallas as pl
from jax.experimental.pallas import tpu as pltpu
from jax.sharding import PartitionSpec as P

INST_BLOCK = 128
CLUSTER = 128
TILE = 256
CHUNK = 256
BLOCKS = 8
SCALE = 0.125
ORDER = ((1, 3, 6, 7), (0, 2, 4, 5))

F32 = jnp.float32
BF16 = jnp.bfloat16
VMEM_LIMIT = 32 * 1024 * 1024


def half_index():
    return lax.axis_index("dp") // (lax.axis_size("dp") // 2)


def place(n_label):
    subs = n_label // 2 // BLOCKS
    pair = lax.axis_index("label") // 2
    return pair // subs, pair % subs, lax.axis_index("label") % 2


def slope_chunks(jobs, scores, w, embed, bias_ref, mask_ref, pos_ref, before, emit):
    half_rows = w.shape[0] // 2
    label_no = lax.broadcasted_iota(jnp.int32, (CLUSTER, TILE), 0).astype(jnp.int16)
    words = {}

    def score(n):
        k, t, h = jobs[n]
        before(k, t, h)
        first = k * half_rows + h * CHUNK
        scores[n % 2] = lax.dot_general(
            w[first : first + CHUNK],
            embed[t * TILE : (t + 1) * TILE],
            (((1,), (1,)), ((), ())),
            preferred_element_type=F32,
        )

    score(0)
    for n, (k, t, h) in enumerate(jobs):
        if n + 1 < len(jobs):
            score(n + 1)
        if (k, t) not in words:
            half = 1 - half_index() if k == 0 else half_index()
            first_label = (lax.axis_index("label") * 2 + half) * half_rows
            local = pos_ref[:, t * TILE : (t + 1) * TILE] - first_label
            inside = (local >= 0) & (local < half_rows)
            bits = jnp.where(inside, jnp.left_shift(1, (local >> 7) & 15), 0).astype(jnp.int16)
            within = (local & (CLUSTER - 1)).astype(jnp.int16)
            word = jnp.zeros((CLUSTER, TILE), jnp.int16)
            for p in range(pos_ref.shape[0]):
                word = word | jnp.where(
                    label_no == jnp.broadcast_to(within[p : p + 1], word.shape),
                    jnp.broadcast_to(bits[p : p + 1], word.shape),
                    jnp.int16(0),
                )
            words[k, t] = word
        for i in range(CHUNK // CLUSTER):
            c = h * (CHUNK // CLUSTER) + i
            hit = (words[k, t] & jnp.int16(1 << c)) != 0
            sign = jnp.where(hit, jnp.bfloat16(-1), jnp.bfloat16(1)).astype(F32)
            groups = []
            for g in range(TILE // INST_BLOCK):
                lanes = slice(g * INST_BLOCK, (g + 1) * INST_BLOCK)
                z = (scores[n % 2, i * CLUSTER : (i + 1) * CLUSTER, lanes] + bias_ref[k, c]) * 0.5
                pair = t // 2 * 2 + g
                groups.append((jnp.tanh(z) + sign[:, lanes]).astype(BF16) * mask_ref[k, c, pair : pair + 1])
            emit(k, t, c, jnp.concatenate(groups, axis=1))


def send_kernel(n_label, embed_hbm, weight_hbm, bias_hbm, beam_hbm, pos_hbm, embed, w, pos, mask, bias_full, slopes_t,
                label_out, own_slopes_t, row_out, bias_raw, beam_raw, pos_raw, beam, scores, slopes, sems):
    half_rows = label_out.shape[0]
    clusters = half_rows // CLUSTER
    tiles = embed.shape[0] // TILE
    half = 1 - half_index()
    over, within, core = place(n_label)
    piece = embed.shape[0] // n_label
    subs = INST_BLOCK // piece // 2
    small = [
        pltpu.make_async_copy(source, target, sems.at[k])
        for k, (source, target) in enumerate(((beam_hbm, beam_raw), (bias_hbm, bias_raw), (pos_hbm, pos_raw)))
    ]
    w_copies = [
        pltpu.make_async_copy(
            weight_hbm.at[pl.ds(pl.multiple_of(which * half_rows, half_rows), half_rows)],
            w.at[pl.ds(k * half_rows, half_rows)],
            sems.at[3 + k],
        )
        for k, which in enumerate((half, 1 - half))
    ]
    e_copies = []
    for t in range(tiles):
        e_copies.append([])
        for r in ORDER[t // 2]:
            for j in range(subs):
                i = t * (TILE // piece) + len(e_copies[t])
                row = (r ^ over) * INST_BLOCK + (2 * (j ^ within if subs > 1 else 0) + (core if t % 2 else 1 - core)) * piece
                e_copies[t].append(
                    pltpu.make_async_copy(
                        embed_hbm.at[pl.ds(pl.multiple_of(row, piece), piece)],
                        embed.at[pl.ds(i * piece, piece)],
                        sems.at[5 + i],
                    )
                )
    for copy in (*small, w_copies[0], *e_copies[0]):
        copy.start()
    for copy in small:
        copy.wait()
    for copy in (*e_copies[1], *e_copies[2], *e_copies[3]):
        copy.start()

    lane = lax.broadcasted_iota(jnp.int32, (BLOCKS, INST_BLOCK), 1)
    low = lane < INST_BLOCK // 2

    def relative_lanes(x):
        code = 2 * within + core
        for k in range((2 * subs).bit_length() - 1):
            shift = piece << k
            turned = jnp.where(
                (lane & shift) != 0, pltpu.roll(x, shift, 1), pltpu.roll(x, INST_BLOCK - shift, 1)
            )
            x = jnp.where((code >> k) % 2 == 1, turned, x)
        if subs > 1:
            x = jnp.concatenate(
                [x[:, (2 * j + c) * piece : (2 * j + c + 1) * piece] for c in range(2) for j in range(subs)], axis=1
            )
        return x

    for n in range(2):
        for g in range(2):
            i = 2 * n + g
            one, two = (
                relative_lanes(pos_raw[:, pl.ds(pl.multiple_of((r ^ over) * INST_BLOCK, INST_BLOCK), INST_BLOCK)])
                for r in ORDER[n][2 * g : 2 * g + 2]
            )
            other = jnp.where(low, pltpu.roll(one, INST_BLOCK // 2, 1), two)
            this = jnp.where(low, one, pltpu.roll(two, INST_BLOCK // 2, 1))
            first = 4 * n * INST_BLOCK + g * INST_BLOCK
            pos[:, first : first + INST_BLOCK] = other
            pos[:, first + TILE : first + TILE + INST_BLOCK] = this
            for h in range(2):
                beam[4 * h + i : 4 * h + i + 1] = beam_raw[pl.ds(ORDER[n][2 * g + h] ^ over, 1)]

    def set_up(k, which):
        first_cluster = (lax.axis_index("label") * 2 + which) * clusters
        biases = bias_raw[...].astype(F32)
        for c in range(clusters):
            chosen = jnp.where(which == 0, biases[c : c + 1], biases[clusters + c : clusters + c + 1])
            bias_full[k, c] = jnp.broadcast_to(chosen, (CLUSTER, CLUSTER)).T
            held = jnp.where(beam[...] == first_cluster + c, 0.5 * SCALE, 0.0)
            held = jnp.broadcast_to(jnp.max(held, axis=1, keepdims=True), (BLOCKS, INST_BLOCK))
            mask[k, c] = jnp.where(low[:4], held[:4], held[4:]).astype(BF16)

    set_up(0, half)
    w_copies[0].wait()

    def before(k, t, h):
        if k == 0 and h == 0:
            for copy in e_copies[t]:
                copy.wait()
            if t == 1:
                w_copies[1].start()
        elif k == 1 and h == 0:
            w_copies[1].wait()

    def emit(k, t, c, part):
        if k == 0:
            slopes_t[c * CLUSTER : (c + 1) * CLUSTER, t * TILE : (t + 1) * TILE] = part
            if t == 0:
                slopes[:, c * CLUSTER : (c + 1) * CLUSTER] = part.T
            if (t, c) == (tiles - 1, 0):
                set_up(1, 1 - half)
        else:
            own_slopes_t[c * CLUSTER : (c + 1) * CLUSTER] = part
            slopes[:, half_rows + c * CLUSTER : half_rows + (c + 1) * CLUSTER] = part.T
        if (k, t) == (0, tiles - 1) and (c + 1) % (CHUNK // CLUSTER) == 0:
            rows = slice((c + 1) * CLUSTER - CHUNK, (c + 1) * CLUSTER)
            label_out[rows] = jnp.dot(slopes_t[rows], embed[...], preferred_element_type=F32).astype(BF16)

    chunks = range(half_rows // CHUNK)
    jobs = [(0, t, h) for t in range(tiles) for h in chunks] + [(1, 0, h) for h in chunks]
    slope_chunks(jobs, scores, w, embed, bias_full, mask, pos, before, emit)
    store_rows([row_out], slopes, w)


def store_rows(outs, slopes, w):
    sums = jnp.dot(slopes[...], w[...], preferred_element_type=F32).astype(BF16)
    count = TILE // len(outs)
    for i, out in enumerate(outs):
        out[...] = sums[i * count : (i + 1) * count].reshape(out.shape)


def row_tile(t, outs, embed, w, pos, mask, bias_full, first_slopes_t, own_slopes_t, scores, slopes):
    half_rows = w.shape[0] // 2

    def emit(k, t, c, part):
        if c == 0:
            slopes[:, :half_rows] = first_slopes_t[:, t * TILE : (t + 1) * TILE].T
        own_slopes_t[c * CLUSTER : (c + 1) * CLUSTER] = part
        slopes[:, half_rows + c * CLUSTER : half_rows + (c + 1) * CLUSTER] = part.T

    jobs = [(1, t, h) for h in range(half_rows // CHUNK)]
    slope_chunks(jobs, scores, w, embed, bias_full, mask, pos, lambda *job: None, emit)
    store_rows(outs, slopes, w)


def keep_rows_kernel(embed, w, pos, mask, bias_full, first_slopes_t, own_slopes_t, row_out, scores, slopes):
    row_tile(1, [row_out], embed, w, pos, mask, bias_full, first_slopes_t, own_slopes_t, scores, slopes)


def last_rows_kernel(embed, w, pos, mask, bias_full, first_slopes_t, one_slopes_t, two_slopes_t, *rest):
    *sends, row_out, label_out, three_slopes_t, four_slopes_t, scores, slopes = rest
    shared = (embed, w, pos, mask, bias_full, first_slopes_t)
    row_tile(2, sends, *shared, three_slopes_t, scores.at[0], slopes.at[0])
    row_tile(3, [row_out], *shared, four_slopes_t, scores.at[1], slopes.at[1])
    total = 0.0
    for t, part in enumerate((one_slopes_t, two_slopes_t, three_slopes_t, four_slopes_t)):
        total = total + jnp.dot(part[...], embed[t * TILE : (t + 1) * TILE], preferred_element_type=F32)
    label_out[...] = total.astype(BF16)


def swapped(value, axis, size, bit):
    return lax.ppermute(value, axis, [(i, i ^ bit) for i in range(size)])


def add(*terms):
    total = terms[0].astype(F32)
    for term in terms[1:]:
        total = total + term.astype(F32)
    return total.astype(BF16)


def on_device(n_dp, n_label, embed, weight, bias, beam, positives):
    rows, features = embed.shape
    labels = weight.shape[0]
    half_rows = labels // 2
    clusters = half_rows // CLUSTER
    piece = rows // n_label
    subs = n_label // 2 // BLOCKS
    pos_count = positives.shape[1]
    bias_rows = bias.reshape(labels // CLUSTER, CLUSTER)
    pos_rows = positives.T
    vmem = pl.BlockSpec(memory_space=pltpu.VMEM)
    hbm = pl.BlockSpec(memory_space=pltpu.HBM)
    params = pltpu.CompilerParams(vmem_limit_bytes=VMEM_LIMIT)
    shape = jax.ShapeDtypeStruct
    tile_shape = shape((half_rows, TILE), BF16)
    row_shape = shape((BLOCKS // 2, subs, piece, features), BF16)
    score_scratch = pltpu.VMEM((2, CHUNK, TILE), F32)
    slope_scratch = pltpu.VMEM((TILE, labels), BF16)

    def cost(halves):
        return pl.CostEstimate(flops=halves * 2 * rows * half_rows * features, bytes_accessed=0, transcendentals=0)

    *shared, label_send, one_slopes_t, first_send = pl.pallas_call(
        functools.partial(send_kernel, n_label),
        out_shape=[
            shape((rows, features), BF16),
            shape((labels, features), BF16),
            shape((pos_count, rows), jnp.int32),
            shape((2, clusters, 4, INST_BLOCK), BF16),
            shape((2, clusters, CLUSTER, INST_BLOCK), F32),
            shape((half_rows, rows), BF16),
            shape((half_rows, features), BF16),
            tile_shape,
            row_shape,
        ],
        in_specs=[hbm] * 5,
        out_specs=[vmem] * 9,
        scratch_shapes=[
            pltpu.VMEM(bias_rows.shape, BF16),
            pltpu.VMEM(beam.shape, jnp.int32),
            pltpu.VMEM(pos_rows.shape, jnp.int32),
            pltpu.VMEM(beam.shape, jnp.int32),
            score_scratch,
            slope_scratch,
            pltpu.SemaphoreType.DMA((5 + n_label,)),
        ],
        compiler_params=params,
        cost_estimate=cost(3),
        name="send_half",
    )(*(pltpu.with_memory_space_constraint(x, pltpu.HBM) for x in (embed, weight, bias_rows, beam, pos_rows)))

    first_got = swapped(first_send, "label", n_label, 1)
    label_got = swapped(label_send, "dp", n_dp, n_dp // 2)
    first_got, *shared = lax.optimization_barrier((first_got, *shared))

    two_slopes_t, first_keep = pl.pallas_call(
        keep_rows_kernel,
        out_shape=[tile_shape, row_shape],
        in_specs=[vmem] * 6,
        out_specs=[vmem] * 2,
        scratch_shapes=[score_scratch, slope_scratch],
        compiler_params=params,
        cost_estimate=cost(0),
        name="keep_rows",
    )(*shared)

    axes = [2 * subs, 4 * subs, 8 * subs]
    one_got = swapped(add(first_keep[:2], first_got[:2]), "label", n_label, axes[0])
    two_got = swapped(add(first_keep[2:], first_got[2:]), "label", n_label, axes[1])

    part_shape = shape((subs, piece, features), BF16)
    *last_send, last_keep, label_keep = pl.pallas_call(
        last_rows_kernel,
        out_shape=[part_shape] * 4 + [row_shape, shape((half_rows, features), BF16)],
        in_specs=[vmem] * 8,
        out_specs=[vmem] * 6,
        scratch_shapes=[
            pltpu.VMEM((half_rows, TILE), BF16),
            pltpu.VMEM((half_rows, TILE), BF16),
            pltpu.VMEM((2, 2, CHUNK, TILE), F32),
            pltpu.VMEM((2, TILE, labels), BF16),
        ],
        compiler_params=params,
        cost_estimate=cost(0),
        name="last_rows",
    )(*shared, one_slopes_t, two_slopes_t)

    last_got = [swapped(part, "label", n_label, 1) for part in last_send]

    two_next = add(last_keep[1], last_got[1], one_got[1])
    five_next = add(last_keep[3], last_got[3], two_got[1])
    two_next_got = swapped(two_next, "label", n_label, axes[1])
    five_next_got = swapped(five_next, "label", n_label, axes[0])
    four = add(last_keep[2], last_got[2], two_got[0], five_next_got)
    four_got = swapped(four, "label", n_label, axes[2])
    row_sum = add(last_keep[0], last_got[0], one_got[0], two_next_got)
    row_got = four_got
    bit = subs
    while bit > 1:
        held = row_sum.shape[0] // 2
        outgoing = add(row_sum[held:], row_got[held:])
        incoming = swapped(outgoing, "label", n_label, bit)
        row_sum = add(row_sum[:held], row_got[:held])
        row_got = incoming
        bit //= 2
    row_out = add(row_sum[0], row_got[0])

    label_sum = add(label_keep, label_got)
    step = n_dp // 4
    at = lax.axis_index("dp")
    while step >= 1:
        held = label_sum.shape[0] // 2
        mine = (at // step) % 2
        outgoing = lax.dynamic_slice_in_dim(label_sum, (1 - mine) * held, held, 0)
        kept = lax.dynamic_slice_in_dim(label_sum, mine * held, held, 0)
        label_sum = add(kept, swapped(outgoing, "dp", n_dp, step))
        step //= 2
    return row_out, label_sum


def solution(mesh):
    in_specs = (P("dp", None), P("label", None), P("label"), P("dp", None), P("dp", None))
    out_specs = (P(("dp", "label"), None), P(("label", "dp"), None))
    body = functools.partial(on_device, mesh.shape["dp"], mesh.shape["label"])
    return jax.shard_map(body, mesh=mesh, in_specs=in_specs, out_specs=out_specs, check_vma=False)
```

time: 149 us -> 29.9 us (0.20)
  waiting for transfers between devices: 90.7 us -> 6.35 us
  matrix products: 25.2 us -> 0 us
  local copies, waits for them, and re-layouts: 14.9 us -> 0 us
  between operations: 14.1 us -> 0.68 us
  starting transfers between devices: 0.08 us -> 11.9 us
  Pallas kernels: 0 us -> 8.8 us
  other arithmetic: 3.87 us -> 2 us
    reduce_scatter x2 -> x0, waiting for transfers between devices: 90.7 us -> none  [the longest x1 64.3 us: on_device(): lax.psum_scatter(row_part, 'label', scatter_dimension=0, tiled=True)]
    dot_general x4 -> x0, matrix products: 25.2 us -> none  [the longest x1 9.95 us: on_device(): jnp.einsum('bnd,bjkd->bnjk', blocks, gathered, preferred_element_type=jnp...]
    ppermute x0 -> x11, starting transfers between devices: none -> 11.9 us  [swapped(): return lax.ppermute(value, axis, [(i, i ^ bit) for i in range(size)])]
    pallas_call x0 -> x3, Pallas kernels: none -> 8.8 us  [the longest x1 5.32 us: on_device(): pl.pallas_call(functools.partial(send_kernel, n_label), out_shape=[shape(...]
    gather x2 -> x0, local copies, waits for them, and re-layouts: 7.62 us -> none  [the longest x1 6.99 us: on_device(): gathered = cluster_slabs[local_ids]]
    ppermute x0 -> x11, waiting for transfers between devices: none -> 6.35 us  [swapped(): return lax.ppermute(value, axis, [(i, i ^ bit) for i in range(size)])]
    dot_general x1 -> x0, local copies, waits for them, and re-layouts: 5.37 us -> none  [on_device(): jnp.einsum('bnd,bjkd->bnjk', blocks, gathered, preferred_element_type=jnp...]
    eq x1 -> x0, local copies, waits for them, and re-layouts: 1.6 us -> none  [on_device(): wanted[:, :, :, None] // CLUSTER == cluster_ids[:, None, None, :]]
  transfers between devices with their start and end apart: 2 -> 11, of which waited for: 2 -> 5; matrix products, arithmetic and copies ran while one was open for 4% -> 4% of each run, Pallas kernels for 0% -> 12%
where the time goes in v1:
time: 29.9 us; the launch traced here: 29.8 us
  starting transfers between devices  11.9 us (40%)
  Pallas kernels  8.8 us (29%)
  waiting for transfers between devices  6.35 us (21%)
  other arithmetic  2 us (7%)
  between operations  0.68 us (2%)
    ppermute x11, starting transfers between devices, swapped(): return lax.ppermute(value, axis, [(i, i ^ bit) for i in range(size)])  11.9 us
    ppermute x11, waiting for transfers between devices, swapped(): return lax.ppermute(value, axis, [(i, i ^ bit) for i in range(size)])  6.35 us
    pallas_call x1, Pallas kernels, on_device(): pl.pallas_call(functools.partial(send_kernel, n_label), out_shape=[shape(...  5.32 us
    pallas_call x1, Pallas kernels, on_device(): pl.pallas_call(last_rows_kernel, out_shape=[part_shape] * 4 + [row_shape,...  2.39 us
    convert_element_type x5, other arithmetic, add(): return total.astype(BF16)  2 us
    pallas_call x1, Pallas kernels, on_device(): pl.pallas_call(keep_rows_kernel, out_shape=[tile_shape, row_shape], in_sp...  1.09 us
  transfers between devices with their start and end apart: 11, of which 5 were waited for; matrix products, arithmetic and copies ran while one was open for 4% of the time, Pallas kernels for 12%

profile of v1, /device:TPU:0, one launch (start us, length us, event | category | flops | bytes accessed | tf_op | source)
XLA Modules:
  0.0 29.8 jit_solution(7569551170624470424)
XLA Ops:
  0.6 5.3 %send_half.1 = (bf16[1024,768]{1,0:T(8,128)(2,1)S(1)}, bf16[1024,768]{1,0:T(8,128)(2,1)S(1)}, s32[8,1024]{1,0:T(8,128)S(1)}, bf16[2,4,4,128]{3,2,1,0:T(4,128)(2,...) custom-call(bf16[1024,768]{1,0:T(8,128)(2,1)} %embed_hbm.1, ...), custom_call_target="tpu_custom_call" | custom-call | flops 2415919104 | tf_op jit(solution)/shard_map/send_half/pallas_call | solution.py:266
  6.0 0.6 %collective-permute-start = (bf16[4,1,64,768]{3,2,1,0:T(8,128)(2,1)S(1)}, bf16[4,1,64,768]{3,2,1,0:T(8,128)(2,1)S(1)}, u32[]{:S(2)}, u32[]{:S(2)}) collective-permute-start(bf16[4,1,64,768]{3,2,1,0:T(8,128)(2,1)S(1)} %get-tuple-element.26), channel_id=1, source_target_pairs={{0,1},{1,0},{2,3},{3,2},{4,5},{5,4},{6,7},{7,6},{8,9},{9,8},{10,11... | collective-permute-start | bytes 1179656 | tf_op jit(solution)/shard_map/ppermute | solution.py:234
  6.5 2.5 %collective-permute-start.10 = (bf16[512,768]{1,0:T(8,128)(2,1)S(1)}, bf16[512,768]{1,0:T(8,128)(2,1)S(1)}, u32[]{:S(2)}, u32[]{:S(2)}) collective-permute-start(bf16[512,768]{1,0:T(8,128)(2,1)S(1)} %get-tuple-element.49), channel_id=1, source_target_pairs={{0,16},{16,0},{1,17},{17,1},{2,18},{18,2},{3,19},{19,3},{4,20},{20... | collective-permute-start | bytes 2359304 | tf_op jit(solution)/shard_map/ppermute | solution.py:234
  9.0 0.0 collective-permute-done
  9.1 1.1 %keep_rows.1 = (bf16[512,256]{1,0:T(8,128)(2,1)S(1)}, bf16[4,1,64,768]{3,2,1,0:T(8,128)(2,1)S(1)}) custom-call(bf16[1024,768]{1,0:T(8,128)(2,1)S(1)} %get-tuple-element.33.embed, bf16[1024,768]{1,0:T(8,128)(2,1)S(1)} %get-tuple-element.34.w, s32[8,1024]{1,0:T(8,128)S(1)} %get-tuple-element.35.pos, bf16[2,4,4,128]{3,2,1,0:T(4,128)(2,1)S(1)} %get-tuple-element.36.mask, ...), custom_call_target="tpu_custom_call" | custom-call | tf_op jit(solution)/shard_map/keep_rows/pallas_call | solution.py:299
  10.1 0.1 add_convert_fusion.2
  10.2 1.7 %collective-permute-start.2 = (bf16[2,1,64,768]{3,2,1,0:T(8,128)(2,1)S(1)}, bf16[2,1,64,768]{3,2,1,0:T(8,128)(2,1)S(1)}, u32[]{:S(2)}, u32[]{:S(2)}) collective-permute-start(bf16[2,1,64,768]{3,2,1,0:T(8,128)(2,1)S(1)} %get-tuple-element.50), channel_id=1, source_target_pairs={{0,2},{1,3},{2,0},{3,1},{4,6},{5,7},{6,4},{7,5},{8,10},{9,11},{10,... | collective-permute-start | bytes 589832 | tf_op jit(solution)/shard_map/ppermute | solution.py:234
  12.0 1.6 %collective-permute-start.6 = (bf16[2,1,64,768]{3,2,1,0:T(8,128)(2,1)S(1)}, bf16[2,1,64,768]{3,2,1,0:T(8,128)(2,1)S(1)}, u32[]{:S(2)}, u32[]{:S(2)}) collective-permute-start(bf16[2,1,64,768]{3,2,1,0:T(8,128)(2,1)S(1)} %get-tuple-element.51), channel_id=1, source_target_pairs={{0,4},{1,5},{2,6},{3,7},{4,0},{5,1},{6,2},{7,3},{8,12},{9,13},{10,... | collective-permute-start | bytes 589832 | tf_op jit(solution)/shard_map/ppermute | solution.py:234
  13.6 2.4 %last_rows.1 = (bf16[1,64,768]{2,1,0:T(8,128)(2,1)S(1)}, bf16[1,64,768]{2,1,0:T(8,128)(2,1)S(1)}, bf16[1,64,768]{2,1,0:T(8,128)(2,1)S(1)}, bf16[1,64,768]{2,1,0:...) custom-call(bf16[1024,768]{1,0:T(8,128)(2,1)S(1)} %get-tuple-element.33.embed, ...), custom_call_target="tpu_custom_call" | custom-call | tf_op jit(solution)/shard_map/last_rows/pallas_call | solution.py:315
  15.9 0.1 collective-permute-start.3
  16.0 0.5 %collective-permute-start.7 = (bf16[1,64,768]{2,1,0:T(8,128)(2,1)S(1)}, bf16[1,64,768]{2,1,0:T(8,128)(2,1)S(1)}, u32[]{:S(2)}, u32[]{:S(2)}) collective-permute-start(bf16[1,64,768]{2,1,0:T(8,128)(2,1)S(1)} %get-tuple-element.47), channel_id=1, source_target_pairs={{0,1},{1,0},{2,3},{3,2},{4,5},{5,4},{6,7},{7,6},{8,9},{9,8},{10,11... | collective-permute-start | bytes 294920 | tf_op jit(solution)/shard_map/ppermute | solution.py:234
  16.5 0.8 %collective-permute-done.3 = bf16[1,64,768]{2,1,0:T(8,128)(2,1)S(1)} collective-permute-done((bf16[1,64,768]{2,1,0:T(8,128)(2,1)S(1)}, bf16[1,64,768]{2,1,0:T(8,128)(2,1)S(1)}, u32[]{:S(2)}, u32[]{:S(2)}) %collective-permute-start.3) | collective-permute-done | bytes 98336 | tf_op jit(solution)/shard_map/ppermute | solution.py:234
  17.3 0.2 collective-permute-start.5
  17.5 0.0 collective-permute-done.7
  17.5 0.0 collective-permute-done.2
  17.5 1.2 %collective-permute-done.6 = bf16[2,1,64,768]{3,2,1,0:T(8,128)(2,1)S(1)} collective-permute-done((bf16[2,1,64,768]{3,2,1,0:T(8,128)(2,1)S(1)}, bf16[2,1,64,768]{3,2,1,0:T(8,128)(2,1)S(1)}, u32[]{:S(2)}, u32[]{:S(2)}) %collective-permute-start.6) | collective-permute-done | bytes 196640 | tf_op jit(solution)/shard_map/ppermute | solution.py:234
  18.6 0.1 fusion.3
  18.7 0.5 %collective-permute-start.8 = (bf16[1,64,768]{2,1,0:T(8,128)(2,1)S(1)}, bf16[1,64,768]{2,1,0:T(8,128)(2,1)S(1)}, u32[]{:S(2)}, u32[]{:S(2)}) collective-permute-start(bf16[1,64,768]{2,1,0:T(8,128)(2,1)S(1)} %get-tuple-element.53), channel_id=1, source_target_pairs={{0,2},{1,3},{2,0},{3,1},{4,6},{5,7},{6,4},{7,5},{8,10},{9,11},{10,... | collective-permute-start | bytes 294920 | tf_op jit(solution)/shard_map/ppermute | solution.py:234
  19.2 0.0 collective-permute-start.1
  19.2 1.7 %collective-permute-start.4 = (bf16[1,64,768]{2,1,0:T(8,128)(2,1)S(1)}, bf16[1,64,768]{2,1,0:T(8,128)(2,1)S(1)}, u32[]{:S(2)}, u32[]{:S(2)}) collective-permute-start(bf16[1,64,768]{2,1,0:T(8,128)(2,1)S(1)} %get-tuple-element.52), channel_id=1, source_target_pairs={{0,4},{1,5},{2,6},{3,7},{4,0},{5,1},{6,2},{7,3},{8,12},{9,13},{10,... | collective-permute-start | bytes 294920 | tf_op jit(solution)/shard_map/ppermute | solution.py:234
  20.9 0.0 collective-permute-done.5
  20.9 2.5 %collective-permute-done.8 = bf16[1,64,768]{2,1,0:T(8,128)(2,1)S(1)} collective-permute-done((bf16[1,64,768]{2,1,0:T(8,128)(2,1)S(1)}, bf16[1,64,768]{2,1,0:T(8,128)(2,1)S(1)}, u32[]{:S(2)}, u32[]{:S(2)}) %collective-permute-start.8) | collective-permute-done | bytes 98336 | tf_op jit(solution)/shard_map/ppermute | solution.py:234
  23.4 0.1 fusion.2
  23.5 2.7 %collective-permute-start.9 = (bf16[1,64,768]{2,1,0:T(8,128)(2,1)S(1)}, bf16[1,64,768]{2,1,0:T(8,128)(2,1)S(1)}, u32[]{:S(2)}, u32[]{:S(2)}) collective-permute-start(bf16[1,64,768]{2,1,0:T(8,128)(2,1)S(1)} %fusion.2), channel_id=1, source_target_pairs={{0,8},{1,9},{2,10},{3,11},{4,12},{5,13},{6,14},{7,15},{8,0},{9,1},... | collective-permute-start | bytes 294920 | tf_op jit(solution)/shard_map/ppermute | solution.py:234
  26.1 1.1 %collective-permute-done.10 = bf16[512,768]{1,0:T(8,128)(2,1)S(1)} collective-permute-done((bf16[512,768]{1,0:T(8,128)(2,1)S(1)}, bf16[512,768]{1,0:T(8,128)(2,1)S(1)}, u32[]{:S(2)}, u32[]{:S(2)}) %collective-permute-start.10) | collective-permute-done | bytes 786464 | tf_op jit(solution)/shard_map/ppermute | solution.py:234
  27.2 1.1 %add_convert_fusion = bf16[512,768]{1,0:T(8,128)(2,1)} fusion(bf16[512,768]{1,0:T(8,128)(2,1)S(1)} %collective-permute-done.10, bf16[512,768]{1,0:T(8,128)(2,1)S(1)} %get-tuple-element.48), kind=kLoop, calls=%fused_computation | loop fusion | flops 1572864 | bytes 2359296 | tf_op jit(solution)/shard_map/convert_element_type | solution.py:241
  28.3 0.0 collective-permute-done.1
  28.3 0.0 collective-permute-done.4
  28.3 0.8 %collective-permute-done.9 = bf16[1,64,768]{2,1,0:T(8,128)(2,1)S(1)} collective-permute-done((bf16[1,64,768]{2,1,0:T(8,128)(2,1)S(1)}, bf16[1,64,768]{2,1,0:T(8,128)(2,1)S(1)}, u32[]{:S(2)}, u32[]{:S(2)}) %collective-permute-start.9) | collective-permute-done | bytes 98336 | tf_op jit(solution)/shard_map/ppermute | solution.py:234
  29.0 0.7 %fusion.6 = bf16[64,768]{1,0:T(8,128)(2,1)} fusion(bf16[1,64,768]{2,1,0:T(8,128)(2,1)S(1)} %collective-permute-done.9, bf16[1,64,768]{2,1,0:T(8,128)(2,1)S(1)} %collective-permute-done.4, bf16[1,64,768]{2,1,0:T(8,128)(2,1)S(1)} %collective-permute-done.1, bf16[2,1,64,768]{3,2,1,0:T(8,128)(2,1)S(1)} %collective-permute-done.2, ...), kind=kLoop, calls=%fused_computation.18 | loop fusion | flops 589824 | bytes 589824 | tf_op jit(solution)/shard_map/convert_element_type | solution.py:241
Async XLA Ops:
  6.0 3.1 %collective-permute-start = (bf16[4,1,64,768]{3,2,1,0:T(8,128)(2,1)S(1)}, bf16[4,1,64,768]{3,2,1,0:T(8,128)(2,1)S(1)}, u32[]{:S(2)}, u32[]{:S(2)}) collective-permute-start(bf16[4,1,64,768]{3,2,1,0:T(8,128)(2,1)S(1)} %get-tuple-element.26), channel_id=1, source_target_pairs={{0,1},{1,0},{2,3},{3,2},{4,5},{5,4},{6,7},{7,6},{8,9},{9,8},{10,11... | collective-permute-start | bytes 1179656 | tf_op jit(solution)/shard_map/ppermute | solution.py:234
  6.5 20.7 %collective-permute-start.10 = (bf16[512,768]{1,0:T(8,128)(2,1)S(1)}, bf16[512,768]{1,0:T(8,128)(2,1)S(1)}, u32[]{:S(2)}, u32[]{:S(2)}) collective-permute-start(bf16[512,768]{1,0:T(8,128)(2,1)S(1)} %get-tuple-element.49), channel_id=1, source_target_pairs={{0,16},{16,0},{1,17},{17,1},{2,18},{18,2},{3,19},{19,3},{4,20},{20... | collective-permute-start | bytes 2359304 | tf_op jit(solution)/shard_map/ppermute | solution.py:234
  10.2 7.2 %collective-permute-start.2 = (bf16[2,1,64,768]{3,2,1,0:T(8,128)(2,1)S(1)}, bf16[2,1,64,768]{3,2,1,0:T(8,128)(2,1)S(1)}, u32[]{:S(2)}, u32[]{:S(2)}) collective-permute-start(bf16[2,1,64,768]{3,2,1,0:T(8,128)(2,1)S(1)} %get-tuple-element.50), channel_id=1, source_target_pairs={{0,2},{1,3},{2,0},{3,1},{4,6},{5,7},{6,4},{7,5},{8,10},{9,11},{10,... | collective-permute-start | bytes 589832 | tf_op jit(solution)/shard_map/ppermute | solution.py:234
  12.0 6.7 %collective-permute-start.6 = (bf16[2,1,64,768]{3,2,1,0:T(8,128)(2,1)S(1)}, bf16[2,1,64,768]{3,2,1,0:T(8,128)(2,1)S(1)}, u32[]{:S(2)}, u32[]{:S(2)}) collective-permute-start(bf16[2,1,64,768]{3,2,1,0:T(8,128)(2,1)S(1)} %get-tuple-element.51), channel_id=1, source_target_pairs={{0,4},{1,5},{2,6},{3,7},{4,0},{5,1},{6,2},{7,3},{8,12},{9,13},{10,... | collective-permute-start | bytes 589832 | tf_op jit(solution)/shard_map/ppermute | solution.py:234
  15.9 1.4 %collective-permute-start.3 = (bf16[1,64,768]{2,1,0:T(8,128)(2,1)S(1)}, bf16[1,64,768]{2,1,0:T(8,128)(2,1)S(1)}, u32[]{:S(2)}, u32[]{:S(2)}) collective-permute-start(bf16[1,64,768]{2,1,0:T(8,128)(2,1)S(1)} %get-tuple-element.45), channel_id=1, source_target_pairs={{0,1},{1,0},{2,3},{3,2},{4,5},{5,4},{6,7},{7,6},{8,9},{9,8},{10,11... | collective-permute-start | bytes 294920 | tf_op jit(solution)/shard_map/ppermute | solution.py:234
  16.0 1.4 %collective-permute-start.7 = (bf16[1,64,768]{2,1,0:T(8,128)(2,1)S(1)}, bf16[1,64,768]{2,1,0:T(8,128)(2,1)S(1)}, u32[]{:S(2)}, u32[]{:S(2)}) collective-permute-start(bf16[1,64,768]{2,1,0:T(8,128)(2,1)S(1)} %get-tuple-element.47), channel_id=1, source_target_pairs={{0,1},{1,0},{2,3},{3,2},{4,5},{5,4},{6,7},{7,6},{8,9},{9,8},{10,11... | collective-permute-start | bytes 294920 | tf_op jit(solution)/shard_map/ppermute | solution.py:234
  17.3 3.6 %collective-permute-start.5 = (bf16[1,64,768]{2,1,0:T(8,128)(2,1)S(1)}, bf16[1,64,768]{2,1,0:T(8,128)(2,1)S(1)}, u32[]{:S(2)}, u32[]{:S(2)}) collective-permute-start(bf16[1,64,768]{2,1,0:T(8,128)(2,1)S(1)} %get-tuple-element.46), channel_id=1, source_target_pairs={{0,1},{1,0},{2,3},{3,2},{4,5},{5,4},{6,7},{7,6},{8,9},{9,8},{10,11... | collective-permute-start | bytes 294920 | tf_op jit(solution)/shard_map/ppermute | solution.py:234
  18.7 4.7 %collective-permute-start.8 = (bf16[1,64,768]{2,1,0:T(8,128)(2,1)S(1)}, bf16[1,64,768]{2,1,0:T(8,128)(2,1)S(1)}, u32[]{:S(2)}, u32[]{:S(2)}) collective-permute-start(bf16[1,64,768]{2,1,0:T(8,128)(2,1)S(1)} %get-tuple-element.53), channel_id=1, source_target_pairs={{0,2},{1,3},{2,0},{3,1},{4,6},{5,7},{6,4},{7,5},{8,10},{9,11},{10,... | collective-permute-start | bytes 294920 | tf_op jit(solution)/shard_map/ppermute | solution.py:234
  19.2 9.1 %collective-permute-start.1 = (bf16[1,64,768]{2,1,0:T(8,128)(2,1)S(1)}, bf16[1,64,768]{2,1,0:T(8,128)(2,1)S(1)}, u32[]{:S(2)}, u32[]{:S(2)}) collective-permute-start(bf16[1,64,768]{2,1,0:T(8,128)(2,1)S(1)} %get-tuple-element.42), channel_id=1, source_target_pairs={{0,1},{1,0},{2,3},{3,2},{4,5},{5,4},{6,7},{7,6},{8,9},{9,8},{10,11... | collective-permute-start | bytes 294920 | tf_op jit(solution)/shard_map/ppermute | solution.py:234
  19.2 9.1 %collective-permute-start.4 = (bf16[1,64,768]{2,1,0:T(8,128)(2,1)S(1)}, bf16[1,64,768]{2,1,0:T(8,128)(2,1)S(1)}, u32[]{:S(2)}, u32[]{:S(2)}) collective-permute-start(bf16[1,64,768]{2,1,0:T(8,128)(2,1)S(1)} %get-tuple-element.52), channel_id=1, source_target_pairs={{0,4},{1,5},{2,6},{3,7},{4,0},{5,1},{6,2},{7,3},{8,12},{9,13},{10,... | collective-permute-start | bytes 294920 | tf_op jit(solution)/shard_map/ppermute | solution.py:234
  23.5 5.6 %collective-permute-start.9 = (bf16[1,64,768]{2,1,0:T(8,128)(2,1)S(1)}, bf16[1,64,768]{2,1,0:T(8,128)(2,1)S(1)}, u32[]{:S(2)}, u32[]{:S(2)}) collective-permute-start(bf16[1,64,768]{2,1,0:T(8,128)(2,1)S(1)} %fusion.2), channel_id=1, source_target_pairs={{0,8},{1,9},{2,10},{3,11},{4,12},{5,13},{6,14},{7,15},{8,0},{9,1},... | collective-permute-start | bytes 294920 | tf_op jit(solution)/shard_map/ppermute | solution.py:234

commit v2 on v1

v2 whole, which is shorter than its diff:
```python
import functools

import jax
import jax.numpy as jnp
from jax import lax
from jax.experimental import pallas as pl
from jax.experimental.pallas import tpu as pltpu
from jax.sharding import PartitionSpec as P

INST_BLOCK = 128
CLUSTER = 128
TILE = 256
CHUNK = 128
BLOCKS = 8
SCALE = 0.125

F32 = jnp.float32
BF16 = jnp.bfloat16
VMEM_LIMIT = 32 * 1024 * 1024


def half_index():
    return lax.axis_index("dp") // (lax.axis_size("dp") // 2)


def place(n_label):
    subs = n_label // 2 // BLOCKS
    pair = lax.axis_index("label") // 2
    return pair // subs, pair % subs, lax.axis_index("label") % 2


def slope_chunks(jobs, scores, w, embed, bias_ref, mask_ref, word_ref, before, emit):
    half_rows = w.shape[0] // 2
    clusters = half_rows // CLUSTER

    def score(n):
        k, t, h = jobs[n]
        before(k, t, h)
        first = k * half_rows + h * CHUNK
        scores[n % 2] = lax.dot_general(
            w[first : first + CHUNK],
            embed[t * TILE : (t + 1) * TILE],
            (((1,), (1,)), ((), ())),
            preferred_element_type=F32,
        )

    score(0)
    for n, (k, t, h) in enumerate(jobs):
        if n + 1 < len(jobs):
            score(n + 1)
        for i in range(CHUNK // CLUSTER):
            c = h * (CHUNK // CLUSTER) + i
            hit = (word_ref[:, t * TILE : (t + 1) * TILE] & jnp.int16(1 << (k * clusters + c))) != 0
            sign = jnp.where(hit, jnp.bfloat16(-1), jnp.bfloat16(1)).astype(F32)
            groups = []
            for g in range(TILE // INST_BLOCK):
                lanes = slice(g * INST_BLOCK, (g + 1) * INST_BLOCK)
                z = scores[n % 2, i * CLUSTER : (i + 1) * CLUSTER, lanes] * 0.5 + bias_ref[k, c]
                group = t * (TILE // INST_BLOCK) + g
                groups.append((jnp.tanh(z) + sign[:, lanes]).astype(BF16) * mask_ref[k, c, group : group + 1])
            emit(k, t, c, jnp.concatenate(groups, axis=1))


def block_in(t, i, over, core):
    first, second, third = 1 - t // 2, i // 2, i % 2
    owner = core if t % 2 else 1 - core
    return (first + 2 * second + 4 * third + owner * (first - second)) ^ over


def send_kernel(n_label, embed_hbm, weight_hbm, bias_hbm, beam_hbm, pos_hbm, embed, w, word, mask, bias_full, slopes_t,
                label_out, own_slopes_t, row_out, bias_raw, beam_raw, pos_raw, beam, scores, slopes, sems):
    half_rows = label_out.shape[0]
    clusters = half_rows // CLUSTER
    tiles = embed.shape[0] // TILE
    half = 1 - half_index()
    over, within, core = place(n_label)
    piece = embed.shape[0] // n_label
    subs = INST_BLOCK // piece // 2
    small = [
        pltpu.make_async_copy(source, target, sems.at[k])
        for k, (source, target) in enumerate(((beam_hbm, beam_raw), (bias_hbm, bias_raw), (pos_hbm, pos_raw)))
    ]
    w_copies = [
        pltpu.make_async_copy(
            weight_hbm.at[pl.ds(pl.multiple_of(which * half_rows, half_rows), half_rows)],
            w.at[pl.ds(k * half_rows, half_rows)],
            sems.at[3 + k],
        )
        for k, which in enumerate((half, 1 - half))
    ]
    e_copies = []
    for t in range(tiles):
        e_copies.append([])
        for i in range(4):
            for j in range(subs):
                at = t * (TILE // piece) + len(e_copies[t])
                row = block_in(t, i, over, core) * INST_BLOCK
                row = row + (2 * (j ^ within if subs > 1 else 0) + (core if t % 2 else 1 - core)) * piece
                e_copies[t].append(
                    pltpu.make_async_copy(
                        embed_hbm.at[pl.ds(pl.multiple_of(row, piece), piece)],
                        embed.at[pl.ds(at * piece, piece)],
                        sems.at[5 + at],
                    )
                )
    for copy in (*small, *e_copies[0], w_copies[0], *e_copies[1]):
        copy.start()
    for copy in small:
        copy.wait()
    for copy in (*e_copies[2], *e_copies[3]):
        copy.start()

    lane = lax.broadcasted_iota(jnp.int32, (BLOCKS, INST_BLOCK), 1)
    low = lane < INST_BLOCK // 2

    def relative_lanes(x):
        code = 2 * within + core
        for k in range((2 * subs).bit_length() - 1):
            shift = piece << k
            turned = jnp.where(
                (lane & shift) != 0, pltpu.roll(x, shift, 1), pltpu.roll(x, INST_BLOCK - shift, 1)
            )
            x = jnp.where((code >> k) % 2 == 1, turned, x)
        if subs > 1:
            x = jnp.concatenate(
                [x[:, (2 * j + c) * piece : (2 * j + c + 1) * piece] for c in range(2) for j in range(subs)], axis=1
            )
        return x

    first_label = lax.axis_index("label") * 2 * half_rows
    label_no = lax.broadcasted_iota(jnp.int32, (CLUSTER, INST_BLOCK), 0).astype(jnp.int16)
    for t in range(tiles):
        for g in range(TILE // INST_BLOCK):
            blocks = [block_in(t, 2 * g + h, over, core) for h in range(2)]
            one, two = (
                relative_lanes(pos_raw[:, pl.ds(pl.multiple_of(b * INST_BLOCK, INST_BLOCK), INST_BLOCK)]) for b in blocks
            )
            if t % 2:
                pos = jnp.where(low, one, pltpu.roll(two, INST_BLOCK // 2, 1))
            else:
                pos = jnp.where(low, pltpu.roll(one, INST_BLOCK // 2, 1), two)
            local = pos - first_label
            inside = (local >= 0) & (local < 2 * half_rows)
            bits = jnp.where(inside, jnp.left_shift(1, ((local >> 7) ^ (half * clusters)) & 15), 0).astype(jnp.int16)
            at = (local & (CLUSTER - 1)).astype(jnp.int16)
            found = jnp.zeros((CLUSTER, INST_BLOCK), jnp.int16)
            for p in range(pos.shape[0]):
                found = found | jnp.where(
                    label_no == jnp.broadcast_to(at[p : p + 1], found.shape),
                    jnp.broadcast_to(bits[p : p + 1], found.shape),
                    jnp.int16(0),
                )
            group = t * (TILE // INST_BLOCK) + g
            word[:, group * INST_BLOCK : (group + 1) * INST_BLOCK] = found
            for h in range(2):
                beam[8 * h + group : 8 * h + group + 1] = beam_raw[pl.ds(blocks[h], 1)]

    row = lax.broadcasted_iota(jnp.int32, (2 * clusters, 2 * clusters * INST_BLOCK), 0)
    column = lax.broadcasted_iota(jnp.int32, (2 * clusters, 2 * clusters * INST_BLOCK), 1)
    spread = jnp.where(row == (column // INST_BLOCK) ^ (half * clusters), 0.5, 0.0).astype(BF16)
    biases = lax.dot_general(bias_raw[...], spread, (((0,), (0,)), ((), ())), preferred_element_type=F32)
    first_cluster = lax.axis_index("label") * 2 * clusters
    for k in range(2):
        for c in range(clusters):
            i = k * clusters + c
            bias_full[k, c] = biases[:, i * INST_BLOCK : (i + 1) * INST_BLOCK]
            held = jnp.where(beam[...] == first_cluster + (i ^ (half * clusters)), 0.5 * SCALE, 0.0)
            held = jnp.broadcast_to(jnp.max(held, axis=1, keepdims=True), (2 * BLOCKS, INST_BLOCK))
            mask[k, c] = jnp.where(low, held[:BLOCKS], held[BLOCKS:]).astype(BF16)
    w_copies[0].wait()

    def before(k, t, h):
        if k == 0 and h == 0:
            for copy in e_copies[t]:
                copy.wait()
            if t == 1:
                w_copies[1].start()
        elif k == 1 and h == 0:
            w_copies[1].wait()

    def emit(k, t, c, part):
        if k == 0:
            slopes_t[c * CLUSTER : (c + 1) * CLUSTER, t * TILE : (t + 1) * TILE] = part
            if t == 0:
                slopes[:, c * CLUSTER : (c + 1) * CLUSTER] = part.T
        else:
            own_slopes_t[c * CLUSTER : (c + 1) * CLUSTER] = part
            slopes[:, half_rows + c * CLUSTER : half_rows + (c + 1) * CLUSTER] = part.T
        if (k, t) == (0, tiles - 1) and (c + 1) % (CHUNK // CLUSTER) == 0:
            rows = slice((c + 1) * CLUSTER - CHUNK, (c + 1) * CLUSTER)
            label_out[rows] = jnp.dot(slopes_t[rows], embed[...], preferred_element_type=F32).astype(BF16)

    chunks = range(half_rows // CHUNK)
    jobs = [(0, t, h) for t in range(tiles) for h in chunks] + [(1, 0, h) for h in chunks]
    slope_chunks(jobs, scores, w, embed, bias_full, mask, word, before, emit)
    store_rows([row_out], slopes, w)


def store_rows(outs, slopes, w):
    sums = jnp.dot(slopes[...], w[...], preferred_element_type=F32).astype(BF16)
    count = TILE // len(outs)
    for i, out in enumerate(outs):
        out[...] = sums[i * count : (i + 1) * count].reshape(out.shape)


def row_tile(t, outs, embed, w, word, mask, bias_full, first_slopes_t, own_slopes_t, scores, slopes):
    half_rows = w.shape[0] // 2

    def emit(k, t, c, part):
        if c == 0:
            slopes[:, :half_rows] = first_slopes_t[:, t * TILE : (t + 1) * TILE].T
        own_slopes_t[c * CLUSTER : (c + 1) * CLUSTER] = part
        slopes[:, half_rows + c * CLUSTER : half_rows + (c + 1) * CLUSTER] = part.T

    jobs = [(1, t, h) for h in range(half_rows // CHUNK)]
    slope_chunks(jobs, scores, w, embed, bias_full, mask, word, lambda *job: None, emit)
    store_rows(outs, slopes, w)


def keep_rows_kernel(embed, w, word, mask, bias_full, first_slopes_t, own_slopes_t, row_out, scores, slopes):
    row_tile(1, [row_out], embed, w, word, mask, bias_full, first_slopes_t, own_slopes_t, scores, slopes)


def last_rows_kernel(embed, w, word, mask, bias_full, first_slopes_t, one_slopes_t, two_slopes_t, *rest):
    *sends, row_out, label_out, three_slopes_t, four_slopes_t, scores, slopes = rest
    shared = (embed, w, word, mask, bias_full, first_slopes_t)
    row_tile(2, sends, *shared, three_slopes_t, scores.at[0], slopes.at[0])
    row_tile(3, [row_out], *shared, four_slopes_t, scores.at[1], slopes.at[1])
    total = 0.0
    for t, part in enumerate((one_slopes_t, two_slopes_t, three_slopes_t, four_slopes_t)):
        total = total + jnp.dot(part[...], embed[t * TILE : (t + 1) * TILE], preferred_element_type=F32)
    label_out[...] = total.astype(BF16)


def sum_kernel(places, *refs):
    *terms, out = refs
    out[...] = add(*(term[at] for term, at in zip(terms, places)))


def half_sum_kernel(kept, got, out):
    out[...] = add(kept[: out.shape[0]], got[: out.shape[0]])


def finish_kernel(kept, got, summed, *refs):
    *row_terms, row_out, label_out, row, rest, sems = refs
    first = summed.shape[0]
    copies = [
        pltpu.make_async_copy(row, row_out, sems.at[0]),
        pltpu.make_async_copy(summed, label_out.at[pl.ds(0, first)], sems.at[1]),
        pltpu.make_async_copy(rest, label_out.at[pl.ds(first, rest.shape[0])], sems.at[2]),
    ]
    copies[1].start()
    row[...] = add(*(term[(0,) * (len(term.shape) - 2)] for term in row_terms))
    copies[0].start()
    rest[...] = add(kept[first:], got[first:])
    copies[2].start()
    for copy in copies:
        copy.wait()


def swapped(value, axis, size, bit):
    return lax.ppermute(value, axis, [(i, i ^ bit) for i in range(size)])


def add(*terms):
    total = terms[0].astype(F32)
    for term in terms[1:]:
        total = total + term.astype(F32)
    return total.astype(BF16)


def on_device(n_dp, n_label, embed, weight, bias, beam, positives):
    rows, features = embed.shape
    labels = weight.shape[0]
    half_rows = labels // 2
    clusters = half_rows // CLUSTER
    piece = rows // n_label
    subs = n_label // 2 // BLOCKS
    bias_rows = bias.reshape(labels // CLUSTER, CLUSTER)
    pos_rows = positives.T
    vmem = pl.BlockSpec(memory_space=pltpu.VMEM)
    hbm = pl.BlockSpec(memory_space=pltpu.HBM)
    params = pltpu.CompilerParams(vmem_limit_bytes=VMEM_LIMIT)
    shape = jax.ShapeDtypeStruct
    tile_shape = shape((half_rows, TILE), BF16)
    row_shape = shape((BLOCKS // 2, subs, piece, features), BF16)
    score_scratch = pltpu.VMEM((2, CHUNK, TILE), F32)
    slope_scratch = pltpu.VMEM((TILE, labels), BF16)

    def cost(halves):
        return pl.CostEstimate(flops=halves * 2 * rows * half_rows * features, bytes_accessed=0, transcendentals=0)

    *shared, label_send, one_slopes_t, first_send = pl.pallas_call(
        functools.partial(send_kernel, n_label),
        out_shape=[
            shape((rows, features), BF16),
            shape((labels, features), BF16),
            shape((CLUSTER, rows), jnp.int16),
            shape((2, clusters, BLOCKS, INST_BLOCK), BF16),
            shape((2, clusters, CLUSTER, INST_BLOCK), F32),
            shape((half_rows, rows), BF16),
            shape((half_rows, features), BF16),
            tile_shape,
            row_shape,
        ],
        in_specs=[hbm] * 5,
        out_specs=[vmem] * 9,
        scratch_shapes=[
            pltpu.VMEM(bias_rows.shape, BF16),
            pltpu.VMEM(beam.shape, jnp.int32),
            pltpu.VMEM(pos_rows.shape, jnp.int32),
            pltpu.VMEM((2 * BLOCKS, beam.shape[1]), jnp.int32),
            score_scratch,
            slope_scratch,
            pltpu.SemaphoreType.DMA((5 + n_label,)),
        ],
        compiler_params=params,
        cost_estimate=cost(3),
        name="send_half",
    )(*(pltpu.with_memory_space_constraint(x, pltpu.HBM) for x in (embed, weight, bias_rows, beam, pos_rows)))

    first_got = swapped(first_send, "label", n_label, 1)
    label_got = swapped(label_send, "dp", n_dp, n_dp // 2)
    first_got, *shared = lax.optimization_barrier((first_got, *shared))

    two_slopes_t, first_keep = pl.pallas_call(
        keep_rows_kernel,
        out_shape=[tile_shape, row_shape],
        in_specs=[vmem] * 6,
        out_specs=[vmem] * 2,
        scratch_shapes=[score_scratch, slope_scratch],
        compiler_params=params,
        cost_estimate=cost(0),
        name="keep_rows",
    )(*shared)

    axes = [2 * subs, 4 * subs, 8 * subs]

    def summed_at(*terms):
        arrays, places = zip(*terms)
        size = places[0].stop - places[0].start
        return pl.pallas_call(
            functools.partial(sum_kernel, places),
            out_shape=shape((size, subs, piece, features), BF16),
            in_specs=[vmem] * len(arrays),
            out_specs=vmem,
            compiler_params=params,
            cost_estimate=cost(0),
            name="row_sum",
        )(*arrays)

    def passed_on(value, stage):
        bits = (axes[stage], axes[stage if stage == 2 else 1 - stage])
        return lax.ppermute(value, "label", [(i, i ^ bits[i % 2]) for i in range(n_label)])

    far_got = passed_on(summed_at((first_keep, slice(1, 4)), (first_got, slice(1, 4))), 0)
    near_got = passed_on(summed_at((first_keep, slice(0, 1)), (first_got, slice(0, 1))), 0)

    part_shape = shape((2, subs, piece, features), BF16)
    *last_send, last_keep, label_keep = pl.pallas_call(
        last_rows_kernel,
        out_shape=[part_shape] * 2 + [row_shape, shape((half_rows, features), BF16)],
        in_specs=[vmem] * 8,
        out_specs=[vmem] * 4,
        scratch_shapes=[
            pltpu.VMEM((half_rows, TILE), BF16),
            pltpu.VMEM((half_rows, TILE), BF16),
            pltpu.VMEM((2, 2, CHUNK, TILE), F32),
            pltpu.VMEM((2, TILE, labels), BF16),
        ],
        compiler_params=params,
        cost_estimate=cost(0),
        name="last_rows",
    )(*shared, one_slopes_t, two_slopes_t)

    last_got = [swapped(part, "label", n_label, 1) for part in last_send]
    three_got = passed_on(summed_at((last_keep, slice(3, 4)), (last_got[1], slice(1, 2)), (far_got, slice(2, 3))), 1)
    two_got = passed_on(summed_at((last_keep, slice(2, 3)), (last_got[1], slice(0, 1)), (far_got, slice(1, 2))), 1)
    row_got = passed_on(summed_at((last_keep, slice(1, 2)), (last_got[0], slice(1, 2)), (far_got, slice(0, 1)), (three_got, slice(0, 1))), 2)
    row_terms = [last_keep, last_got[0], near_got, two_got, row_got]
    bit = subs
    while bit > 1:
        row_sum = add(*(term.reshape(-1, subs, piece, features)[0] for term in row_terms[:-1]))
        held = row_sum.shape[0] // 2
        came = row_terms[-1].reshape(subs, piece, features)
        incoming = swapped(add(row_sum[held:], came[held:]), "label", n_label, bit)
        row_terms = [add(row_sum[:held], came[:held]), incoming]
        subs = held
        bit //= 2

    kept, got = label_keep, label_got
    step = n_dp // 4
    at = lax.axis_index("dp")
    while step >= 1:
        label_sum = add(kept, got)
        size = label_sum.shape[0] // 2
        mine = (at // step) % 2
        outgoing = lax.dynamic_slice_in_dim(label_sum, (1 - mine) * size, size, 0)
        kept = lax.dynamic_slice_in_dim(label_sum, mine * size, size, 0)
        got = swapped(outgoing, "dp", n_dp, step)
        step //= 2

    size = kept.shape[0]
    summed = pl.pallas_call(
        half_sum_kernel,
        out_shape=shape((size // 2, features), BF16),
        in_specs=[vmem] * 2,
        out_specs=vmem,
        compiler_params=params,
        cost_estimate=cost(2),
        name="half_sum",
    )(kept, got)
    return pl.pallas_call(
        finish_kernel,
        out_shape=[shape((piece, features), BF16), shape((size, features), BF16)],
        in_specs=[vmem] * (3 + len(row_terms)),
        out_specs=[hbm] * 2,
        scratch_shapes=[
            pltpu.VMEM((piece, features), BF16),
            pltpu.VMEM((size // 2, features), BF16),
            pltpu.SemaphoreType.DMA((3,)),
        ],
        compiler_params=params,
        cost_estimate=cost(0),
        name="finish",
    )(kept, got, summed, *row_terms)


def solution(mesh):
    in_specs = (P("dp", None), P("label", None), P("label"), P("dp", None), P("dp", None))
    out_specs = (P(("dp", "label"), None), P(("label", "dp"), None))
    body = functools.partial(on_device, mesh.shape["dp"], mesh.shape["label"])
    return jax.shard_map(body, mesh=mesh, in_specs=in_specs, out_specs=out_specs, check_vma=False)
```

time: 29.9 us -> 30.6 us (1.023)
  Pallas kernels: 8.8 us -> 11.7 us
  other arithmetic: 2 us -> 0 us
  waiting for transfers between devices: 6.35 us -> 6.02 us
    ppermute x0 -> x5, starting transfers between devices: none -> 8.28 us  [passed_on(): lax.ppermute(value, 'label', [(i, i ^ bits[i % 2]) for i in range(n_label)])]
    ppermute x11 -> x4, starting transfers between devices: 11.9 us -> 3.65 us  [swapped(): return lax.ppermute(value, axis, [(i, i ^ bit) for i in range(size)])]
    ppermute x11 -> x4, waiting for transfers between devices: 6.35 us -> 2.63 us  [swapped(): return lax.ppermute(value, axis, [(i, i ^ bit) for i in range(size)])]
    ppermute x0 -> x5, waiting for transfers between devices: none -> 3.39 us  [passed_on(): lax.ppermute(value, 'label', [(i, i ^ bits[i % 2]) for i in range(n_label)])]
    convert_element_type x5 -> x0, other arithmetic: 2 us -> none  [add(): return total.astype(BF16)]
    pallas_call x1 -> x8, Pallas kernels: 2.39 us -> 4.09 us  [the longest x1 2.84 us: on_device(): pl.pallas_call(last_rows_kernel, out_shape=[part_shape] * 2 + [row_shape,...]
    pallas_call x1, Pallas kernels: 5.32 us -> 6.35 us  [on_device(): pl.pallas_call(functools.partial(send_kernel, n_label), out_shape=[shape(...]
  transfers between devices with their start and end apart: 11 -> 9, of which waited for: 5 -> 5; matrix products, arithmetic and copies ran while one was open for 4% -> 0% of each run, Pallas kernels for 12% -> 15%
where the time goes in v2:
time: 30.6 us; the launch traced here: 30.4 us
  starting transfers between devices  11.9 us (39%)
  Pallas kernels  11.7 us (38%)
  waiting for transfers between devices  6.02 us (20%)
  between operations  0.7 us (2%)
    ppermute x5, starting transfers between devices, passed_on(): lax.ppermute(value, 'label', [(i, i ^ bits[i % 2]) for i in range(n_label)])  8.28 us
    pallas_call x1, Pallas kernels, on_device(): pl.pallas_call(functools.partial(send_kernel, n_label), out_shape=[shape(...  6.35 us
    ppermute x4, starting transfers between devices, swapped(): return lax.ppermute(value, axis, [(i, i ^ bit) for i in range(size)])  3.65 us
    ppermute x5, waiting for transfers between devices, passed_on(): lax.ppermute(value, 'label', [(i, i ^ bits[i % 2]) for i in range(n_label)])  3.39 us
    pallas_call x1, Pallas kernels, on_device(): pl.pallas_call(last_rows_kernel, out_shape=[part_shape] * 2 + [row_shape,...  2.84 us
    ppermute x4, waiting for transfers between devices, swapped(): return lax.ppermute(value, axis, [(i, i ^ bit) for i in range(size)])  2.63 us
    pallas_call x1, Pallas kernels, on_device(): pl.pallas_call(keep_rows_kernel, out_shape=[tile_shape, row_shape], in_sp...  1.28 us
    pallas_call x1, Pallas kernels, on_device(): pl.pallas_call(finish_kernel, out_shape=[shape((piece, features), BF16),...  0.93 us
  transfers between devices with their start and end apart: 9, of which 5 were waited for; matrix products, arithmetic and copies ran while one was open for 0% of the time, Pallas kernels for 15%

profile of v2, /device:TPU:0, one launch (start us, length us, event | category | flops | bytes accessed | tf_op | source)
XLA Modules:
  0.0 30.4 jit_solution(2179301484604423673)
XLA Ops:
  0.6 6.4 %send_half.1 = (bf16[1024,768]{1,0:T(8,128)(2,1)S(1)}, bf16[1024,768]{1,0:T(8,128)(2,1)S(1)}, s16[128,1024]{1,0:T(8,128)(2,1)S(1)}, bf16[2,4,8,128]{3,2,1,0:T(8,...) custom-call(bf16[1024,768]{1,0:T(8,128)(2,1)} %embed_hbm.1, ...), custom_call_target="tpu_custom_call" | custom-call | flops 2415919104 | tf_op jit(solution)/shard_map/send_half/pallas_call | solution.py:293
  7.0 0.5 %collective-permute-start = (bf16[4,1,64,768]{3,2,1,0:T(8,128)(2,1)S(1)}, bf16[4,1,64,768]{3,2,1,0:T(8,128)(2,1)S(1)}, u32[]{:S(2)}, u32[]{:S(2)}) collective-permute-start(bf16[4,1,64,768]{3,2,1,0:T(8,128)(2,1)S(1)} %get-tuple-element.24), channel_id=1, source_target_pairs={{0,1},{1,0},{2,3},{3,2},{4,5},{5,4},{6,7},{7,6},{8,9},{9,8},{10,11... | collective-permute-start | bytes 1179656 | tf_op jit(solution)/shard_map/ppermute | solution.py:262
  7.5 2.6 %collective-permute-start.1 = (bf16[512,768]{1,0:T(8,128)(2,1)S(1)}, bf16[512,768]{1,0:T(8,128)(2,1)S(1)}, u32[]{:S(2)}, u32[]{:S(2)}) collective-permute-start(bf16[512,768]{1,0:T(8,128)(2,1)S(1)} %get-tuple-element.40), channel_id=1, source_target_pairs={{0,16},{16,0},{1,17},{17,1},{2,18},{18,2},{3,19},{19,3},{4,20},{20... | collective-permute-start | bytes 2359304 | tf_op jit(solution)/shard_map/ppermute | solution.py:262
  10.1 0.0 collective-permute-done.refs_1_
  10.1 1.3 %keep_rows.1 = (bf16[512,256]{1,0:T(8,128)(2,1)S(1)}, bf16[4,1,64,768]{3,2,1,0:T(8,128)(2,1)S(1)}) custom-call(bf16[1024,768]{1,0:T(8,128)(2,1)S(1)} %get-tuple-element.31.embed, bf16[1024,768]{1,0:T(8,128)(2,1)S(1)} %get-tuple-element.32.w, s16[128,1024]{1,0:T(8,128)(2,1)S(1)} %get-tuple-element.33.word, bf16[2,4,8,128]{3,2,1,0:T(8,128)(2,1)S(1)} %get-tuple-element.34.mask, ...), custom_call_target="tpu_custom_call" | custom-call | tf_op jit(solution)/shard_map/keep_rows/pallas_call | solution.py:326
  11.4 0.1 row_sum.6
  11.4 1.7 %collective-permute-start.5 = (bf16[3,1,64,768]{3,2,1,0:T(8,128)(2,1)S(1)}, bf16[3,1,64,768]{3,2,1,0:T(8,128)(2,1)S(1)}, u32[]{:S(2)}, u32[]{:S(2)}) collective-permute-start(bf16[3,1,64,768]{3,2,1,0:T(8,128)(2,1)S(1)} %row_sum.6), channel_id=1, source_target_pairs={{0,2},{1,5},{2,0},{3,7},{4,6},{5,1},{6,4},{7,3},{8,10},{9,13},{10,... | collective-permute-start | bytes 884744 | tf_op jit(solution)/shard_map/ppermute | solution.py:354
  13.2 2.8 %last_rows.1 = (bf16[2,1,64,768]{3,2,1,0:T(8,128)(2,1)S(1)}, bf16[2,1,64,768]{3,2,1,0:T(8,128)(2,1)S(1)}, bf16[4,1,64,768]{3,2,1,0:T(8,128)(2,1)S(1)}, bf16[512,768]{1,0:T(8,128)(2,1)S(1)}) custom-call(bf16[1024,768]{1,0:T(8,128)(2,1)S(1)} %get-tuple-element.31.embed, bf16[1024,768]{1,0:T(8,128)(2,1)S(1)} %get-tuple-element.32.w, ...), custom_call_target="tpu_custom_call" | custom-call | tf_op jit(solution)/shard_map/last_rows/pallas_call | solution.py:360
  16.0 0.1 collective-permute-start.4
  16.1 0.5 %collective-permute-start.2 = (bf16[2,1,64,768]{3,2,1,0:T(8,128)(2,1)S(1)}, bf16[2,1,64,768]{3,2,1,0:T(8,128)(2,1)S(1)}, u32[]{:S(2)}, u32[]{:S(2)}) collective-permute-start(bf16[2,1,64,768]{3,2,1,0:T(8,128)(2,1)S(1)} %get-tuple-element.42), channel_id=1, source_target_pairs={{0,1},{1,0},{2,3},{3,2},{4,5},{5,4},{6,7},{7,6},{8,9},{9,8},{10,11... | collective-permute-start | bytes 589832 | tf_op jit(solution)/shard_map/ppermute | solution.py:262
  16.6 0.9 %collective-permute-done.4.refs_1_ = bf16[2,1,64,768]{3,2,1,0:T(8,128)(2,1)S(1)} collective-permute-done((bf16[2,1,64,768]{3,2,1,0:T(8,128)(2,1)S(1)}, bf16[2,1,64,768]{3,2,1,0:T(8,128)(2,1)S(1)}, u32[]{:S(2)}, u32[]{:S(2)}) %collective-permute-start.4) | collective-permute-done | bytes 196640 | tf_op jit(solution)/shard_map/ppermute | solution.py:262
  17.5 0.7 %collective-permute-done.5.refs_2_ = bf16[3,1,64,768]{3,2,1,0:T(8,128)(2,1)S(1)} collective-permute-done((bf16[3,1,64,768]{3,2,1,0:T(8,128)(2,1)S(1)}, bf16[3,1,64,768]{3,2,1,0:T(8,128)(2,1)S(1)}, u32[]{:S(2)}, u32[]{:S(2)}) %collective-permute-start.5) | collective-permute-done | bytes 294944 | tf_op jit(solution)/shard_map/ppermute | solution.py:354
  18.3 1.8 %collective-permute-start.7 = (bf16[1,1,64,768]{3,2,1,0:T(8,128)(2,1)S(1)}, bf16[1,1,64,768]{3,2,1,0:T(8,128)(2,1)S(1)}, u32[]{:S(2)}, u32[]{:S(2)}) collective-permute-start(bf16[1,1,64,768]{3,2,1,0:T(8,128)(2,1)S(1)} %row_sum.8), channel_id=1, source_target_pairs={{0,4},{1,3},{2,6},{3,1},{4,0},{5,7},{6,2},{7,5},{8,12},{9,11},{10,... | collective-permute-start | bytes 294920 | tf_op jit(solution)/shard_map/ppermute | solution.py:354
  20.1 1.6 %collective-permute-start.3 = (bf16[1,1,64,768]{3,2,1,0:T(8,128)(2,1)S(1)}, bf16[1,1,64,768]{3,2,1,0:T(8,128)(2,1)S(1)}, u32[]{:S(2)}, u32[]{:S(2)}) collective-permute-start(bf16[1,1,64,768]{3,2,1,0:T(8,128)(2,1)S(1)} %row_sum.5), channel_id=1, source_target_pairs={{0,2},{1,5},{2,0},{3,7},{4,6},{5,1},{6,4},{7,3},{8,10},{9,13},{10,... | collective-permute-start | bytes 294920 | tf_op jit(solution)/shard_map/ppermute | solution.py:354
  21.7 0.5 %collective-permute-start.6 = (bf16[1,1,64,768]{3,2,1,0:T(8,128)(2,1)S(1)}, bf16[1,1,64,768]{3,2,1,0:T(8,128)(2,1)S(1)}, u32[]{:S(2)}, u32[]{:S(2)}) collective-permute-start(bf16[1,1,64,768]{3,2,1,0:T(8,128)(2,1)S(1)} %row_sum.7), channel_id=1, source_target_pairs={{0,4},{1,3},{2,6},{3,1},{4,0},{5,7},{6,2},{7,5},{8,12},{9,11},{10,... | collective-permute-start | bytes 294920 | tf_op jit(solution)/shard_map/ppermute | solution.py:354
  22.2 0.0 collective-permute-done.2.refs_1_
  22.2 1.6 %collective-permute-done.7.refs_3_ = bf16[1,1,64,768]{3,2,1,0:T(8,128)(2,1)S(1)} collective-permute-done((bf16[1,1,64,768]{3,2,1,0:T(8,128)(2,1)S(1)}, bf16[1,1,64,768]{3,2,1,0:T(8,128)(2,1)S(1)}, u32[]{:S(2)}, u32[]{:S(2)}) %collective-permute-start.7) | collective-permute-done | bytes 98336 | tf_op jit(solution)/shard_map/ppermute | solution.py:354
  23.8 0.1 row_sum.9
  23.9 2.7 %collective-permute-start.8 = (bf16[1,1,64,768]{3,2,1,0:T(8,128)(2,1)S(1)}, bf16[1,1,64,768]{3,2,1,0:T(8,128)(2,1)S(1)}, u32[]{:S(2)}, u32[]{:S(2)}) collective-permute-start(bf16[1,1,64,768]{3,2,1,0:T(8,128)(2,1)S(1)} %row_sum.9), channel_id=1, source_target_pairs={{0,8},{1,9},{2,10},{3,11},{4,12},{5,13},{6,14},{7,15},{8,0},{9,1},... | collective-permute-start | bytes 294920 | tf_op jit(solution)/shard_map/ppermute | solution.py:354
  26.5 1.7 %collective-permute-done.1.got = bf16[512,768]{1,0:T(8,128)(2,1)S(1)} collective-permute-done((bf16[512,768]{1,0:T(8,128)(2,1)S(1)}, bf16[512,768]{1,0:T(8,128)(2,1)S(1)}, u32[]{:S(2)}, u32[]{:S(2)}) %collective-permute-start.1) | collective-permute-done | bytes 786464 | tf_op jit(solution)/shard_map/ppermute | solution.py:262
  28.2 0.1 half_sum.1.summed
  28.3 0.0 collective-permute-done.3.refs_2_
  28.3 0.0 collective-permute-done.6.refs_3_
  28.3 1.1 %collective-permute-done.8.refs_4_ = bf16[1,1,64,768]{3,2,1,0:T(8,128)(2,1)S(1)} collective-permute-done((bf16[1,1,64,768]{3,2,1,0:T(8,128)(2,1)S(1)}, bf16[1,1,64,768]{3,2,1,0:T(8,128)(2,1)S(1)}, u32[]{:S(2)}, u32[]{:S(2)}) %collective-permute-start.8) | collective-permute-done | bytes 98336 | tf_op jit(solution)/shard_map/ppermute | solution.py:354
  29.4 0.9 %finish.1 = (bf16[64,768]{1,0:T(8,128)(2,1)}, bf16[512,768]{1,0:T(8,128)(2,1)}) custom-call(bf16[512,768]{1,0:T(8,128)(2,1)S(1)} %get-tuple-element.39.kept, bf16[512,768]{1,0:T(8,128)(2,1)S(1)} %collective-permute-done.1.got, bf16[256,768]{1,0:T(8,128)(2,1)S(1)} %half_sum.1.summed, bf16[4,1,64,768]{3,2,1,0:T(8,128)(2,1)S(1)} %get-tuple-element.41.refs_0_, ...), custom_call_target="tpu_custom_call" | custom-call | tf_op jit(solution)/shard_map/finish/pallas_call | solution.py:413
  (3 shorter events, 0.1 us)
Async XLA Ops:
  7.0 3.1 %collective-permute-start = (bf16[4,1,64,768]{3,2,1,0:T(8,128)(2,1)S(1)}, bf16[4,1,64,768]{3,2,1,0:T(8,128)(2,1)S(1)}, u32[]{:S(2)}, u32[]{:S(2)}) collective-permute-start(bf16[4,1,64,768]{3,2,1,0:T(8,128)(2,1)S(1)} %get-tuple-element.24), channel_id=1, source_target_pairs={{0,1},{1,0},{2,3},{3,2},{4,5},{5,4},{6,7},{7,6},{8,9},{9,8},{10,11... | collective-permute-start | bytes 1179656 | tf_op jit(solution)/shard_map/ppermute | solution.py:262
  7.5 20.7 %collective-permute-start.1 = (bf16[512,768]{1,0:T(8,128)(2,1)S(1)}, bf16[512,768]{1,0:T(8,128)(2,1)S(1)}, u32[]{:S(2)}, u32[]{:S(2)}) collective-permute-start(bf16[512,768]{1,0:T(8,128)(2,1)S(1)} %get-tuple-element.40), channel_id=1, source_target_pairs={{0,16},{16,0},{1,17},{17,1},{2,18},{18,2},{3,19},{19,3},{4,20},{20... | collective-permute-start | bytes 2359304 | tf_op jit(solution)/shard_map/ppermute | solution.py:262
  11.4 6.8 %collective-permute-start.5 = (bf16[3,1,64,768]{3,2,1,0:T(8,128)(2,1)S(1)}, bf16[3,1,64,768]{3,2,1,0:T(8,128)(2,1)S(1)}, u32[]{:S(2)}, u32[]{:S(2)}) collective-permute-start(bf16[3,1,64,768]{3,2,1,0:T(8,128)(2,1)S(1)} %row_sum.6), channel_id=1, source_target_pairs={{0,2},{1,5},{2,0},{3,7},{4,6},{5,1},{6,4},{7,3},{8,10},{9,13},{10,... | collective-permute-start | bytes 884744 | tf_op jit(solution)/shard_map/ppermute | solution.py:354
  16.0 1.5 %collective-permute-start.4 = (bf16[2,1,64,768]{3,2,1,0:T(8,128)(2,1)S(1)}, bf16[2,1,64,768]{3,2,1,0:T(8,128)(2,1)S(1)}, u32[]{:S(2)}, u32[]{:S(2)}) collective-permute-start(bf16[2,1,64,768]{3,2,1,0:T(8,128)(2,1)S(1)} %get-tuple-element.45), channel_id=1, source_target_pairs={{0,1},{1,0},{2,3},{3,2},{4,5},{5,4},{6,7},{7,6},{8,9},{9,8},{10,11... | collective-permute-start | bytes 589832 | tf_op jit(solution)/shard_map/ppermute | solution.py:262
  16.1 6.1 %collective-permute-start.2 = (bf16[2,1,64,768]{3,2,1,0:T(8,128)(2,1)S(1)}, bf16[2,1,64,768]{3,2,1,0:T(8,128)(2,1)S(1)}, u32[]{:S(2)}, u32[]{:S(2)}) collective-permute-start(bf16[2,1,64,768]{3,2,1,0:T(8,128)(2,1)S(1)} %get-tuple-element.42), channel_id=1, source_target_pairs={{0,1},{1,0},{2,3},{3,2},{4,5},{5,4},{6,7},{7,6},{8,9},{9,8},{10,11... | collective-permute-start | bytes 589832 | tf_op jit(solution)/shard_map/ppermute | solution.py:262
  18.3 5.5 %collective-permute-start.7 = (bf16[1,1,64,768]{3,2,1,0:T(8,128)(2,1)S(1)}, bf16[1,1,64,768]{3,2,1,0:T(8,128)(2,1)S(1)}, u32[]{:S(2)}, u32[]{:S(2)}) collective-permute-start(bf16[1,1,64,768]{3,2,1,0:T(8,128)(2,1)S(1)} %row_sum.8), channel_id=1, source_target_pairs={{0,4},{1,3},{2,6},{3,1},{4,0},{5,7},{6,2},{7,5},{8,12},{9,11},{10,... | collective-permute-start | bytes 294920 | tf_op jit(solution)/shard_map/ppermute | solution.py:354
  20.1 8.2 %collective-permute-start.3 = (bf16[1,1,64,768]{3,2,1,0:T(8,128)(2,1)S(1)}, bf16[1,1,64,768]{3,2,1,0:T(8,128)(2,1)S(1)}, u32[]{:S(2)}, u32[]{:S(2)}) collective-permute-start(bf16[1,1,64,768]{3,2,1,0:T(8,128)(2,1)S(1)} %row_sum.5), channel_id=1, source_target_pairs={{0,2},{1,5},{2,0},{3,7},{4,6},{5,1},{6,4},{7,3},{8,10},{9,13},{10,... | collective-permute-start | bytes 294920 | tf_op jit(solution)/shard_map/ppermute | solution.py:354
  21.7 6.6 %collective-permute-start.6 = (bf16[1,1,64,768]{3,2,1,0:T(8,128)(2,1)S(1)}, bf16[1,1,64,768]{3,2,1,0:T(8,128)(2,1)S(1)}, u32[]{:S(2)}, u32[]{:S(2)}) collective-permute-start(bf16[1,1,64,768]{3,2,1,0:T(8,128)(2,1)S(1)} %row_sum.7), channel_id=1, source_target_pairs={{0,4},{1,3},{2,6},{3,1},{4,0},{5,7},{6,2},{7,5},{8,12},{9,11},{10,... | collective-permute-start | bytes 294920 | tf_op jit(solution)/shard_map/ppermute | solution.py:354
  23.9 5.6 %collective-permute-start.8 = (bf16[1,1,64,768]{3,2,1,0:T(8,128)(2,1)S(1)}, bf16[1,1,64,768]{3,2,1,0:T(8,128)(2,1)S(1)}, u32[]{:S(2)}, u32[]{:S(2)}) collective-permute-start(bf16[1,1,64,768]{3,2,1,0:T(8,128)(2,1)S(1)} %row_sum.9), channel_id=1, source_target_pairs={{0,8},{1,9},{2,10},{3,11},{4,12},{5,13},{6,14},{7,15},{8,0},{9,1},... | collective-permute-start | bytes 294920 | tf_op jit(solution)/shard_map/ppermute | solution.py:354

commit v3 on v2

--- a/solution.py
+++ b/solution.py
@@ -10,7 +10,8 @@
 INST_BLOCK = 128
 CLUSTER = 128
 TILE = 256
-CHUNK = 128
+CHUNK = 256
+CLUSTERS = 8
 BLOCKS = 8
 SCALE = 0.125
 
@@ -67,9 +68,30 @@
     return (first + 2 * second + 4 * third + owner * (first - second)) ^ over
 
 
-def send_kernel(n_label, embed_hbm, weight_hbm, bias_hbm, beam_hbm, pos_hbm, embed, w, word, mask, bias_full, slopes_t,
-                label_out, own_slopes_t, row_out, bias_raw, beam_raw, pos_raw, beam, scores, slopes, sems):
-    half_rows = label_out.shape[0]
+def set_words(tiles, pos_ref, word):
+    half_rows = CLUSTER * CLUSTERS // 2
+    first_label = lax.axis_index("label") * 2 * half_rows
+    send_half = 1 - half_index()
+    label_no = lax.broadcasted_iota(jnp.int32, (CLUSTER, TILE), 0).astype(jnp.int16)
+    for t in tiles:
+        lanes = slice(t * TILE, (t + 1) * TILE)
+        local = pos_ref[:, lanes] - first_label
+        inside = (local >= 0) & (local < 2 * half_rows)
+        bits = jnp.where(inside, jnp.left_shift(1, ((local >> 7) ^ (send_half * (CLUSTERS // 2))) & 15), 0).astype(jnp.int16)
+        at = (local & (CLUSTER - 1)).astype(jnp.int16)
+        found = jnp.zeros((CLUSTER, TILE), jnp.int16)
+        for p in range(pos_ref.shape[0]):
+            found = found | jnp.where(
+                label_no == jnp.broadcast_to(at[p : p + 1], found.shape),
+                jnp.broadcast_to(bits[p : p + 1], found.shape),
+                jnp.int16(0),
+            )
+        word[:, lanes] = found
+
+
+def first_kernel(n_label, embed_hbm, weight_hbm, bias_hbm, beam_hbm, pos_hbm, embed, w, pos, mask, bias_full,
+                 first_slopes_t, own_slopes_t, row_out, bias_raw, beam_raw, pos_raw, beam, word, scores, slopes, sems):
+    half_rows = own_slopes_t.shape[0]
     clusters = half_rows // CLUSTER
     tiles = embed.shape[0] // TILE
     half = 1 - half_index()
@@ -103,11 +125,11 @@
                         sems.at[5 + at],
                     )
                 )
-    for copy in (*small, *e_copies[0], w_copies[0], *e_copies[1]):
+    for copy in (*small, *e_copies[0], *w_copies):
         copy.start()
     for copy in small:
         copy.wait()
-    for copy in (*e_copies[2], *e_copies[3]):
+    for copy in (*e_copies[1], *e_copies[2], *e_copies[3]):
         copy.start()
 
     lane = lax.broadcasted_iota(jnp.int32, (BLOCKS, INST_BLOCK), 1)
@@ -127,33 +149,21 @@
             )
         return x
 
-    first_label = lax.axis_index("label") * 2 * half_rows
-    label_no = lax.broadcasted_iota(jnp.int32, (CLUSTER, INST_BLOCK), 0).astype(jnp.int16)
     for t in range(tiles):
         for g in range(TILE // INST_BLOCK):
             blocks = [block_in(t, 2 * g + h, over, core) for h in range(2)]
             one, two = (
                 relative_lanes(pos_raw[:, pl.ds(pl.multiple_of(b * INST_BLOCK, INST_BLOCK), INST_BLOCK)]) for b in blocks
             )
-            if t % 2:
-                pos = jnp.where(low, one, pltpu.roll(two, INST_BLOCK // 2, 1))
-            else:
-                pos = jnp.where(low, pltpu.roll(one, INST_BLOCK // 2, 1), two)
-            local = pos - first_label
-            inside = (local >= 0) & (local < 2 * half_rows)
-            bits = jnp.where(inside, jnp.left_shift(1, ((local >> 7) ^ (half * clusters)) & 15), 0).astype(jnp.int16)
-            at = (local & (CLUSTER - 1)).astype(jnp.int16)
-            found = jnp.zeros((CLUSTER, INST_BLOCK), jnp.int16)
-            for p in range(pos.shape[0]):
-                found = found | jnp.where(
-                    label_no == jnp.broadcast_to(at[p : p + 1], found.shape),
-                    jnp.broadcast_to(bits[p : p + 1], found.shape),
-                    jnp.int16(0),
-                )
             group = t * (TILE // INST_BLOCK) + g
-            word[:, group * INST_BLOCK : (group + 1) * INST_BLOCK] = found
+            pos[:, group * INST_BLOCK : (group + 1) * INST_BLOCK] = (
+                jnp.where(low, one, pltpu.roll(two, INST_BLOCK // 2, 1))
+                if t % 2
+                else jnp.where(low, pltpu.roll(one, INST_BLOCK // 2, 1), two)
+            )
             for h in range(2):
                 beam[8 * h + group : 8 * h + group + 1] = beam_raw[pl.ds(blocks[h], 1)]
+    set_words([0], pos, word)
 
     row = lax.broadcasted_iota(jnp.int32, (2 * clusters, 2 * clusters * INST_BLOCK), 0)
     column = lax.broadcasted_iota(jnp.int32, (2 * clusters, 2 * clusters * INST_BLOCK), 1)
@@ -167,33 +177,41 @@
             held = jnp.where(beam[...] == first_cluster + (i ^ (half * clusters)), 0.5 * SCALE, 0.0)
             held = jnp.broadcast_to(jnp.max(held, axis=1, keepdims=True), (2 * BLOCKS, INST_BLOCK))
             mask[k, c] = jnp.where(low, held[:BLOCKS], held[BLOCKS:]).astype(BF16)
-    w_copies[0].wait()
+    for copy in (w_copies[0], *e_copies[0]):
+        copy.wait()
 
     def before(k, t, h):
-        if k == 0 and h == 0:
-            for copy in e_copies[t]:
-                copy.wait()
-            if t == 1:
-                w_copies[1].start()
-        elif k == 1 and h == 0:
+        if (k, h) == (1, 0):
             w_copies[1].wait()
 
     def emit(k, t, c, part):
-        if k == 0:
-            slopes_t[c * CLUSTER : (c + 1) * CLUSTER, t * TILE : (t + 1) * TILE] = part
-            if t == 0:
-                slopes[:, c * CLUSTER : (c + 1) * CLUSTER] = part.T
-        else:
-            own_slopes_t[c * CLUSTER : (c + 1) * CLUSTER] = part
-            slopes[:, half_rows + c * CLUSTER : half_rows + (c + 1) * CLUSTER] = part.T
-        if (k, t) == (0, tiles - 1) and (c + 1) % (CHUNK // CLUSTER) == 0:
-            rows = slice((c + 1) * CLUSTER - CHUNK, (c + 1) * CLUSTER)
-            label_out[rows] = jnp.dot(slopes_t[rows], embed[...], preferred_element_type=F32).astype(BF16)
-
-    chunks = range(half_rows // CHUNK)
-    jobs = [(0, t, h) for t in range(tiles) for h in chunks] + [(1, 0, h) for h in chunks]
+        out = own_slopes_t if k else first_slopes_t
+        out[c * CLUSTER : (c + 1) * CLUSTER] = part
+        slopes[:, (k * clusters + c) * CLUSTER : (k * clusters + c + 1) * CLUSTER] = part.T
+
+    jobs = [(k, 0, h) for k in range(2) for h in range(half_rows // CHUNK)]
     slope_chunks(jobs, scores, w, embed, bias_full, mask, word, before, emit)
     store_rows([row_out], slopes, w)
+    for copy in (*e_copies[1], *e_copies[2], *e_copies[3]):
+        copy.wait()
+
+
+def label_kernel(embed, w, pos, mask, bias_full, one_slopes_t, word, slopes_t, label_out, scores):
+    half_rows = label_out.shape[0]
+    tiles = embed.shape[0] // TILE
+    set_words(range(1, tiles), pos, word)
+
+    def emit(k, t, c, part):
+        slopes_t[c * CLUSTER : (c + 1) * CLUSTER, (t - 1) * TILE : t * TILE] = part
+        if t == tiles - 1 and (c + 1) % (CHUNK // CLUSTER) == 0:
+            rows = slice((c + 1) * CLUSTER - CHUNK, (c + 1) * CLUSTER)
+            label_out[rows] = (
+                jnp.dot(one_slopes_t[rows], embed[:TILE], preferred_element_type=F32)
+                + jnp.dot(slopes_t[rows], embed[TILE:], preferred_element_type=F32)
+            ).astype(BF16)
+
+    jobs = [(0, t, h) for t in range(1, tiles) for h in range(half_rows // CHUNK)]
+    slope_chunks(jobs, scores, w, embed, bias_full, mask, word, lambda *job: None, emit)
 
 
 def store_rows(outs, slopes, w):
@@ -208,7 +226,7 @@
 
     def emit(k, t, c, part):
         if c == 0:
-            slopes[:, :half_rows] = first_slopes_t[:, t * TILE : (t + 1) * TILE].T
+            slopes[:, :half_rows] = first_slopes_t[:, (t - 1) * TILE : t * TILE].T
         own_slopes_t[c * CLUSTER : (c + 1) * CLUSTER] = part
         slopes[:, half_rows + c * CLUSTER : half_rows + (c + 1) * CLUSTER] = part.T
 
@@ -290,36 +308,54 @@
     def cost(halves):
         return pl.CostEstimate(flops=halves * 2 * rows * half_rows * features, bytes_accessed=0, transcendentals=0)
 
-    *shared, label_send, one_slopes_t, first_send = pl.pallas_call(
-        functools.partial(send_kernel, n_label),
+    *common, head_slopes_t, one_slopes_t, first_send = pl.pallas_call(
+        functools.partial(first_kernel, n_label),
         out_shape=[
             shape((rows, features), BF16),
             shape((labels, features), BF16),
-            shape((CLUSTER, rows), jnp.int16),
+            shape(pos_rows.shape, jnp.int32),
             shape((2, clusters, BLOCKS, INST_BLOCK), BF16),
             shape((2, clusters, CLUSTER, INST_BLOCK), F32),
-            shape((half_rows, rows), BF16),
-            shape((half_rows, features), BF16),
+            tile_shape,
             tile_shape,
             row_shape,
         ],
         in_specs=[hbm] * 5,
-        out_specs=[vmem] * 9,
+        out_specs=[vmem] * 8,
         scratch_shapes=[
             pltpu.VMEM(bias_rows.shape, BF16),
             pltpu.VMEM(beam.shape, jnp.int32),
             pltpu.VMEM(pos_rows.shape, jnp.int32),
             pltpu.VMEM((2 * BLOCKS, beam.shape[1]), jnp.int32),
+            pltpu.VMEM((CLUSTER, TILE), jnp.int16),
             score_scratch,
             slope_scratch,
             pltpu.SemaphoreType.DMA((5 + n_label,)),
         ],
         compiler_params=params,
-        cost_estimate=cost(3),
+        cost_estimate=cost(2),
+        name="first_rows",
+    )(*(pltpu.with_memory_space_constraint(x, pltpu.HBM) for x in (embed, weight, bias_rows, beam, pos_rows)))
+
+    first_got = swapped(first_send, "label", n_label, 1)
+
+    word, first_slopes_t, label_send = pl.pallas_call(
+        label_kernel,
+        out_shape=[
+            shape((CLUSTER, rows), jnp.int16),
+            shape((half_rows, rows - TILE), BF16),
+            shape((half_rows, features), BF16),
+        ],
+        in_specs=[vmem] * 6,
+        out_specs=[vmem] * 3,
+        scratch_shapes=[score_scratch],
+        compiler_params=params,
+        cost_estimate=cost(0),
         name="send_half",
-    )(*(pltpu.with_memory_space_constraint(x, pltpu.HBM) for x in (embed, weight, bias_rows, beam, pos_rows)))
-
-    first_got = swapped(first_send, "label", n_label, 1)
+    )(*common, head_slopes_t)
+    embed_own, w, _, mask, bias_full = common
+    shared = (embed_own, w, word, mask, bias_full, first_slopes_t)
+
     label_got = swapped(label_send, "dp", n_dp, n_dp // 2)
     first_got, *shared = lax.optimization_barrier((first_got, *shared))
 

time: 30.6 us -> 28.8 us (0.941)
  Pallas kernels: 11.7 us -> 9.53 us
  waiting for transfers between devices: 6.02 us -> 6.7 us
    pallas_call x1 -> x2, Pallas kernels: 6.35 us -> 4.82 us  [the longest x1 3.18 us: on_device(): pl.pallas_call(functools.partial(first_kernel, n_label), out_shape=[shape...]
    pallas_call x1, Pallas kernels: 2.84 us -> 2.38 us  [on_device(): pl.pallas_call(last_rows_kernel, out_shape=[part_shape] * 2 + [row_shape,...]
    ppermute x5, waiting for transfers between devices: 3.39 us -> 3.73 us  [passed_on(): lax.ppermute(value, 'label', [(i, i ^ bits[i % 2]) for i in range(n_label)])]
    ppermute x4, waiting for transfers between devices: 2.63 us -> 2.96 us  [swapped(): return lax.ppermute(value, axis, [(i, i ^ bit) for i in range(size)])]
  transfers between devices with their start and end apart: 9 -> 9, of which waited for: 5 -> 5; matrix products, arithmetic and copies ran while one was open for 0% -> 0% of each run, Pallas kernels for 15% -> 19%
where the time goes in v3:
time: 28.8 us; the launch traced here: 28.6 us
  starting transfers between devices  11.6 us (40%)
  Pallas kernels  9.53 us (33%)
  waiting for transfers between devices  6.7 us (23%)
  between operations  0.71 us (2%)
    ppermute x5, starting transfers between devices, passed_on(): lax.ppermute(value, 'label', [(i, i ^ bits[i % 2]) for i in range(n_label)])  8 us
    ppermute x5, waiting for transfers between devices, passed_on(): lax.ppermute(value, 'label', [(i, i ^ bits[i % 2]) for i in range(n_label)])  3.73 us
    ppermute x4, starting transfers between devices, swapped(): return lax.ppermute(value, axis, [(i, i ^ bit) for i in range(size)])  3.65 us
    pallas_call x1, Pallas kernels, on_device(): pl.pallas_call(functools.partial(first_kernel, n_label), out_shape=[shape...  3.18 us
    ppermute x4, waiting for transfers between devices, swapped(): return lax.ppermute(value, axis, [(i, i ^ bit) for i in range(size)])  2.96 us
    pallas_call x1, Pallas kernels, on_device(): pl.pallas_call(last_rows_kernel, out_shape=[part_shape] * 2 + [row_shape,...  2.38 us
    pallas_call x1, Pallas kernels, on_device(): pl.pallas_call(label_kernel, out_shape=[shape((CLUSTER, rows), jnp.int16)...  1.64 us
    pallas_call x1, Pallas kernels, on_device(): pl.pallas_call(keep_rows_kernel, out_shape=[tile_shape, row_shape], in_sp...  1.08 us
  transfers between devices with their start and end apart: 9, of which 5 were waited for; matrix products, arithmetic and copies ran while one was open for 0% of the time, Pallas kernels for 19%

profile of v3, /device:TPU:0, one launch (start us, length us, event | category | flops | bytes accessed | tf_op | source)
XLA Modules:
  0.0 28.6 jit_solution(5071567883256826950)
XLA Ops:
  0.6 3.2 %first_rows.1 = (bf16[1024,768]{1,0:T(8,128)(2,1)S(1)}, bf16[1024,768]{1,0:T(8,128)(2,1)S(1)}, s32[8,1024]{1,0:T(8,128)S(1)}, bf16[2,4,8,128]{3,2,1,0:T(8,128)(2...) custom-call(bf16[1024,768]{1,0:T(8,128)(2,1)} %embed_hbm.1, ...), custom_call_target="tpu_custom_call" | custom-call | flops 1610612736 | tf_op jit(solution)/shard_map/first_rows/pallas_call | solution.py:311
  3.8 0.5 %collective-permute-start = (bf16[4,1,64,768]{3,2,1,0:T(8,128)(2,1)S(1)}, bf16[4,1,64,768]{3,2,1,0:T(8,128)(2,1)S(1)}, u32[]{:S(2)}, u32[]{:S(2)}) collective-permute-start(bf16[4,1,64,768]{3,2,1,0:T(8,128)(2,1)S(1)} %get-tuple-element.26), channel_id=1, source_target_pairs={{0,1},{1,0},{2,3},{3,2},{4,5},{5,4},{6,7},{7,6},{8,9},{9,8},{10,11... | collective-permute-start | bytes 1179656 | tf_op jit(solution)/shard_map/ppermute | solution.py:280
  4.3 1.6 %send_half.1 = (s16[128,1024]{1,0:T(8,128)(2,1)S(1)}, bf16[512,768]{1,0:T(8,128)(2,1)S(1)}, bf16[512,768]{1,0:T(8,128)(2,1)S(1)}) custom-call(bf16[1024,768]{1,0:T(8,128)(2,1)S(1)} %get-tuple-element.35.embed, bf16[1024,768]{1,0:T(8,128)(2,1)S(1)} %get-tuple-element.36.w, s32[8,1024]{1,0:T(8,128)S(1)} %get-tuple-element.29.pos, ...), custom_call_target="tpu_custom_call" | custom-call | tf_op jit(solution)/shard_map/send_half/pallas_call | solution.py:342
  6.0 2.6 %collective-permute-start.1 = (bf16[512,768]{1,0:T(8,128)(2,1)S(1)}, bf16[512,768]{1,0:T(8,128)(2,1)S(1)}, u32[]{:S(2)}, u32[]{:S(2)}) collective-permute-start(bf16[512,768]{1,0:T(8,128)(2,1)S(1)} %get-tuple-element.44), channel_id=1, source_target_pairs={{0,16},{16,0},{1,17},{17,1},{2,18},{18,2},{3,19},{19,3},{4,20},{20... | collective-permute-start | bytes 2359304 | tf_op jit(solution)/shard_map/ppermute | solution.py:280
  8.5 0.0 collective-permute-done.refs_1_
  8.6 1.1 %keep_rows.1 = (bf16[512,256]{1,0:T(8,128)(2,1)S(1)}, bf16[4,1,64,768]{3,2,1,0:T(8,128)(2,1)S(1)}) custom-call(bf16[1024,768]{1,0:T(8,128)(2,1)S(1)} %get-tuple-element.35.embed, bf16[1024,768]{1,0:T(8,128)(2,1)S(1)} %get-tuple-element.36.w, s16[128,1024]{1,0:T(8,128)(2,1)S(1)} %get-tuple-element.37.word, bf16[2,4,8,128]{3,2,1,0:T(8,128)(2,1)S(1)} %get-tuple-element.38.mask, ...), custom_call_target="tpu_custom_call" | custom-call | tf_op jit(solution)/shard_map/keep_rows/pallas_call | solution.py:362
  9.6 0.1 row_sum.6
  9.7 1.6 %collective-permute-start.5 = (bf16[3,1,64,768]{3,2,1,0:T(8,128)(2,1)S(1)}, bf16[3,1,64,768]{3,2,1,0:T(8,128)(2,1)S(1)}, u32[]{:S(2)}, u32[]{:S(2)}) collective-permute-start(bf16[3,1,64,768]{3,2,1,0:T(8,128)(2,1)S(1)} %row_sum.6), channel_id=1, source_target_pairs={{0,2},{1,5},{2,0},{3,7},{4,6},{5,1},{6,4},{7,3},{8,10},{9,13},{10,... | collective-permute-start | bytes 884744 | tf_op jit(solution)/shard_map/ppermute | solution.py:390
  11.3 2.4 %last_rows.1 = (bf16[2,1,64,768]{3,2,1,0:T(8,128)(2,1)S(1)}, bf16[2,1,64,768]{3,2,1,0:T(8,128)(2,1)S(1)}, bf16[4,1,64,768]{3,2,1,0:T(8,128)(2,1)S(1)}, bf16[512,768]{1,0:T(8,128)(2,1)S(1)}) custom-call(bf16[1024,768]{1,0:T(8,128)(2,1)S(1)} %get-tuple-element.35.embed, bf16[1024,768]{1,0:T(8,128)(2,1)S(1)} %get-tuple-element.36.w, ...), custom_call_target="tpu_custom_call" | custom-call | tf_op jit(solution)/shard_map/last_rows/pallas_call | solution.py:396
  13.7 0.1 collective-permute-start.4
  13.8 0.5 %collective-permute-start.2 = (bf16[2,1,64,768]{3,2,1,0:T(8,128)(2,1)S(1)}, bf16[2,1,64,768]{3,2,1,0:T(8,128)(2,1)S(1)}, u32[]{:S(2)}, u32[]{:S(2)}) collective-permute-start(bf16[2,1,64,768]{3,2,1,0:T(8,128)(2,1)S(1)} %get-tuple-element.46), channel_id=1, source_target_pairs={{0,1},{1,0},{2,3},{3,2},{4,5},{5,4},{6,7},{7,6},{8,9},{9,8},{10,11... | collective-permute-start | bytes 589832 | tf_op jit(solution)/shard_map/ppermute | solution.py:280
  14.3 0.9 %collective-permute-done.4.refs_1_ = bf16[2,1,64,768]{3,2,1,0:T(8,128)(2,1)S(1)} collective-permute-done((bf16[2,1,64,768]{3,2,1,0:T(8,128)(2,1)S(1)}, bf16[2,1,64,768]{3,2,1,0:T(8,128)(2,1)S(1)}, u32[]{:S(2)}, u32[]{:S(2)}) %collective-permute-start.4) | collective-permute-done | bytes 196640 | tf_op jit(solution)/shard_map/ppermute | solution.py:280
  15.2 1.3 %collective-permute-done.5.refs_2_ = bf16[3,1,64,768]{3,2,1,0:T(8,128)(2,1)S(1)} collective-permute-done((bf16[3,1,64,768]{3,2,1,0:T(8,128)(2,1)S(1)}, bf16[3,1,64,768]{3,2,1,0:T(8,128)(2,1)S(1)}, u32[]{:S(2)}, u32[]{:S(2)}) %collective-permute-start.5) | collective-permute-done | bytes 294944 | tf_op jit(solution)/shard_map/ppermute | solution.py:390
  16.5 1.6 %collective-permute-start.7 = (bf16[1,1,64,768]{3,2,1,0:T(8,128)(2,1)S(1)}, bf16[1,1,64,768]{3,2,1,0:T(8,128)(2,1)S(1)}, u32[]{:S(2)}, u32[]{:S(2)}) collective-permute-start(bf16[1,1,64,768]{3,2,1,0:T(8,128)(2,1)S(1)} %row_sum.8), channel_id=1, source_target_pairs={{0,4},{1,3},{2,6},{3,1},{4,0},{5,7},{6,2},{7,5},{8,12},{9,11},{10,... | collective-permute-start | bytes 294920 | tf_op jit(solution)/shard_map/ppermute | solution.py:390
  18.2 1.6 %collective-permute-start.3 = (bf16[1,1,64,768]{3,2,1,0:T(8,128)(2,1)S(1)}, bf16[1,1,64,768]{3,2,1,0:T(8,128)(2,1)S(1)}, u32[]{:S(2)}, u32[]{:S(2)}) collective-permute-start(bf16[1,1,64,768]{3,2,1,0:T(8,128)(2,1)S(1)} %row_sum.5), channel_id=1, source_target_pairs={{0,2},{1,5},{2,0},{3,7},{4,6},{5,1},{6,4},{7,3},{8,10},{9,13},{10,... | collective-permute-start | bytes 294920 | tf_op jit(solution)/shard_map/ppermute | solution.py:390
  19.8 0.5 %collective-permute-start.6 = (bf16[1,1,64,768]{3,2,1,0:T(8,128)(2,1)S(1)}, bf16[1,1,64,768]{3,2,1,0:T(8,128)(2,1)S(1)}, u32[]{:S(2)}, u32[]{:S(2)}) collective-permute-start(bf16[1,1,64,768]{3,2,1,0:T(8,128)(2,1)S(1)} %row_sum.7), channel_id=1, source_target_pairs={{0,4},{1,3},{2,6},{3,1},{4,0},{5,7},{6,2},{7,5},{8,12},{9,11},{10,... | collective-permute-start | bytes 294920 | tf_op jit(solution)/shard_map/ppermute | solution.py:390
  20.4 0.0 collective-permute-done.2.refs_1_
  20.4 1.6 %collective-permute-done.7.refs_3_ = bf16[1,1,64,768]{3,2,1,0:T(8,128)(2,1)S(1)} collective-permute-done((bf16[1,1,64,768]{3,2,1,0:T(8,128)(2,1)S(1)}, bf16[1,1,64,768]{3,2,1,0:T(8,128)(2,1)S(1)}, u32[]{:S(2)}, u32[]{:S(2)}) %collective-permute-start.7) | collective-permute-done | bytes 98336 | tf_op jit(solution)/shard_map/ppermute | solution.py:390
  22.0 0.1 row_sum.9
  22.1 2.7 %collective-permute-start.8 = (bf16[1,1,64,768]{3,2,1,0:T(8,128)(2,1)S(1)}, bf16[1,1,64,768]{3,2,1,0:T(8,128)(2,1)S(1)}, u32[]{:S(2)}, u32[]{:S(2)}) collective-permute-start(bf16[1,1,64,768]{3,2,1,0:T(8,128)(2,1)S(1)} %row_sum.9), channel_id=1, source_target_pairs={{0,8},{1,9},{2,10},{3,11},{4,12},{5,13},{6,14},{7,15},{8,0},{9,1},... | collective-permute-start | bytes 294920 | tf_op jit(solution)/shard_map/ppermute | solution.py:390
  24.7 2.0 %collective-permute-done.1.got = bf16[512,768]{1,0:T(8,128)(2,1)S(1)} collective-permute-done((bf16[512,768]{1,0:T(8,128)(2,1)S(1)}, bf16[512,768]{1,0:T(8,128)(2,1)S(1)}, u32[]{:S(2)}, u32[]{:S(2)}) %collective-permute-start.1) | collective-permute-done | bytes 786464 | tf_op jit(solution)/shard_map/ppermute | solution.py:280
  26.7 0.1 half_sum.1.summed
  26.8 0.0 collective-permute-done.3.refs_2_
  26.9 0.0 collective-permute-done.6.refs_3_
  26.9 0.8 %collective-permute-done.8.refs_4_ = bf16[1,1,64,768]{3,2,1,0:T(8,128)(2,1)S(1)} collective-permute-done((bf16[1,1,64,768]{3,2,1,0:T(8,128)(2,1)S(1)}, bf16[1,1,64,768]{3,2,1,0:T(8,128)(2,1)S(1)}, u32[]{:S(2)}, u32[]{:S(2)}) %collective-permute-start.8) | collective-permute-done | bytes 98336 | tf_op jit(solution)/shard_map/ppermute | solution.py:390
  27.7 0.9 %finish.1 = (bf16[64,768]{1,0:T(8,128)(2,1)}, bf16[512,768]{1,0:T(8,128)(2,1)}) custom-call(bf16[512,768]{1,0:T(8,128)(2,1)S(1)} %get-tuple-element.43.kept, bf16[512,768]{1,0:T(8,128)(2,1)S(1)} %collective-permute-done.1.got, bf16[256,768]{1,0:T(8,128)(2,1)S(1)} %half_sum.1.summed, bf16[4,1,64,768]{3,2,1,0:T(8,128)(2,1)S(1)} %get-tuple-element.45.refs_0_, ...), custom_call_target="tpu_custom_call" | custom-call | tf_op jit(solution)/shard_map/finish/pallas_call | solution.py:449
  (3 shorter events, 0.1 us)
Async XLA Ops:
  3.8 4.7 %collective-permute-start = (bf16[4,1,64,768]{3,2,1,0:T(8,128)(2,1)S(1)}, bf16[4,1,64,768]{3,2,1,0:T(8,128)(2,1)S(1)}, u32[]{:S(2)}, u32[]{:S(2)}) collective-permute-start(bf16[4,1,64,768]{3,2,1,0:T(8,128)(2,1)S(1)} %get-tuple-element.26), channel_id=1, source_target_pairs={{0,1},{1,0},{2,3},{3,2},{4,5},{5,4},{6,7},{7,6},{8,9},{9,8},{10,11... | collective-permute-start | bytes 1179656 | tf_op jit(solution)/shard_map/ppermute | solution.py:280
  6.0 20.8 %collective-permute-start.1 = (bf16[512,768]{1,0:T(8,128)(2,1)S(1)}, bf16[512,768]{1,0:T(8,128)(2,1)S(1)}, u32[]{:S(2)}, u32[]{:S(2)}) collective-permute-start(bf16[512,768]{1,0:T(8,128)(2,1)S(1)} %get-tuple-element.44), channel_id=1, source_target_pairs={{0,16},{16,0},{1,17},{17,1},{2,18},{18,2},{3,19},{19,3},{4,20},{20... | collective-permute-start | bytes 2359304 | tf_op jit(solution)/shard_map/ppermute | solution.py:280
  9.7 6.8 %collective-permute-start.5 = (bf16[3,1,64,768]{3,2,1,0:T(8,128)(2,1)S(1)}, bf16[3,1,64,768]{3,2,1,0:T(8,128)(2,1)S(1)}, u32[]{:S(2)}, u32[]{:S(2)}) collective-permute-start(bf16[3,1,64,768]{3,2,1,0:T(8,128)(2,1)S(1)} %row_sum.6), channel_id=1, source_target_pairs={{0,2},{1,5},{2,0},{3,7},{4,6},{5,1},{6,4},{7,3},{8,10},{9,13},{10,... | collective-permute-start | bytes 884744 | tf_op jit(solution)/shard_map/ppermute | solution.py:390
  13.7 1.5 %collective-permute-start.4 = (bf16[2,1,64,768]{3,2,1,0:T(8,128)(2,1)S(1)}, bf16[2,1,64,768]{3,2,1,0:T(8,128)(2,1)S(1)}, u32[]{:S(2)}, u32[]{:S(2)}) collective-permute-start(bf16[2,1,64,768]{3,2,1,0:T(8,128)(2,1)S(1)} %get-tuple-element.49), channel_id=1, source_target_pairs={{0,1},{1,0},{2,3},{3,2},{4,5},{5,4},{6,7},{7,6},{8,9},{9,8},{10,11... | collective-permute-start | bytes 589832 | tf_op jit(solution)/shard_map/ppermute | solution.py:280
  13.8 6.6 %collective-permute-start.2 = (bf16[2,1,64,768]{3,2,1,0:T(8,128)(2,1)S(1)}, bf16[2,1,64,768]{3,2,1,0:T(8,128)(2,1)S(1)}, u32[]{:S(2)}, u32[]{:S(2)}) collective-permute-start(bf16[2,1,64,768]{3,2,1,0:T(8,128)(2,1)S(1)} %get-tuple-element.46), channel_id=1, source_target_pairs={{0,1},{1,0},{2,3},{3,2},{4,5},{5,4},{6,7},{7,6},{8,9},{9,8},{10,11... | collective-permute-start | bytes 589832 | tf_op jit(solution)/shard_map/ppermute | solution.py:280
  16.5 5.5 %collective-permute-start.7 = (bf16[1,1,64,768]{3,2,1,0:T(8,128)(2,1)S(1)}, bf16[1,1,64,768]{3,2,1,0:T(8,128)(2,1)S(1)}, u32[]{:S(2)}, u32[]{:S(2)}) collective-permute-start(bf16[1,1,64,768]{3,2,1,0:T(8,128)(2,1)S(1)} %row_sum.8), channel_id=1, source_target_pairs={{0,4},{1,3},{2,6},{3,1},{4,0},{5,7},{6,2},{7,5},{8,12},{9,11},{10,... | collective-permute-start | bytes 294920 | tf_op jit(solution)/shard_map/ppermute | solution.py:390
  18.2 8.6 %collective-permute-start.3 = (bf16[1,1,64,768]{3,2,1,0:T(8,128)(2,1)S(1)}, bf16[1,1,64,768]{3,2,1,0:T(8,128)(2,1)S(1)}, u32[]{:S(2)}, u32[]{:S(2)}) collective-permute-start(bf16[1,1,64,768]{3,2,1,0:T(8,128)(2,1)S(1)} %row_sum.5), channel_id=1, source_target_pairs={{0,2},{1,5},{2,0},{3,7},{4,6},{5,1},{6,4},{7,3},{8,10},{9,13},{10,... | collective-permute-start | bytes 294920 | tf_op jit(solution)/shard_map/ppermute | solution.py:390
  19.8 7.0 %collective-permute-start.6 = (bf16[1,1,64,768]{3,2,1,0:T(8,128)(2,1)S(1)}, bf16[1,1,64,768]{3,2,1,0:T(8,128)(2,1)S(1)}, u32[]{:S(2)}, u32[]{:S(2)}) collective-permute-start(bf16[1,1,64,768]{3,2,1,0:T(8,128)(2,1)S(1)} %row_sum.7), channel_id=1, source_target_pairs={{0,4},{1,3},{2,6},{3,1},{4,0},{5,7},{6,2},{7,5},{8,12},{9,11},{10,... | collective-permute-start | bytes 294920 | tf_op jit(solution)/shard_map/ppermute | solution.py:390
  22.1 5.6 %collective-permute-start.8 = (bf16[1,1,64,768]{3,2,1,0:T(8,128)(2,1)S(1)}, bf16[1,1,64,768]{3,2,1,0:T(8,128)(2,1)S(1)}, u32[]{:S(2)}, u32[]{:S(2)}) collective-permute-start(bf16[1,1,64,768]{3,2,1,0:T(8,128)(2,1)S(1)} %row_sum.9), channel_id=1, source_target_pairs={{0,8},{1,9},{2,10},{3,11},{4,12},{5,13},{6,14},{7,15},{8,0},{9,1},... | collective-permute-start | bytes 294920 | tf_op jit(solution)/shard_map/ppermute | solution.py:390

commit v4 on v3

--- a/solution.py
+++ b/solution.py
@@ -129,8 +129,6 @@
         copy.start()
     for copy in small:
         copy.wait()
-    for copy in (*e_copies[1], *e_copies[2], *e_copies[3]):
-        copy.start()
 
     lane = lax.broadcasted_iota(jnp.int32, (BLOCKS, INST_BLOCK), 1)
     low = lane < INST_BLOCK // 2
@@ -149,11 +147,13 @@
             )
         return x
 
-    for t in range(tiles):
+    def set_positives(t):
         for g in range(TILE // INST_BLOCK):
-            blocks = [block_in(t, 2 * g + h, over, core) for h in range(2)]
             one, two = (
-                relative_lanes(pos_raw[:, pl.ds(pl.multiple_of(b * INST_BLOCK, INST_BLOCK), INST_BLOCK)]) for b in blocks
+                relative_lanes(
+                    pos_raw[:, pl.ds(pl.multiple_of(block_in(t, 2 * g + h, over, core) * INST_BLOCK, INST_BLOCK), INST_BLOCK)]
+                )
+                for h in range(2)
             )
             group = t * (TILE // INST_BLOCK) + g
             pos[:, group * INST_BLOCK : (group + 1) * INST_BLOCK] = (
@@ -161,8 +161,12 @@
                 if t % 2
                 else jnp.where(low, pltpu.roll(one, INST_BLOCK // 2, 1), two)
             )
-            for h in range(2):
-                beam[8 * h + group : 8 * h + group + 1] = beam_raw[pl.ds(blocks[h], 1)]
+
+    for t in range(tiles):
+        for i in range(4):
+            group = 8 * (i % 2) + t * 2 + i // 2
+            beam[group : group + 1] = beam_raw[pl.ds(block_in(t, i, over, core), 1)]
+    set_positives(0)
     set_words([0], pos, word)
 
     row = lax.broadcasted_iota(jnp.int32, (2 * clusters, 2 * clusters * INST_BLOCK), 0)
@@ -183,6 +187,8 @@
     def before(k, t, h):
         if (k, h) == (1, 0):
             w_copies[1].wait()
+            for copy in (*e_copies[1], *e_copies[2], *e_copies[3]):
+                copy.start()
 
     def emit(k, t, c, part):
         out = own_slopes_t if k else first_slopes_t
@@ -191,6 +197,8 @@
 
     jobs = [(k, 0, h) for k in range(2) for h in range(half_rows // CHUNK)]
     slope_chunks(jobs, scores, w, embed, bias_full, mask, word, before, emit)
+    for t in range(1, tiles):
+        set_positives(t)
     store_rows([row_out], slopes, w)
     for copy in (*e_copies[1], *e_copies[2], *e_copies[3]):
         copy.wait()
@@ -239,13 +247,17 @@
     row_tile(1, [row_out], embed, w, word, mask, bias_full, first_slopes_t, own_slopes_t, scores, slopes)
 
 
-def last_rows_kernel(embed, w, word, mask, bias_full, first_slopes_t, one_slopes_t, two_slopes_t, *rest):
-    *sends, row_out, label_out, three_slopes_t, four_slopes_t, scores, slopes = rest
+def last_rows_kernel(embed, w, word, mask, bias_full, first_slopes_t, *rest):
+    *outs, three_slopes_t, four_slopes_t, scores, slopes = rest
     shared = (embed, w, word, mask, bias_full, first_slopes_t)
-    row_tile(2, sends, *shared, three_slopes_t, scores.at[0], slopes.at[0])
-    row_tile(3, [row_out], *shared, four_slopes_t, scores.at[1], slopes.at[1])
+    row_tile(2, outs[:-1], *shared, three_slopes_t, scores.at[0], slopes.at[0])
+    row_tile(3, outs[-1:], *shared, four_slopes_t, scores.at[1], slopes.at[1])
+
+
+def keep_kernel(embed, *refs):
+    *slopes_t, label_out = refs
     total = 0.0
-    for t, part in enumerate((one_slopes_t, two_slopes_t, three_slopes_t, four_slopes_t)):
+    for t, part in enumerate(slopes_t):
         total = total + jnp.dot(part[...], embed[t * TILE : (t + 1) * TILE], preferred_element_type=F32)
     label_out[...] = total.astype(BF16)
 
@@ -389,30 +401,28 @@
         bits = (axes[stage], axes[stage if stage == 2 else 1 - stage])
         return lax.ppermute(value, "label", [(i, i ^ bits[i % 2]) for i in range(n_label)])
 
-    far_got = passed_on(summed_at((first_keep, slice(1, 4)), (first_got, slice(1, 4))), 0)
-    near_got = passed_on(summed_at((first_keep, slice(0, 1)), (first_got, slice(0, 1))), 0)
+    far_got = passed_on(summed_at((first_keep, slice(2, 4)), (first_got, slice(2, 4))), 0)
+    near_got = passed_on(summed_at((first_keep, slice(0, 2)), (first_got, slice(0, 2))), 0)
 
     part_shape = shape((2, subs, piece, features), BF16)
-    *last_send, last_keep, label_keep = pl.pallas_call(
+    *last_send, last_keep, three_slopes_t, four_slopes_t = pl.pallas_call(
         last_rows_kernel,
-        out_shape=[part_shape] * 2 + [row_shape, shape((half_rows, features), BF16)],
-        in_specs=[vmem] * 8,
-        out_specs=[vmem] * 4,
+        out_shape=[part_shape] * 2 + [row_shape, tile_shape, tile_shape],
+        in_specs=[vmem] * 6,
+        out_specs=[vmem] * 5,
         scratch_shapes=[
-            pltpu.VMEM((half_rows, TILE), BF16),
-            pltpu.VMEM((half_rows, TILE), BF16),
             pltpu.VMEM((2, 2, CHUNK, TILE), F32),
             pltpu.VMEM((2, TILE, labels), BF16),
         ],
         compiler_params=params,
-        cost_estimate=cost(0),
+        cost_estimate=cost(2),
         name="last_rows",
-    )(*shared, one_slopes_t, two_slopes_t)
+    )(*shared)
 
     last_got = [swapped(part, "label", n_label, 1) for part in last_send]
-    three_got = passed_on(summed_at((last_keep, slice(3, 4)), (last_got[1], slice(1, 2)), (far_got, slice(2, 3))), 1)
-    two_got = passed_on(summed_at((last_keep, slice(2, 3)), (last_got[1], slice(0, 1)), (far_got, slice(1, 2))), 1)
-    row_got = passed_on(summed_at((last_keep, slice(1, 2)), (last_got[0], slice(1, 2)), (far_got, slice(0, 1)), (three_got, slice(0, 1))), 2)
+    three_got = passed_on(summed_at((last_keep, slice(3, 4)), (last_got[1], slice(1, 2)), (far_got, slice(1, 2))), 1)
+    two_got = passed_on(summed_at((last_keep, slice(2, 3)), (last_got[1], slice(0, 1)), (far_got, slice(0, 1))), 1)
+    row_got = passed_on(summed_at((last_keep, slice(1, 2)), (last_got[0], slice(1, 2)), (near_got, slice(1, 2)), (three_got, slice(0, 1))), 2)
     row_terms = [last_keep, last_got[0], near_got, two_got, row_got]
     bit = subs
     while bit > 1:
@@ -423,6 +433,16 @@
         row_terms = [add(row_sum[:held], came[:held]), incoming]
         subs = held
         bit //= 2
+
+    label_keep = pl.pallas_call(
+        keep_kernel,
+        out_shape=shape((half_rows, features), BF16),
+        in_specs=[vmem] * 5,
+        out_specs=vmem,
+        compiler_params=params,
+        cost_estimate=cost(0),
+        name="keep_half",
+    )(embed_own, one_slopes_t, two_slopes_t, three_slopes_t, four_slopes_t)
 
     kept, got = label_keep, label_got
     step = n_dp // 4

time: 28.8 us -> 29.3 us (1.017)
  Pallas kernels: 9.53 us -> 10.1 us
    pallas_call x0 -> x1, Pallas kernels: none -> 0.98 us  [on_device(): pl.pallas_call(keep_kernel, out_shape=shape((half_rows, features), BF16),...]
    ppermute x4, waiting for transfers between devices: 2.96 us -> 3.88 us  [swapped(): return lax.ppermute(value, axis, [(i, i ^ bit) for i in range(size)])]
    ppermute x5, waiting for transfers between devices: 3.73 us -> 2.94 us  [passed_on(): lax.ppermute(value, 'label', [(i, i ^ bits[i % 2]) for i in range(n_label)])]
    pallas_call x1, Pallas kernels: 2.38 us -> 1.71 us  [on_device(): pl.pallas_call(last_rows_kernel, out_shape=[part_shape] * 2 + [row_shape,...]
  transfers between devices with their start and end apart: 9 -> 9, of which waited for: 5 -> 5; matrix products, arithmetic and copies ran while one was open for 0% -> 0% of each run, Pallas kernels for 19% -> 20%
where the time goes in v4:
time: 29.3 us; the launch traced here: 29.1 us
  starting transfers between devices  11.4 us (39%)
  Pallas kernels  10.1 us (34%)
  waiting for transfers between devices  6.82 us (23%)
  between operations  0.73 us (2%)
    ppermute x5, starting transfers between devices, passed_on(): lax.ppermute(value, 'label', [(i, i ^ bits[i % 2]) for i in range(n_label)])  7.94 us
    ppermute x4, waiting for transfers between devices, swapped(): return lax.ppermute(value, axis, [(i, i ^ bit) for i in range(size)])  3.88 us
    ppermute x4, starting transfers between devices, swapped(): return lax.ppermute(value, axis, [(i, i ^ bit) for i in range(size)])  3.46 us
    pallas_call x1, Pallas kernels, on_device(): pl.pallas_call(functools.partial(first_kernel, n_label), out_shape=[shape...  3.45 us
    ppermute x5, waiting for transfers between devices, passed_on(): lax.ppermute(value, 'label', [(i, i ^ bits[i % 2]) for i in range(n_label)])  2.94 us
    pallas_call x1, Pallas kernels, on_device(): pl.pallas_call(last_rows_kernel, out_shape=[part_shape] * 2 + [row_shape,...  1.71 us
    pallas_call x1, Pallas kernels, on_device(): pl.pallas_call(label_kernel, out_shape=[shape((CLUSTER, rows), jnp.int16)...  1.64 us
    pallas_call x1, Pallas kernels, on_device(): pl.pallas_call(keep_rows_kernel, out_shape=[tile_shape, row_shape], in_sp...  1.08 us
  transfers between devices with their start and end apart: 9, of which 5 were waited for; matrix products, arithmetic and copies ran while one was open for 0% of the time, Pallas kernels for 20%

profile of v4, /device:TPU:0, one launch (start us, length us, event | category | flops | bytes accessed | tf_op | source)
XLA Modules:
  0.0 29.1 jit_solution(6654602053165740863)
XLA Ops:
  0.6 3.5 %first_rows.1 = (bf16[1024,768]{1,0:T(8,128)(2,1)S(1)}, bf16[1024,768]{1,0:T(8,128)(2,1)S(1)}, s32[8,1024]{1,0:T(8,128)S(1)}, bf16[2,4,8,128]{3,2,1,0:T(8,128)(2...) custom-call(bf16[1024,768]{1,0:T(8,128)(2,1)} %embed_hbm.1, ...), custom_call_target="tpu_custom_call" | custom-call | flops 1610612736 | tf_op jit(solution)/shard_map/first_rows/pallas_call | solution.py:323
  4.1 0.5 %collective-permute-start = (bf16[4,1,64,768]{3,2,1,0:T(8,128)(2,1)S(1)}, bf16[4,1,64,768]{3,2,1,0:T(8,128)(2,1)S(1)}, u32[]{:S(2)}, u32[]{:S(2)}) collective-permute-start(bf16[4,1,64,768]{3,2,1,0:T(8,128)(2,1)S(1)} %get-tuple-element.29), channel_id=1, source_target_pairs={{0,1},{1,0},{2,3},{3,2},{4,5},{5,4},{6,7},{7,6},{8,9},{9,8},{10,11... | collective-permute-start | bytes 1179656 | tf_op jit(solution)/shard_map/ppermute | solution.py:292
  4.6 1.6 %send_half.1 = (s16[128,1024]{1,0:T(8,128)(2,1)S(1)}, bf16[512,768]{1,0:T(8,128)(2,1)S(1)}, bf16[512,768]{1,0:T(8,128)(2,1)S(1)}) custom-call(bf16[1024,768]{1,0:T(8,128)(2,1)S(1)} %get-tuple-element.37.embed, bf16[1024,768]{1,0:T(8,128)(2,1)S(1)} %get-tuple-element.38.w, s32[8,1024]{1,0:T(8,128)S(1)} %get-tuple-element.31.pos, ...), custom_call_target="tpu_custom_call" | custom-call | tf_op jit(solution)/shard_map/send_half/pallas_call | solution.py:354
  6.3 2.6 %collective-permute-start.1 = (bf16[512,768]{1,0:T(8,128)(2,1)S(1)}, bf16[512,768]{1,0:T(8,128)(2,1)S(1)}, u32[]{:S(2)}, u32[]{:S(2)}) collective-permute-start(bf16[512,768]{1,0:T(8,128)(2,1)S(1)} %get-tuple-element.46), channel_id=1, source_target_pairs={{0,16},{16,0},{1,17},{17,1},{2,18},{18,2},{3,19},{19,3},{4,20},{20... | collective-permute-start | bytes 2359304 | tf_op jit(solution)/shard_map/ppermute | solution.py:292
  8.8 0.0 collective-permute-done.refs_1_
  8.8 1.1 %keep_rows.1 = (bf16[512,256]{1,0:T(8,128)(2,1)S(1)}, bf16[4,1,64,768]{3,2,1,0:T(8,128)(2,1)S(1)}) custom-call(bf16[1024,768]{1,0:T(8,128)(2,1)S(1)} %get-tuple-element.37.embed, bf16[1024,768]{1,0:T(8,128)(2,1)S(1)} %get-tuple-element.38.w, s16[128,1024]{1,0:T(8,128)(2,1)S(1)} %get-tuple-element.39.word, bf16[2,4,8,128]{3,2,1,0:T(8,128)(2,1)S(1)} %get-tuple-element.40.mask, ...), custom_call_target="tpu_custom_call" | custom-call | tf_op jit(solution)/shard_map/keep_rows/pallas_call | solution.py:374
  10.0 1.6 %collective-permute-start.5 = (bf16[2,1,64,768]{3,2,1,0:T(8,128)(2,1)S(1)}, bf16[2,1,64,768]{3,2,1,0:T(8,128)(2,1)S(1)}, u32[]{:S(2)}, u32[]{:S(2)}) collective-permute-start(bf16[2,1,64,768]{3,2,1,0:T(8,128)(2,1)S(1)} %row_sum.6), channel_id=1, source_target_pairs={{0,2},{1,5},{2,0},{3,7},{4,6},{5,1},{6,4},{7,3},{8,10},{9,13},{10,... | collective-permute-start | bytes 589832 | tf_op jit(solution)/shard_map/ppermute | solution.py:402
  11.6 1.7 %last_rows.1 = (bf16[2,1,64,768]{3,2,1,0:T(8,128)(2,1)S(1)}, bf16[2,1,64,768]{3,2,1,0:T(8,128)(2,1)S(1)}, bf16[4,1,64,768]{3,2,1,0:T(8,128)(2,1)S(1)}, bf16[512,256]{1,0:T(8,128)(2,1)S(1)}, bf16[512,256]{1,0:T(8,128)(2,1)S(1)}) custom-call(bf16[1024,768]{1,0:T(8,128)(2,1)S(1)} %get-tuple-element.37.embed, bf16[1024,768]{1,0:T(8,128)(2,1)S(1)} %get-tuple-element.38.w, ...), custom_call_target="tpu_custom_call" | custom-call | flops 1610612736 | tf_op jit(solution)/shard_map/last_rows/pallas_call | solution.py:408
  13.3 0.1 collective-permute-start.4
  13.4 1.5 %collective-permute-start.3 = (bf16[2,1,64,768]{3,2,1,0:T(8,128)(2,1)S(1)}, bf16[2,1,64,768]{3,2,1,0:T(8,128)(2,1)S(1)}, u32[]{:S(2)}, u32[]{:S(2)}) collective-permute-start(bf16[2,1,64,768]{3,2,1,0:T(8,128)(2,1)S(1)} %row_sum.5), channel_id=1, source_target_pairs={{0,2},{1,5},{2,0},{3,7},{4,6},{5,1},{6,4},{7,3},{8,10},{9,13},{10,... | collective-permute-start | bytes 589832 | tf_op jit(solution)/shard_map/ppermute | solution.py:402
  15.0 0.3 %collective-permute-start.2 = (bf16[2,1,64,768]{3,2,1,0:T(8,128)(2,1)S(1)}, bf16[2,1,64,768]{3,2,1,0:T(8,128)(2,1)S(1)}, u32[]{:S(2)}, u32[]{:S(2)}) collective-permute-start(bf16[2,1,64,768]{3,2,1,0:T(8,128)(2,1)S(1)} %get-tuple-element.48), channel_id=1, source_target_pairs={{0,1},{1,0},{2,3},{3,2},{4,5},{5,4},{6,7},{7,6},{8,9},{9,8},{10,11... | collective-permute-start | bytes 589832 | tf_op jit(solution)/shard_map/ppermute | solution.py:292
  15.3 0.4 %collective-permute-done.5.refs_2_ = bf16[2,1,64,768]{3,2,1,0:T(8,128)(2,1)S(1)} collective-permute-done((bf16[2,1,64,768]{3,2,1,0:T(8,128)(2,1)S(1)}, bf16[2,1,64,768]{3,2,1,0:T(8,128)(2,1)S(1)}, u32[]{:S(2)}, u32[]{:S(2)}) %collective-permute-start.5) | collective-permute-done | bytes 196640 | tf_op jit(solution)/shard_map/ppermute | solution.py:402
  15.7 0.0 collective-permute-done.4.refs_1_
  15.8 1.6 %collective-permute-start.7 = (bf16[1,1,64,768]{3,2,1,0:T(8,128)(2,1)S(1)}, bf16[1,1,64,768]{3,2,1,0:T(8,128)(2,1)S(1)}, u32[]{:S(2)}, u32[]{:S(2)}) collective-permute-start(bf16[1,1,64,768]{3,2,1,0:T(8,128)(2,1)S(1)} %row_sum.8), channel_id=1, source_target_pairs={{0,4},{1,3},{2,6},{3,1},{4,0},{5,7},{6,2},{7,5},{8,12},{9,11},{10,... | collective-permute-start | bytes 294920 | tf_op jit(solution)/shard_map/ppermute | solution.py:402
  17.4 1.0 %keep_half.1.kept = bf16[512,768]{1,0:T(8,128)(2,1)S(1)} custom-call(bf16[1024,768]{1,0:T(8,128)(2,1)S(1)} %get-tuple-element.37.embed, bf16[512,256]{1,0:T(8,128)(2,1)S(1)} %get-tuple-element.28.refs_0_, bf16[512,256]{1,0:T(8,128)(2,1)S(1)} %get-tuple-element.43.refs_1_, bf16[512,256]{1,0:T(8,128)(2,1)S(1)} %get-tuple-element.44.refs_2_, ...), custom_call_target="tpu_custom_call" | custom-call | tf_op jit(solution)/shard_map/keep_half/pallas_call | solution.py:437
  18.4 0.5 %collective-permute-start.6 = (bf16[1,1,64,768]{3,2,1,0:T(8,128)(2,1)S(1)}, bf16[1,1,64,768]{3,2,1,0:T(8,128)(2,1)S(1)}, u32[]{:S(2)}, u32[]{:S(2)}) collective-permute-start(bf16[1,1,64,768]{3,2,1,0:T(8,128)(2,1)S(1)} %row_sum.7), channel_id=1, source_target_pairs={{0,4},{1,3},{2,6},{3,1},{4,0},{5,7},{6,2},{7,5},{8,12},{9,11},{10,... | collective-permute-start | bytes 294920 | tf_op jit(solution)/shard_map/ppermute | solution.py:402
  19.0 1.1 %collective-permute-done.3.refs_2_ = bf16[2,1,64,768]{3,2,1,0:T(8,128)(2,1)S(1)} collective-permute-done((bf16[2,1,64,768]{3,2,1,0:T(8,128)(2,1)S(1)}, bf16[2,1,64,768]{3,2,1,0:T(8,128)(2,1)S(1)}, u32[]{:S(2)}, u32[]{:S(2)}) %collective-permute-start.3) | collective-permute-done | bytes 196640 | tf_op jit(solution)/shard_map/ppermute | solution.py:402
  20.1 0.0 collective-permute-done.2.refs_1_
  20.1 0.3 %collective-permute-done.7.refs_3_ = bf16[1,1,64,768]{3,2,1,0:T(8,128)(2,1)S(1)} collective-permute-done((bf16[1,1,64,768]{3,2,1,0:T(8,128)(2,1)S(1)}, bf16[1,1,64,768]{3,2,1,0:T(8,128)(2,1)S(1)}, u32[]{:S(2)}, u32[]{:S(2)}) %collective-permute-start.7) | collective-permute-done | bytes 98336 | tf_op jit(solution)/shard_map/ppermute | solution.py:402
  20.4 0.1 row_sum.9
  20.5 2.7 %collective-permute-start.8 = (bf16[1,1,64,768]{3,2,1,0:T(8,128)(2,1)S(1)}, bf16[1,1,64,768]{3,2,1,0:T(8,128)(2,1)S(1)}, u32[]{:S(2)}, u32[]{:S(2)}) collective-permute-start(bf16[1,1,64,768]{3,2,1,0:T(8,128)(2,1)S(1)} %row_sum.9), channel_id=1, source_target_pairs={{0,8},{1,9},{2,10},{3,11},{4,12},{5,13},{6,14},{7,15},{8,0},{9,1},... | collective-permute-start | bytes 294920 | tf_op jit(solution)/shard_map/ppermute | solution.py:402
  23.2 3.9 %collective-permute-done.1.got = bf16[512,768]{1,0:T(8,128)(2,1)S(1)} collective-permute-done((bf16[512,768]{1,0:T(8,128)(2,1)S(1)}, bf16[512,768]{1,0:T(8,128)(2,1)S(1)}, u32[]{:S(2)}, u32[]{:S(2)}) %collective-permute-start.1) | collective-permute-done | bytes 786464 | tf_op jit(solution)/shard_map/ppermute | solution.py:292
  27.0 0.1 half_sum.1.summed
  27.1 0.0 collective-permute-done.6.refs_3_
  27.1 1.0 %collective-permute-done.8.refs_4_ = bf16[1,1,64,768]{3,2,1,0:T(8,128)(2,1)S(1)} collective-permute-done((bf16[1,1,64,768]{3,2,1,0:T(8,128)(2,1)S(1)}, bf16[1,1,64,768]{3,2,1,0:T(8,128)(2,1)S(1)}, u32[]{:S(2)}, u32[]{:S(2)}) %collective-permute-start.8) | collective-permute-done | bytes 98336 | tf_op jit(solution)/shard_map/ppermute | solution.py:402
  28.1 0.9 %finish.1 = (bf16[64,768]{1,0:T(8,128)(2,1)}, bf16[512,768]{1,0:T(8,128)(2,1)}) custom-call(bf16[512,768]{1,0:T(8,128)(2,1)S(1)} %keep_half.1.kept, bf16[512,768]{1,0:T(8,128)(2,1)S(1)} %collective-permute-done.1.got, bf16[256,768]{1,0:T(8,128)(2,1)S(1)} %half_sum.1.summed, bf16[4,1,64,768]{3,2,1,0:T(8,128)(2,1)S(1)} %get-tuple-element.47.refs_0_, ...), custom_call_target="tpu_custom_call" | custom-call | tf_op jit(solution)/shard_map/finish/pallas_call | solution.py:469
  (4 shorter events, 0.2 us)
Async XLA Ops:
  4.1 4.7 %collective-permute-start = (bf16[4,1,64,768]{3,2,1,0:T(8,128)(2,1)S(1)}, bf16[4,1,64,768]{3,2,1,0:T(8,128)(2,1)S(1)}, u32[]{:S(2)}, u32[]{:S(2)}) collective-permute-start(bf16[4,1,64,768]{3,2,1,0:T(8,128)(2,1)S(1)} %get-tuple-element.29), channel_id=1, source_target_pairs={{0,1},{1,0},{2,3},{3,2},{4,5},{5,4},{6,7},{7,6},{8,9},{9,8},{10,11... | collective-permute-start | bytes 1179656 | tf_op jit(solution)/shard_map/ppermute | solution.py:292
  6.3 20.8 %collective-permute-start.1 = (bf16[512,768]{1,0:T(8,128)(2,1)S(1)}, bf16[512,768]{1,0:T(8,128)(2,1)S(1)}, u32[]{:S(2)}, u32[]{:S(2)}) collective-permute-start(bf16[512,768]{1,0:T(8,128)(2,1)S(1)} %get-tuple-element.46), channel_id=1, source_target_pairs={{0,16},{16,0},{1,17},{17,1},{2,18},{18,2},{3,19},{19,3},{4,20},{20... | collective-permute-start | bytes 2359304 | tf_op jit(solution)/shard_map/ppermute | solution.py:292
  10.0 5.7 %collective-permute-start.5 = (bf16[2,1,64,768]{3,2,1,0:T(8,128)(2,1)S(1)}, bf16[2,1,64,768]{3,2,1,0:T(8,128)(2,1)S(1)}, u32[]{:S(2)}, u32[]{:S(2)}) collective-permute-start(bf16[2,1,64,768]{3,2,1,0:T(8,128)(2,1)S(1)} %row_sum.6), channel_id=1, source_target_pairs={{0,2},{1,5},{2,0},{3,7},{4,6},{5,1},{6,4},{7,3},{8,10},{9,13},{10,... | collective-permute-start | bytes 589832 | tf_op jit(solution)/shard_map/ppermute | solution.py:402
  13.3 2.4 %collective-permute-start.4 = (bf16[2,1,64,768]{3,2,1,0:T(8,128)(2,1)S(1)}, bf16[2,1,64,768]{3,2,1,0:T(8,128)(2,1)S(1)}, u32[]{:S(2)}, u32[]{:S(2)}) collective-permute-start(bf16[2,1,64,768]{3,2,1,0:T(8,128)(2,1)S(1)} %get-tuple-element.51), channel_id=1, source_target_pairs={{0,1},{1,0},{2,3},{3,2},{4,5},{5,4},{6,7},{7,6},{8,9},{9,8},{10,11... | collective-permute-start | bytes 589832 | tf_op jit(solution)/shard_map/ppermute | solution.py:292
  13.4 6.7 %collective-permute-start.3 = (bf16[2,1,64,768]{3,2,1,0:T(8,128)(2,1)S(1)}, bf16[2,1,64,768]{3,2,1,0:T(8,128)(2,1)S(1)}, u32[]{:S(2)}, u32[]{:S(2)}) collective-permute-start(bf16[2,1,64,768]{3,2,1,0:T(8,128)(2,1)S(1)} %row_sum.5), channel_id=1, source_target_pairs={{0,2},{1,5},{2,0},{3,7},{4,6},{5,1},{6,4},{7,3},{8,10},{9,13},{10,... | collective-permute-start | bytes 589832 | tf_op jit(solution)/shard_map/ppermute | solution.py:402
  15.0 5.1 %collective-permute-start.2 = (bf16[2,1,64,768]{3,2,1,0:T(8,128)(2,1)S(1)}, bf16[2,1,64,768]{3,2,1,0:T(8,128)(2,1)S(1)}, u32[]{:S(2)}, u32[]{:S(2)}) collective-permute-start(bf16[2,1,64,768]{3,2,1,0:T(8,128)(2,1)S(1)} %get-tuple-element.48), channel_id=1, source_target_pairs={{0,1},{1,0},{2,3},{3,2},{4,5},{5,4},{6,7},{7,6},{8,9},{9,8},{10,11... | collective-permute-start | bytes 589832 | tf_op jit(solution)/shard_map/ppermute | solution.py:292
  15.8 4.7 %collective-permute-start.7 = (bf16[1,1,64,768]{3,2,1,0:T(8,128)(2,1)S(1)}, bf16[1,1,64,768]{3,2,1,0:T(8,128)(2,1)S(1)}, u32[]{:S(2)}, u32[]{:S(2)}) collective-permute-start(bf16[1,1,64,768]{3,2,1,0:T(8,128)(2,1)S(1)} %row_sum.8), channel_id=1, source_target_pairs={{0,4},{1,3},{2,6},{3,1},{4,0},{5,7},{6,2},{7,5},{8,12},{9,11},{10,... | collective-permute-start | bytes 294920 | tf_op jit(solution)/shard_map/ppermute | solution.py:402
  18.4 8.7 %collective-permute-start.6 = (bf16[1,1,64,768]{3,2,1,0:T(8,128)(2,1)S(1)}, bf16[1,1,64,768]{3,2,1,0:T(8,128)(2,1)S(1)}, u32[]{:S(2)}, u32[]{:S(2)}) collective-permute-start(bf16[1,1,64,768]{3,2,1,0:T(8,128)(2,1)S(1)} %row_sum.7), channel_id=1, source_target_pairs={{0,4},{1,3},{2,6},{3,1},{4,0},{5,7},{6,2},{7,5},{8,12},{9,11},{10,... | collective-permute-start | bytes 294920 | tf_op jit(solution)/shard_map/ppermute | solution.py:402
  20.5 7.7 %collective-permute-start.8 = (bf16[1,1,64,768]{3,2,1,0:T(8,128)(2,1)S(1)}, bf16[1,1,64,768]{3,2,1,0:T(8,128)(2,1)S(1)}, u32[]{:S(2)}, u32[]{:S(2)}) collective-permute-start(bf16[1,1,64,768]{3,2,1,0:T(8,128)(2,1)S(1)} %row_sum.9), channel_id=1, source_target_pairs={{0,8},{1,9},{2,10},{3,11},{4,12},{5,13},{6,14},{7,15},{8,0},{9,1},... | collective-permute-start | bytes 294920 | tf_op jit(solution)/shard_map/ppermute | solution.py:402

commit v5 on v4

--- a/solution.py
+++ b/solution.py
@@ -65,7 +65,7 @@
 def block_in(t, i, over, core):
     first, second, third = 1 - t // 2, i // 2, i % 2
     owner = core if t % 2 else 1 - core
-    return (first + 2 * second + 4 * third + owner * (first - second)) ^ over
+    return (first + 2 * second + 4 * third + owner * (first + 2 * second - 3 * third)) ^ over
 
 
 def set_words(tiles, pos_ref, word):
@@ -129,6 +129,8 @@
         copy.start()
     for copy in small:
         copy.wait()
+    for copy in (*e_copies[1], *e_copies[2], *e_copies[3]):
+        copy.start()
 
     lane = lax.broadcasted_iota(jnp.int32, (BLOCKS, INST_BLOCK), 1)
     low = lane < INST_BLOCK // 2
@@ -166,7 +168,8 @@
         for i in range(4):
             group = 8 * (i % 2) + t * 2 + i // 2
             beam[group : group + 1] = beam_raw[pl.ds(block_in(t, i, over, core), 1)]
-    set_positives(0)
+    for t in range(tiles):
+        set_positives(t)
     set_words([0], pos, word)
 
     row = lax.broadcasted_iota(jnp.int32, (2 * clusters, 2 * clusters * INST_BLOCK), 0)
@@ -187,8 +190,6 @@
     def before(k, t, h):
         if (k, h) == (1, 0):
             w_copies[1].wait()
-            for copy in (*e_copies[1], *e_copies[2], *e_copies[3]):
-                copy.start()
 
     def emit(k, t, c, part):
         out = own_slopes_t if k else first_slopes_t
@@ -197,8 +198,6 @@
 
     jobs = [(k, 0, h) for k in range(2) for h in range(half_rows // CHUNK)]
     slope_chunks(jobs, scores, w, embed, bias_full, mask, word, before, emit)
-    for t in range(1, tiles):
-        set_positives(t)
     store_rows([row_out], slopes, w)
     for copy in (*e_copies[1], *e_copies[2], *e_copies[3]):
         copy.wait()
@@ -398,7 +397,7 @@
         )(*arrays)
 
     def passed_on(value, stage):
-        bits = (axes[stage], axes[stage if stage == 2 else 1 - stage])
+        bits = (axes[stage], axes[(stage + 1) % 3])
         return lax.ppermute(value, "label", [(i, i ^ bits[i % 2]) for i in range(n_label)])
 
     far_got = passed_on(summed_at((first_keep, slice(2, 4)), (first_got, slice(2, 4))), 0)

time: 29.3 us -> 28 us (0.956)
  waiting for transfers between devices: 6.82 us -> 6.24 us
  starting transfers between devices: 11.4 us -> 11 us
    ppermute x5, starting transfers between devices: 7.94 us -> 7.53 us  [passed_on(): lax.ppermute(value, 'label', [(i, i ^ bits[i % 2]) for i in range(n_label)])]
    ppermute x4, waiting for transfers between devices: 3.88 us -> 3.55 us  [swapped(): return lax.ppermute(value, axis, [(i, i ^ bit) for i in range(size)])]
  transfers between devices with their start and end apart: 9 -> 9, of which waited for: 5 -> 4; matrix products, arithmetic and copies ran while one was open for 0% -> 0% of each run, Pallas kernels for 20% -> 21%
where the time goes in v5:
time: 28 us; the launch traced here: 27.8 us
  starting transfers between devices  11 us (39%)
  Pallas kernels  9.85 us (35%)
  waiting for transfers between devices  6.24 us (22%)
  between operations  0.73 us (3%)
    ppermute x5, starting transfers between devices, passed_on(): lax.ppermute(value, 'label', [(i, i ^ bits[i % 2]) for i in range(n_label)])  7.53 us
    ppermute x4, waiting for transfers between devices, swapped(): return lax.ppermute(value, axis, [(i, i ^ bit) for i in range(size)])  3.55 us
    ppermute x4, starting transfers between devices, swapped(): return lax.ppermute(value, axis, [(i, i ^ bit) for i in range(size)])  3.45 us
    pallas_call x1, Pallas kernels, on_device(): pl.pallas_call(functools.partial(first_kernel, n_label), out_shape=[shape...  3.18 us
    ppermute x5, waiting for transfers between devices, passed_on(): lax.ppermute(value, 'label', [(i, i ^ bits[i % 2]) for i in range(n_label)])  2.69 us
    pallas_call x1, Pallas kernels, on_device(): pl.pallas_call(last_rows_kernel, out_shape=[part_shape] * 2 + [row_shape,...  1.71 us
    pallas_call x1, Pallas kernels, on_device(): pl.pallas_call(label_kernel, out_shape=[shape((CLUSTER, rows), jnp.int16)...  1.64 us
    pallas_call x1, Pallas kernels, on_device(): pl.pallas_call(keep_rows_kernel, out_shape=[tile_shape, row_shape], in_sp...  1.08 us
  transfers between devices with their start and end apart: 9, of which 4 were waited for; matrix products, arithmetic and copies ran while one was open for 0% of the time, Pallas kernels for 21%

profile of v5, /device:TPU:0, one launch (start us, length us, event | category | flops | bytes accessed | tf_op | source)
XLA Modules:
  0.0 27.8 jit_solution(6579901532017915817)
XLA Ops:
  0.6 3.2 %first_rows.1 = (bf16[1024,768]{1,0:T(8,128)(2,1)S(1)}, bf16[1024,768]{1,0:T(8,128)(2,1)S(1)}, s32[8,1024]{1,0:T(8,128)S(1)}, bf16[2,4,8,128]{3,2,1,0:T(8,128)(2...) custom-call(bf16[1024,768]{1,0:T(8,128)(2,1)} %embed_hbm.1, ...), custom_call_target="tpu_custom_call" | custom-call | flops 1610612736 | tf_op jit(solution)/shard_map/first_rows/pallas_call | solution.py:322
  3.8 0.5 %collective-permute-start = (bf16[4,1,64,768]{3,2,1,0:T(8,128)(2,1)S(1)}, bf16[4,1,64,768]{3,2,1,0:T(8,128)(2,1)S(1)}, u32[]{:S(2)}, u32[]{:S(2)}) collective-permute-start(bf16[4,1,64,768]{3,2,1,0:T(8,128)(2,1)S(1)} %get-tuple-element.29), channel_id=1, source_target_pairs={{0,1},{1,0},{2,3},{3,2},{4,5},{5,4},{6,7},{7,6},{8,9},{9,8},{10,11... | collective-permute-start | bytes 1179656 | tf_op jit(solution)/shard_map/ppermute | solution.py:291
  4.3 1.6 %send_half.1 = (s16[128,1024]{1,0:T(8,128)(2,1)S(1)}, bf16[512,768]{1,0:T(8,128)(2,1)S(1)}, bf16[512,768]{1,0:T(8,128)(2,1)S(1)}) custom-call(bf16[1024,768]{1,0:T(8,128)(2,1)S(1)} %get-tuple-element.37.embed, bf16[1024,768]{1,0:T(8,128)(2,1)S(1)} %get-tuple-element.38.w, s32[8,1024]{1,0:T(8,128)S(1)} %get-tuple-element.31.pos, ...), custom_call_target="tpu_custom_call" | custom-call | tf_op jit(solution)/shard_map/send_half/pallas_call | solution.py:353
  6.0 2.6 %collective-permute-start.1 = (bf16[512,768]{1,0:T(8,128)(2,1)S(1)}, bf16[512,768]{1,0:T(8,128)(2,1)S(1)}, u32[]{:S(2)}, u32[]{:S(2)}) collective-permute-start(bf16[512,768]{1,0:T(8,128)(2,1)S(1)} %get-tuple-element.46), channel_id=1, source_target_pairs={{0,16},{16,0},{1,17},{17,1},{2,18},{18,2},{3,19},{19,3},{4,20},{20... | collective-permute-start | bytes 2359304 | tf_op jit(solution)/shard_map/ppermute | solution.py:291
  8.6 0.0 collective-permute-done.refs_1_
  8.6 1.1 %keep_rows.1 = (bf16[512,256]{1,0:T(8,128)(2,1)S(1)}, bf16[4,1,64,768]{3,2,1,0:T(8,128)(2,1)S(1)}) custom-call(bf16[1024,768]{1,0:T(8,128)(2,1)S(1)} %get-tuple-element.37.embed, bf16[1024,768]{1,0:T(8,128)(2,1)S(1)} %get-tuple-element.38.w, s16[128,1024]{1,0:T(8,128)(2,1)S(1)} %get-tuple-element.39.word, bf16[2,4,8,128]{3,2,1,0:T(8,128)(2,1)S(1)} %get-tuple-element.40.mask, ...), custom_call_target="tpu_custom_call" | custom-call | tf_op jit(solution)/shard_map/keep_rows/pallas_call | solution.py:373
  9.7 1.6 %collective-permute-start.5 = (bf16[2,1,64,768]{3,2,1,0:T(8,128)(2,1)S(1)}, bf16[2,1,64,768]{3,2,1,0:T(8,128)(2,1)S(1)}, u32[]{:S(2)}, u32[]{:S(2)}) collective-permute-start(bf16[2,1,64,768]{3,2,1,0:T(8,128)(2,1)S(1)} %row_sum.6), channel_id=1, source_target_pairs={{0,2},{1,5},{2,0},{3,7},{4,6},{5,1},{6,4},{7,3},{8,10},{9,13},{10,... | collective-permute-start | bytes 589832 | tf_op jit(solution)/shard_map/ppermute | solution.py:401
  11.3 1.7 %last_rows.1 = (bf16[2,1,64,768]{3,2,1,0:T(8,128)(2,1)S(1)}, bf16[2,1,64,768]{3,2,1,0:T(8,128)(2,1)S(1)}, bf16[4,1,64,768]{3,2,1,0:T(8,128)(2,1)S(1)}, bf16[512,256]{1,0:T(8,128)(2,1)S(1)}, bf16[512,256]{1,0:T(8,128)(2,1)S(1)}) custom-call(bf16[1024,768]{1,0:T(8,128)(2,1)S(1)} %get-tuple-element.37.embed, bf16[1024,768]{1,0:T(8,128)(2,1)S(1)} %get-tuple-element.38.w, ...), custom_call_target="tpu_custom_call" | custom-call | flops 1610612736 | tf_op jit(solution)/shard_map/last_rows/pallas_call | solution.py:407
  13.0 0.1 collective-permute-start.4
  13.1 1.6 %collective-permute-start.3 = (bf16[2,1,64,768]{3,2,1,0:T(8,128)(2,1)S(1)}, bf16[2,1,64,768]{3,2,1,0:T(8,128)(2,1)S(1)}, u32[]{:S(2)}, u32[]{:S(2)}) collective-permute-start(bf16[2,1,64,768]{3,2,1,0:T(8,128)(2,1)S(1)} %row_sum.5), channel_id=1, source_target_pairs={{0,2},{1,5},{2,0},{3,7},{4,6},{5,1},{6,4},{7,3},{8,10},{9,13},{10,... | collective-permute-start | bytes 589832 | tf_op jit(solution)/shard_map/ppermute | solution.py:401
  14.7 0.3 %collective-permute-start.2 = (bf16[2,1,64,768]{3,2,1,0:T(8,128)(2,1)S(1)}, bf16[2,1,64,768]{3,2,1,0:T(8,128)(2,1)S(1)}, u32[]{:S(2)}, u32[]{:S(2)}) collective-permute-start(bf16[2,1,64,768]{3,2,1,0:T(8,128)(2,1)S(1)} %get-tuple-element.48), channel_id=1, source_target_pairs={{0,1},{1,0},{2,3},{3,2},{4,5},{5,4},{6,7},{7,6},{8,9},{9,8},{10,11... | collective-permute-start | bytes 589832 | tf_op jit(solution)/shard_map/ppermute | solution.py:291
  15.0 0.4 %collective-permute-done.5.refs_2_ = bf16[2,1,64,768]{3,2,1,0:T(8,128)(2,1)S(1)} collective-permute-done((bf16[2,1,64,768]{3,2,1,0:T(8,128)(2,1)S(1)}, bf16[2,1,64,768]{3,2,1,0:T(8,128)(2,1)S(1)}, u32[]{:S(2)}, u32[]{:S(2)}) %collective-permute-start.5) | collective-permute-done | bytes 196640 | tf_op jit(solution)/shard_map/ppermute | solution.py:401
  15.4 0.0 collective-permute-done.4.refs_1_
  15.5 1.6 %collective-permute-start.7 = (bf16[1,1,64,768]{3,2,1,0:T(8,128)(2,1)S(1)}, bf16[1,1,64,768]{3,2,1,0:T(8,128)(2,1)S(1)}, u32[]{:S(2)}, u32[]{:S(2)}) collective-permute-start(bf16[1,1,64,768]{3,2,1,0:T(8,128)(2,1)S(1)} %row_sum.8), channel_id=1, source_target_pairs={{0,4},{1,9},{2,6},{3,11},{4,0},{5,13},{6,2},{7,15},{8,12},{9,1},{1... | collective-permute-start | bytes 294920 | tf_op jit(solution)/shard_map/ppermute | solution.py:401
  17.1 1.0 %keep_half.1.kept = bf16[512,768]{1,0:T(8,128)(2,1)S(1)} custom-call(bf16[1024,768]{1,0:T(8,128)(2,1)S(1)} %get-tuple-element.37.embed, bf16[512,256]{1,0:T(8,128)(2,1)S(1)} %get-tuple-element.28.refs_0_, bf16[512,256]{1,0:T(8,128)(2,1)S(1)} %get-tuple-element.43.refs_1_, bf16[512,256]{1,0:T(8,128)(2,1)S(1)} %get-tuple-element.44.refs_2_, ...), custom_call_target="tpu_custom_call" | custom-call | tf_op jit(solution)/shard_map/keep_half/pallas_call | solution.py:436
  18.2 0.5 %collective-permute-start.6 = (bf16[1,1,64,768]{3,2,1,0:T(8,128)(2,1)S(1)}, bf16[1,1,64,768]{3,2,1,0:T(8,128)(2,1)S(1)}, u32[]{:S(2)}, u32[]{:S(2)}) collective-permute-start(bf16[1,1,64,768]{3,2,1,0:T(8,128)(2,1)S(1)} %row_sum.7), channel_id=1, source_target_pairs={{0,4},{1,9},{2,6},{3,11},{4,0},{5,13},{6,2},{7,15},{8,12},{9,1},{1... | collective-permute-start | bytes 294920 | tf_op jit(solution)/shard_map/ppermute | solution.py:401
  18.7 0.2 collective-permute-done.3.refs_2_
  18.9 0.0 collective-permute-done.2.refs_1_
  18.9 2.0 %collective-permute-done.7.refs_3_ = bf16[1,1,64,768]{3,2,1,0:T(8,128)(2,1)S(1)} collective-permute-done((bf16[1,1,64,768]{3,2,1,0:T(8,128)(2,1)S(1)}, bf16[1,1,64,768]{3,2,1,0:T(8,128)(2,1)S(1)}, u32[]{:S(2)}, u32[]{:S(2)}) %collective-permute-start.7) | collective-permute-done | bytes 98336 | tf_op jit(solution)/shard_map/ppermute | solution.py:401
  20.9 0.1 row_sum.9
  21.0 2.2 %collective-permute-start.8 = (bf16[1,1,64,768]{3,2,1,0:T(8,128)(2,1)S(1)}, bf16[1,1,64,768]{3,2,1,0:T(8,128)(2,1)S(1)}, u32[]{:S(2)}, u32[]{:S(2)}) collective-permute-start(bf16[1,1,64,768]{3,2,1,0:T(8,128)(2,1)S(1)} %row_sum.9), channel_id=1, source_target_pairs={{0,8},{1,3},{2,10},{3,1},{4,12},{5,7},{6,14},{7,5},{8,0},{9,11},{1... | collective-permute-start | bytes 294920 | tf_op jit(solution)/shard_map/ppermute | solution.py:401
  23.2 3.5 %collective-permute-done.1.got = bf16[512,768]{1,0:T(8,128)(2,1)S(1)} collective-permute-done((bf16[512,768]{1,0:T(8,128)(2,1)S(1)}, bf16[512,768]{1,0:T(8,128)(2,1)S(1)}, u32[]{:S(2)}, u32[]{:S(2)}) %collective-permute-start.1) | collective-permute-done | bytes 786464 | tf_op jit(solution)/shard_map/ppermute | solution.py:291
  26.8 0.1 half_sum.1.summed
  26.8 0.0 collective-permute-done.6.refs_3_
  26.9 0.0 collective-permute-done.8.refs_4_
  26.9 0.9 %finish.1 = (bf16[64,768]{1,0:T(8,128)(2,1)}, bf16[512,768]{1,0:T(8,128)(2,1)}) custom-call(bf16[512,768]{1,0:T(8,128)(2,1)S(1)} %keep_half.1.kept, bf16[512,768]{1,0:T(8,128)(2,1)S(1)} %collective-permute-done.1.got, bf16[256,768]{1,0:T(8,128)(2,1)S(1)} %half_sum.1.summed, bf16[4,1,64,768]{3,2,1,0:T(8,128)(2,1)S(1)} %get-tuple-element.47.refs_0_, ...), custom_call_target="tpu_custom_call" | custom-call | tf_op jit(solution)/shard_map/finish/pallas_call | solution.py:468
  (4 shorter events, 0.2 us)
Async XLA Ops:
  3.8 4.7 %collective-permute-start = (bf16[4,1,64,768]{3,2,1,0:T(8,128)(2,1)S(1)}, bf16[4,1,64,768]{3,2,1,0:T(8,128)(2,1)S(1)}, u32[]{:S(2)}, u32[]{:S(2)}) collective-permute-start(bf16[4,1,64,768]{3,2,1,0:T(8,128)(2,1)S(1)} %get-tuple-element.29), channel_id=1, source_target_pairs={{0,1},{1,0},{2,3},{3,2},{4,5},{5,4},{6,7},{7,6},{8,9},{9,8},{10,11... | collective-permute-start | bytes 1179656 | tf_op jit(solution)/shard_map/ppermute | solution.py:291
  6.0 20.8 %collective-permute-start.1 = (bf16[512,768]{1,0:T(8,128)(2,1)S(1)}, bf16[512,768]{1,0:T(8,128)(2,1)S(1)}, u32[]{:S(2)}, u32[]{:S(2)}) collective-permute-start(bf16[512,768]{1,0:T(8,128)(2,1)S(1)} %get-tuple-element.46), channel_id=1, source_target_pairs={{0,16},{16,0},{1,17},{17,1},{2,18},{18,2},{3,19},{19,3},{4,20},{20... | collective-permute-start | bytes 2359304 | tf_op jit(solution)/shard_map/ppermute | solution.py:291
  9.7 5.7 %collective-permute-start.5 = (bf16[2,1,64,768]{3,2,1,0:T(8,128)(2,1)S(1)}, bf16[2,1,64,768]{3,2,1,0:T(8,128)(2,1)S(1)}, u32[]{:S(2)}, u32[]{:S(2)}) collective-permute-start(bf16[2,1,64,768]{3,2,1,0:T(8,128)(2,1)S(1)} %row_sum.6), channel_id=1, source_target_pairs={{0,2},{1,5},{2,0},{3,7},{4,6},{5,1},{6,4},{7,3},{8,10},{9,13},{10,... | collective-permute-start | bytes 589832 | tf_op jit(solution)/shard_map/ppermute | solution.py:401
  13.0 2.4 %collective-permute-start.4 = (bf16[2,1,64,768]{3,2,1,0:T(8,128)(2,1)S(1)}, bf16[2,1,64,768]{3,2,1,0:T(8,128)(2,1)S(1)}, u32[]{:S(2)}, u32[]{:S(2)}) collective-permute-start(bf16[2,1,64,768]{3,2,1,0:T(8,128)(2,1)S(1)} %get-tuple-element.51), channel_id=1, source_target_pairs={{0,1},{1,0},{2,3},{3,2},{4,5},{5,4},{6,7},{7,6},{8,9},{9,8},{10,11... | collective-permute-start | bytes 589832 | tf_op jit(solution)/shard_map/ppermute | solution.py:291
  13.1 5.7 %collective-permute-start.3 = (bf16[2,1,64,768]{3,2,1,0:T(8,128)(2,1)S(1)}, bf16[2,1,64,768]{3,2,1,0:T(8,128)(2,1)S(1)}, u32[]{:S(2)}, u32[]{:S(2)}) collective-permute-start(bf16[2,1,64,768]{3,2,1,0:T(8,128)(2,1)S(1)} %row_sum.5), channel_id=1, source_target_pairs={{0,2},{1,5},{2,0},{3,7},{4,6},{5,1},{6,4},{7,3},{8,10},{9,13},{10,... | collective-permute-start | bytes 589832 | tf_op jit(solution)/shard_map/ppermute | solution.py:401
  14.7 4.2 %collective-permute-start.2 = (bf16[2,1,64,768]{3,2,1,0:T(8,128)(2,1)S(1)}, bf16[2,1,64,768]{3,2,1,0:T(8,128)(2,1)S(1)}, u32[]{:S(2)}, u32[]{:S(2)}) collective-permute-start(bf16[2,1,64,768]{3,2,1,0:T(8,128)(2,1)S(1)} %get-tuple-element.48), channel_id=1, source_target_pairs={{0,1},{1,0},{2,3},{3,2},{4,5},{5,4},{6,7},{7,6},{8,9},{9,8},{10,11... | collective-permute-start | bytes 589832 | tf_op jit(solution)/shard_map/ppermute | solution.py:291
  15.5 5.4 %collective-permute-start.7 = (bf16[1,1,64,768]{3,2,1,0:T(8,128)(2,1)S(1)}, bf16[1,1,64,768]{3,2,1,0:T(8,128)(2,1)S(1)}, u32[]{:S(2)}, u32[]{:S(2)}) collective-permute-start(bf16[1,1,64,768]{3,2,1,0:T(8,128)(2,1)S(1)} %row_sum.8), channel_id=1, source_target_pairs={{0,4},{1,9},{2,6},{3,11},{4,0},{5,13},{6,2},{7,15},{8,12},{9,1},{1... | collective-permute-start | bytes 294920 | tf_op jit(solution)/shard_map/ppermute | solution.py:401
  18.2 8.7 %collective-permute-start.6 = (bf16[1,1,64,768]{3,2,1,0:T(8,128)(2,1)S(1)}, bf16[1,1,64,768]{3,2,1,0:T(8,128)(2,1)S(1)}, u32[]{:S(2)}, u32[]{:S(2)}) collective-permute-start(bf16[1,1,64,768]{3,2,1,0:T(8,128)(2,1)S(1)} %row_sum.7), channel_id=1, source_target_pairs={{0,4},{1,9},{2,6},{3,11},{4,0},{5,13},{6,2},{7,15},{8,12},{9,1},{1... | collective-permute-start | bytes 294920 | tf_op jit(solution)/shard_map/ppermute | solution.py:401
  21.0 5.9 %collective-permute-start.8 = (bf16[1,1,64,768]{3,2,1,0:T(8,128)(2,1)S(1)}, bf16[1,1,64,768]{3,2,1,0:T(8,128)(2,1)S(1)}, u32[]{:S(2)}, u32[]{:S(2)}) collective-permute-start(bf16[1,1,64,768]{3,2,1,0:T(8,128)(2,1)S(1)} %row_sum.9), channel_id=1, source_target_pairs={{0,8},{1,3},{2,10},{3,1},{4,12},{5,7},{6,14},{7,5},{8,0},{9,11},{1... | collective-permute-start | bytes 294920 | tf_op jit(solution)/shard_map/ppermute | solution.py:401

commit v6 on v5

--- a/solution.py
+++ b/solution.py
@@ -89,9 +89,9 @@
         word[:, lanes] = found
 
 
-def first_kernel(n_label, embed_hbm, weight_hbm, bias_hbm, beam_hbm, pos_hbm, embed, w, pos, mask, bias_full,
-                 first_slopes_t, own_slopes_t, row_out, bias_raw, beam_raw, pos_raw, beam, word, scores, slopes, sems):
-    half_rows = own_slopes_t.shape[0]
+def send_kernel(n_label, embed_hbm, weight_hbm, bias_hbm, beam_hbm, pos_hbm, embed, w, word, mask, bias_full, slopes_t,
+                label_out, bias_raw, beam_raw, pos_raw, beam, pos, scores, sems):
+    half_rows = label_out.shape[0]
     clusters = half_rows // CLUSTER
     tiles = embed.shape[0] // TILE
     half = 1 - half_index()
@@ -125,7 +125,7 @@
                         sems.at[5 + at],
                     )
                 )
-    for copy in (*small, *e_copies[0], *w_copies):
+    for copy in (*small, *e_copies[0], w_copies[0]):
         copy.start()
     for copy in small:
         copy.wait()
@@ -170,7 +170,7 @@
             beam[group : group + 1] = beam_raw[pl.ds(block_in(t, i, over, core), 1)]
     for t in range(tiles):
         set_positives(t)
-    set_words([0], pos, word)
+    set_words(range(tiles), pos, word)
 
     row = lax.broadcasted_iota(jnp.int32, (2 * clusters, 2 * clusters * INST_BLOCK), 0)
     column = lax.broadcasted_iota(jnp.int32, (2 * clusters, 2 * clusters * INST_BLOCK), 1)
@@ -184,41 +184,24 @@
             held = jnp.where(beam[...] == first_cluster + (i ^ (half * clusters)), 0.5 * SCALE, 0.0)
             held = jnp.broadcast_to(jnp.max(held, axis=1, keepdims=True), (2 * BLOCKS, INST_BLOCK))
             mask[k, c] = jnp.where(low, held[:BLOCKS], held[BLOCKS:]).astype(BF16)
-    for copy in (w_copies[0], *e_copies[0]):
-        copy.wait()
+    w_copies[0].wait()
 
     def before(k, t, h):
-        if (k, h) == (1, 0):
-            w_copies[1].wait()
+        if h == 0:
+            for copy in e_copies[t]:
+                copy.wait()
+            if t == 1:
+                w_copies[1].start()
 
     def emit(k, t, c, part):
-        out = own_slopes_t if k else first_slopes_t
-        out[c * CLUSTER : (c + 1) * CLUSTER] = part
-        slopes[:, (k * clusters + c) * CLUSTER : (k * clusters + c + 1) * CLUSTER] = part.T
-
-    jobs = [(k, 0, h) for k in range(2) for h in range(half_rows // CHUNK)]
-    slope_chunks(jobs, scores, w, embed, bias_full, mask, word, before, emit)
-    store_rows([row_out], slopes, w)
-    for copy in (*e_copies[1], *e_copies[2], *e_copies[3]):
-        copy.wait()
-
-
-def label_kernel(embed, w, pos, mask, bias_full, one_slopes_t, word, slopes_t, label_out, scores):
-    half_rows = label_out.shape[0]
-    tiles = embed.shape[0] // TILE
-    set_words(range(1, tiles), pos, word)
-
-    def emit(k, t, c, part):
-        slopes_t[c * CLUSTER : (c + 1) * CLUSTER, (t - 1) * TILE : t * TILE] = part
+        slopes_t[c * CLUSTER : (c + 1) * CLUSTER, t * TILE : (t + 1) * TILE] = part
         if t == tiles - 1 and (c + 1) % (CHUNK // CLUSTER) == 0:
             rows = slice((c + 1) * CLUSTER - CHUNK, (c + 1) * CLUSTER)
-            label_out[rows] = (
-                jnp.dot(one_slopes_t[rows], embed[:TILE], preferred_element_type=F32)
-                + jnp.dot(slopes_t[rows], embed[TILE:], preferred_element_type=F32)
-            ).astype(BF16)
-
-    jobs = [(0, t, h) for t in range(1, tiles) for h in range(half_rows // CHUNK)]
-    slope_chunks(jobs, scores, w, embed, bias_full, mask, word, lambda *job: None, emit)
+            label_out[rows] = jnp.dot(slopes_t[rows], embed[...], preferred_element_type=F32).astype(BF16)
+
+    jobs = [(0, t, h) for t in range(tiles) for h in range(half_rows // CHUNK)]
+    slope_chunks(jobs, scores, w, embed, bias_full, mask, word, before, emit)
+    w_copies[1].wait()
 
 
 def store_rows(outs, slopes, w):
@@ -233,7 +216,7 @@
 
     def emit(k, t, c, part):
         if c == 0:
-            slopes[:, :half_rows] = first_slopes_t[:, (t - 1) * TILE : t * TILE].T
+            slopes[:, :half_rows] = first_slopes_t[:, t * TILE : (t + 1) * TILE].T
         own_slopes_t[c * CLUSTER : (c + 1) * CLUSTER] = part
         slopes[:, half_rows + c * CLUSTER : half_rows + (c + 1) * CLUSTER] = part.T
 
@@ -242,8 +225,8 @@
     store_rows(outs, slopes, w)
 
 
-def keep_rows_kernel(embed, w, word, mask, bias_full, first_slopes_t, own_slopes_t, row_out, scores, slopes):
-    row_tile(1, [row_out], embed, w, word, mask, bias_full, first_slopes_t, own_slopes_t, scores, slopes)
+def rows_kernel(t, embed, w, word, mask, bias_full, first_slopes_t, own_slopes_t, row_out, scores, slopes):
+    row_tile(t, [row_out], embed, w, word, mask, bias_full, first_slopes_t, own_slopes_t, scores, slopes)
 
 
 def last_rows_kernel(embed, w, word, mask, bias_full, first_slopes_t, *rest):
@@ -319,67 +302,52 @@
     def cost(halves):
         return pl.CostEstimate(flops=halves * 2 * rows * half_rows * features, bytes_accessed=0, transcendentals=0)
 
-    *common, head_slopes_t, one_slopes_t, first_send = pl.pallas_call(
-        functools.partial(first_kernel, n_label),
+    *shared, label_send = pl.pallas_call(
+        functools.partial(send_kernel, n_label),
         out_shape=[
             shape((rows, features), BF16),
             shape((labels, features), BF16),
-            shape(pos_rows.shape, jnp.int32),
+            shape((CLUSTER, rows), jnp.int16),
             shape((2, clusters, BLOCKS, INST_BLOCK), BF16),
             shape((2, clusters, CLUSTER, INST_BLOCK), F32),
-            tile_shape,
-            tile_shape,
-            row_shape,
+            shape((half_rows, rows), BF16),
+            shape((half_rows, features), BF16),
         ],
         in_specs=[hbm] * 5,
-        out_specs=[vmem] * 8,
+        out_specs=[vmem] * 7,
         scratch_shapes=[
             pltpu.VMEM(bias_rows.shape, BF16),
             pltpu.VMEM(beam.shape, jnp.int32),
             pltpu.VMEM(pos_rows.shape, jnp.int32),
             pltpu.VMEM((2 * BLOCKS, beam.shape[1]), jnp.int32),
-            pltpu.VMEM((CLUSTER, TILE), jnp.int16),
+            pltpu.VMEM(pos_rows.shape, jnp.int32),
             score_scratch,
-            slope_scratch,
             pltpu.SemaphoreType.DMA((5 + n_label,)),
         ],
         compiler_params=params,
         cost_estimate=cost(2),
-        name="first_rows",
+        name="send_half",
     )(*(pltpu.with_memory_space_constraint(x, pltpu.HBM) for x in (embed, weight, bias_rows, beam, pos_rows)))
-
+    embed_own = shared[0]
+
+    label_got = swapped(label_send, "dp", n_dp, n_dp // 2)
+
+    def tile_rows(t, name, inputs):
+        return pl.pallas_call(
+            functools.partial(rows_kernel, t),
+            out_shape=[tile_shape, row_shape],
+            in_specs=[vmem] * 6,
+            out_specs=[vmem] * 2,
+            scratch_shapes=[score_scratch, slope_scratch],
+            compiler_params=params,
+            cost_estimate=cost(0),
+            name=name,
+        )(*inputs)
+
+    one_slopes_t, first_send = tile_rows(0, "first_rows", shared)
     first_got = swapped(first_send, "label", n_label, 1)
-
-    word, first_slopes_t, label_send = pl.pallas_call(
-        label_kernel,
-        out_shape=[
-            shape((CLUSTER, rows), jnp.int16),
-            shape((half_rows, rows - TILE), BF16),
-            shape((half_rows, features), BF16),
-        ],
-        in_specs=[vmem] * 6,
-        out_specs=[vmem] * 3,
-        scratch_shapes=[score_scratch],
-        compiler_params=params,
-        cost_estimate=cost(0),
-        name="send_half",
-    )(*common, head_slopes_t)
-    embed_own, w, _, mask, bias_full = common
-    shared = (embed_own, w, word, mask, bias_full, first_slopes_t)
-
-    label_got = swapped(label_send, "dp", n_dp, n_dp // 2)
+    two_slopes_t, first_keep = tile_rows(1, "keep_rows", shared)
     first_got, *shared = lax.optimization_barrier((first_got, *shared))
-
-    two_slopes_t, first_keep = pl.pallas_call(
-        keep_rows_kernel,
-        out_shape=[tile_shape, row_shape],
-        in_specs=[vmem] * 6,
-        out_specs=[vmem] * 2,
-        scratch_shapes=[score_scratch, slope_scratch],
-        compiler_params=params,
-        cost_estimate=cost(0),
-        name="keep_rows",
-    )(*shared)
 
     axes = [2 * subs, 4 * subs, 8 * subs]
 
@@ -414,7 +382,7 @@
             pltpu.VMEM((2, TILE, labels), BF16),
         ],
         compiler_params=params,
-        cost_estimate=cost(2),
+        cost_estimate=cost(0),
         name="last_rows",
     )(*shared)
 

time: 28 us -> 29 us (1.036)
  Pallas kernels: 9.85 us -> 10.6 us
    ppermute x5, waiting for transfers between devices: 2.69 us -> 4.68 us  [passed_on(): lax.ppermute(value, 'label', [(i, i ^ bits[i % 2]) for i in range(n_label)])]
    ppermute x4, waiting for transfers between devices: 3.55 us -> 1.73 us  [swapped(): return lax.ppermute(value, axis, [(i, i ^ bit) for i in range(size)])]
    pallas_call x3, Pallas kernels: 5.9 us -> 6.64 us  [the longest x1 4.48 us: on_device(): pl.pallas_call(functools.partial(send_kernel, n_label), out_shape=[shape(...]
  transfers between devices with their start and end apart: 9 -> 9, of which waited for: 4 -> 6; matrix products, arithmetic and copies ran while one was open for 0% -> 0% of each run, Pallas kernels for 21% -> 18%
where the time goes in v6:
time: 29 us; the launch traced here: 28.8 us
  starting transfers between devices  11 us (38%)
  Pallas kernels  10.6 us (37%)
  waiting for transfers between devices  6.41 us (22%)
  between operations  0.73 us (3%)
    ppermute x5, starting transfers between devices, passed_on(): lax.ppermute(value, 'label', [(i, i ^ bits[i % 2]) for i in range(n_label)])  7.53 us
    ppermute x5, waiting for transfers between devices, passed_on(): lax.ppermute(value, 'label', [(i, i ^ bits[i % 2]) for i in range(n_label)])  4.68 us
    pallas_call x1, Pallas kernels, on_device(): pl.pallas_call(functools.partial(send_kernel, n_label), out_shape=[shape(...  4.48 us
    ppermute x4, starting transfers between devices, swapped(): return lax.ppermute(value, axis, [(i, i ^ bit) for i in range(size)])  3.51 us
    pallas_call x2, Pallas kernels, tile_rows(): pl.pallas_call(functools.partial(rows_kernel, t), out_shape=[tile_shape,...  2.15 us
    ppermute x4, waiting for transfers between devices, swapped(): return lax.ppermute(value, axis, [(i, i ^ bit) for i in range(size)])  1.73 us
    pallas_call x1, Pallas kernels, on_device(): pl.pallas_call(last_rows_kernel, out_shape=[part_shape] * 2 + [row_shape,...  1.71 us
    pallas_call x1, Pallas kernels, on_device(): pl.pallas_call(keep_kernel, out_shape=shape((half_rows, features), BF16),...  0.98 us
  transfers between devices with their start and end apart: 9, of which 6 were waited for; matrix products, arithmetic and copies ran while one was open for 0% of the time, Pallas kernels for 18%

profile of v6, /device:TPU:0, one launch (start us, length us, event | category | flops | bytes accessed | tf_op | source)
XLA Modules:
  0.0 28.8 jit_solution(17540685566426705165)
XLA Ops:
  0.6 4.5 %send_half.1 = (bf16[1024,768]{1,0:T(8,128)(2,1)S(1)}, bf16[1024,768]{1,0:T(8,128)(2,1)S(1)}, s16[128,1024]{1,0:T(8,128)(2,1)S(1)}, bf16[2,4,8,128]{3,2,1,0:T(8,...) custom-call(bf16[1024,768]{1,0:T(8,128)(2,1)} %embed_hbm.1, ...), custom_call_target="tpu_custom_call" | custom-call | flops 1610612736 | tf_op jit(solution)/shard_map/send_half/pallas_call | solution.py:305
  5.1 3.0 %collective-permute-start.1 = (bf16[512,768]{1,0:T(8,128)(2,1)S(1)}, bf16[512,768]{1,0:T(8,128)(2,1)S(1)}, u32[]{:S(2)}, u32[]{:S(2)}) collective-permute-start(bf16[512,768]{1,0:T(8,128)(2,1)S(1)} %get-tuple-element.42), channel_id=1, source_target_pairs={{0,16},{16,0},{1,17},{17,1},{2,18},{18,2},{3,19},{19,3},{4,20},{20... | collective-permute-start | bytes 2359304 | tf_op jit(solution)/shard_map/ppermute | solution.py:274
  8.1 1.1 %first_rows.1 = (bf16[512,256]{1,0:T(8,128)(2,1)S(1)}, bf16[4,1,64,768]{3,2,1,0:T(8,128)(2,1)S(1)}) custom-call(bf16[1024,768]{1,0:T(8,128)(2,1)S(1)} %get-tuple-element.34.embed, bf16[1024,768]{1,0:T(8,128)(2,1)S(1)} %get-tuple-element.35.w, s16[128,1024]{1,0:T(8,128)(2,1)S(1)} %get-tuple-element.36.word, ...), custom_call_target="tpu_custom_call" | custom-call | tf_op jit(solution)/shard_map/first_rows/pallas_call | solution.py:336
  9.2 0.1 collective-permute-start
  9.3 1.1 %keep_rows.1 = (bf16[512,256]{1,0:T(8,128)(2,1)S(1)}, bf16[4,1,64,768]{3,2,1,0:T(8,128)(2,1)S(1)}) custom-call(bf16[1024,768]{1,0:T(8,128)(2,1)S(1)} %get-tuple-element.34.embed, bf16[1024,768]{1,0:T(8,128)(2,1)S(1)} %get-tuple-element.35.w, s16[128,1024]{1,0:T(8,128)(2,1)S(1)} %get-tuple-element.36.word, bf16[2,4,8,128]{3,2,1,0:T(8,128)(2,1)S(1)} %get-tuple-element.37.mask, ...), custom_call_target="tpu_custom_call" | custom-call | tf_op jit(solution)/shard_map/keep_rows/pallas_call | solution.py:336
  10.4 0.6 %collective-permute-done.refs_1_ = bf16[4,1,64,768]{3,2,1,0:T(8,128)(2,1)S(1)} collective-permute-done((bf16[4,1,64,768]{3,2,1,0:T(8,128)(2,1)S(1)}, bf16[4,1,64,768]{3,2,1,0:T(8,128)(2,1)S(1)}, u32[]{:S(2)}, u32[]{:S(2)}) %collective-permute-start) | collective-permute-done | bytes 393248 | tf_op jit(solution)/shard_map/ppermute | solution.py:274
  11.1 1.6 %collective-permute-start.5 = (bf16[2,1,64,768]{3,2,1,0:T(8,128)(2,1)S(1)}, bf16[2,1,64,768]{3,2,1,0:T(8,128)(2,1)S(1)}, u32[]{:S(2)}, u32[]{:S(2)}) collective-permute-start(bf16[2,1,64,768]{3,2,1,0:T(8,128)(2,1)S(1)} %row_sum.6), channel_id=1, source_target_pairs={{0,2},{1,5},{2,0},{3,7},{4,6},{5,1},{6,4},{7,3},{8,10},{9,13},{10,... | collective-permute-start | bytes 589832 | tf_op jit(solution)/shard_map/ppermute | solution.py:369
  12.6 1.7 %last_rows.1 = (bf16[2,1,64,768]{3,2,1,0:T(8,128)(2,1)S(1)}, bf16[2,1,64,768]{3,2,1,0:T(8,128)(2,1)S(1)}, bf16[4,1,64,768]{3,2,1,0:T(8,128)(2,1)S(1)}, bf16[512,256]{1,0:T(8,128)(2,1)S(1)}, bf16[512,256]{1,0:T(8,128)(2,1)S(1)}) custom-call(bf16[1024,768]{1,0:T(8,128)(2,1)S(1)} %get-tuple-element.34.embed, bf16[1024,768]{1,0:T(8,128)(2,1)S(1)} %get-tuple-element.35.w, ...), custom_call_target="tpu_custom_call" | custom-call | tf_op jit(solution)/shard_map/last_rows/pallas_call | solution.py:375
  14.4 0.1 collective-permute-start.4
  14.5 1.5 %collective-permute-start.3 = (bf16[2,1,64,768]{3,2,1,0:T(8,128)(2,1)S(1)}, bf16[2,1,64,768]{3,2,1,0:T(8,128)(2,1)S(1)}, u32[]{:S(2)}, u32[]{:S(2)}) collective-permute-start(bf16[2,1,64,768]{3,2,1,0:T(8,128)(2,1)S(1)} %row_sum.5), channel_id=1, source_target_pairs={{0,2},{1,5},{2,0},{3,7},{4,6},{5,1},{6,4},{7,3},{8,10},{9,13},{10,... | collective-permute-start | bytes 589832 | tf_op jit(solution)/shard_map/ppermute | solution.py:369
  16.0 0.4 %collective-permute-start.2 = (bf16[2,1,64,768]{3,2,1,0:T(8,128)(2,1)S(1)}, bf16[2,1,64,768]{3,2,1,0:T(8,128)(2,1)S(1)}, u32[]{:S(2)}, u32[]{:S(2)}) collective-permute-start(bf16[2,1,64,768]{3,2,1,0:T(8,128)(2,1)S(1)} %get-tuple-element.44), channel_id=1, source_target_pairs={{0,1},{1,0},{2,3},{3,2},{4,5},{5,4},{6,7},{7,6},{8,9},{9,8},{10,11... | collective-permute-start | bytes 589832 | tf_op jit(solution)/shard_map/ppermute | solution.py:274
  16.3 0.4 %collective-permute-done.5.refs_2_ = bf16[2,1,64,768]{3,2,1,0:T(8,128)(2,1)S(1)} collective-permute-done((bf16[2,1,64,768]{3,2,1,0:T(8,128)(2,1)S(1)}, bf16[2,1,64,768]{3,2,1,0:T(8,128)(2,1)S(1)}, u32[]{:S(2)}, u32[]{:S(2)}) %collective-permute-start.5) | collective-permute-done | bytes 196640 | tf_op jit(solution)/shard_map/ppermute | solution.py:369
  16.8 0.0 collective-permute-done.4.refs_1_
  16.8 1.6 %collective-permute-start.7 = (bf16[1,1,64,768]{3,2,1,0:T(8,128)(2,1)S(1)}, bf16[1,1,64,768]{3,2,1,0:T(8,128)(2,1)S(1)}, u32[]{:S(2)}, u32[]{:S(2)}) collective-permute-start(bf16[1,1,64,768]{3,2,1,0:T(8,128)(2,1)S(1)} %row_sum.8), channel_id=1, source_target_pairs={{0,4},{1,9},{2,6},{3,11},{4,0},{5,13},{6,2},{7,15},{8,12},{9,1},{1... | collective-permute-start | bytes 294920 | tf_op jit(solution)/shard_map/ppermute | solution.py:369
  18.5 1.0 %keep_half.1.kept = bf16[512,768]{1,0:T(8,128)(2,1)S(1)} custom-call(bf16[1024,768]{1,0:T(8,128)(2,1)S(1)} %get-tuple-element.34.embed, bf16[512,256]{1,0:T(8,128)(2,1)S(1)} %get-tuple-element.31.refs_0_, bf16[512,256]{1,0:T(8,128)(2,1)S(1)} %get-tuple-element.32.refs_1_, bf16[512,256]{1,0:T(8,128)(2,1)S(1)} %get-tuple-element.40.refs_2_, ...), custom_call_target="tpu_custom_call" | custom-call | tf_op jit(solution)/shard_map/keep_half/pallas_call | solution.py:404
  19.5 0.5 %collective-permute-start.6 = (bf16[1,1,64,768]{3,2,1,0:T(8,128)(2,1)S(1)}, bf16[1,1,64,768]{3,2,1,0:T(8,128)(2,1)S(1)}, u32[]{:S(2)}, u32[]{:S(2)}) collective-permute-start(bf16[1,1,64,768]{3,2,1,0:T(8,128)(2,1)S(1)} %row_sum.7), channel_id=1, source_target_pairs={{0,4},{1,9},{2,6},{3,11},{4,0},{5,13},{6,2},{7,15},{8,12},{9,1},{1... | collective-permute-start | bytes 294920 | tf_op jit(solution)/shard_map/ppermute | solution.py:369
  20.0 0.2 collective-permute-done.3.refs_2_
  20.2 0.0 collective-permute-done.2.refs_1_
  20.2 2.0 %collective-permute-done.7.refs_3_ = bf16[1,1,64,768]{3,2,1,0:T(8,128)(2,1)S(1)} collective-permute-done((bf16[1,1,64,768]{3,2,1,0:T(8,128)(2,1)S(1)}, bf16[1,1,64,768]{3,2,1,0:T(8,128)(2,1)S(1)}, u32[]{:S(2)}, u32[]{:S(2)}) %collective-permute-start.7) | collective-permute-done | bytes 98336 | tf_op jit(solution)/shard_map/ppermute | solution.py:369
  22.2 0.1 row_sum.9
  22.3 2.3 %collective-permute-start.8 = (bf16[1,1,64,768]{3,2,1,0:T(8,128)(2,1)S(1)}, bf16[1,1,64,768]{3,2,1,0:T(8,128)(2,1)S(1)}, u32[]{:S(2)}, u32[]{:S(2)}) collective-permute-start(bf16[1,1,64,768]{3,2,1,0:T(8,128)(2,1)S(1)} %row_sum.9), channel_id=1, source_target_pairs={{0,8},{1,3},{2,10},{3,1},{4,12},{5,7},{6,14},{7,5},{8,0},{9,11},{1... | collective-permute-start | bytes 294920 | tf_op jit(solution)/shard_map/ppermute | solution.py:369
  24.6 1.1 %collective-permute-done.1.got = bf16[512,768]{1,0:T(8,128)(2,1)S(1)} collective-permute-done((bf16[512,768]{1,0:T(8,128)(2,1)S(1)}, bf16[512,768]{1,0:T(8,128)(2,1)S(1)}, u32[]{:S(2)}, u32[]{:S(2)}) %collective-permute-start.1) | collective-permute-done | bytes 786464 | tf_op jit(solution)/shard_map/ppermute | solution.py:274
  25.7 0.1 half_sum.1.summed
  25.8 0.0 collective-permute-done.6.refs_3_
  25.8 2.1 %collective-permute-done.8.refs_4_ = bf16[1,1,64,768]{3,2,1,0:T(8,128)(2,1)S(1)} collective-permute-done((bf16[1,1,64,768]{3,2,1,0:T(8,128)(2,1)S(1)}, bf16[1,1,64,768]{3,2,1,0:T(8,128)(2,1)S(1)}, u32[]{:S(2)}, u32[]{:S(2)}) %collective-permute-start.8) | collective-permute-done | bytes 98336 | tf_op jit(solution)/shard_map/ppermute | solution.py:369
  27.8 0.9 %finish.1 = (bf16[64,768]{1,0:T(8,128)(2,1)}, bf16[512,768]{1,0:T(8,128)(2,1)}) custom-call(bf16[512,768]{1,0:T(8,128)(2,1)S(1)} %keep_half.1.kept, bf16[512,768]{1,0:T(8,128)(2,1)S(1)} %collective-permute-done.1.got, bf16[256,768]{1,0:T(8,128)(2,1)S(1)} %half_sum.1.summed, bf16[4,1,64,768]{3,2,1,0:T(8,128)(2,1)S(1)} %get-tuple-element.43.refs_0_, ...), custom_call_target="tpu_custom_call" | custom-call | tf_op jit(solution)/shard_map/finish/pallas_call | solution.py:436
  (4 shorter events, 0.2 us)
Async XLA Ops:
  5.1 20.5 %collective-permute-start.1 = (bf16[512,768]{1,0:T(8,128)(2,1)S(1)}, bf16[512,768]{1,0:T(8,128)(2,1)S(1)}, u32[]{:S(2)}, u32[]{:S(2)}) collective-permute-start(bf16[512,768]{1,0:T(8,128)(2,1)S(1)} %get-tuple-element.42), channel_id=1, source_target_pairs={{0,16},{16,0},{1,17},{17,1},{2,18},{18,2},{3,19},{19,3},{4,20},{20... | collective-permute-start | bytes 2359304 | tf_op jit(solution)/shard_map/ppermute | solution.py:274
  9.2 1.8 %collective-permute-start = (bf16[4,1,64,768]{3,2,1,0:T(8,128)(2,1)S(1)}, bf16[4,1,64,768]{3,2,1,0:T(8,128)(2,1)S(1)}, u32[]{:S(2)}, u32[]{:S(2)}) collective-permute-start(bf16[4,1,64,768]{3,2,1,0:T(8,128)(2,1)S(1)} %get-tuple-element.33), channel_id=1, source_target_pairs={{0,1},{1,0},{2,3},{3,2},{4,5},{5,4},{6,7},{7,6},{8,9},{9,8},{10,11... | collective-permute-start | bytes 1179656 | tf_op jit(solution)/shard_map/ppermute | solution.py:274
  11.1 5.7 %collective-permute-start.5 = (bf16[2,1,64,768]{3,2,1,0:T(8,128)(2,1)S(1)}, bf16[2,1,64,768]{3,2,1,0:T(8,128)(2,1)S(1)}, u32[]{:S(2)}, u32[]{:S(2)}) collective-permute-start(bf16[2,1,64,768]{3,2,1,0:T(8,128)(2,1)S(1)} %row_sum.6), channel_id=1, source_target_pairs={{0,2},{1,5},{2,0},{3,7},{4,6},{5,1},{6,4},{7,3},{8,10},{9,13},{10,... | collective-permute-start | bytes 589832 | tf_op jit(solution)/shard_map/ppermute | solution.py:369
  14.4 2.4 %collective-permute-start.4 = (bf16[2,1,64,768]{3,2,1,0:T(8,128)(2,1)S(1)}, bf16[2,1,64,768]{3,2,1,0:T(8,128)(2,1)S(1)}, u32[]{:S(2)}, u32[]{:S(2)}) collective-permute-start(bf16[2,1,64,768]{3,2,1,0:T(8,128)(2,1)S(1)} %get-tuple-element.47), channel_id=1, source_target_pairs={{0,1},{1,0},{2,3},{3,2},{4,5},{5,4},{6,7},{7,6},{8,9},{9,8},{10,11... | collective-permute-start | bytes 589832 | tf_op jit(solution)/shard_map/ppermute | solution.py:274
  14.5 5.7 %collective-permute-start.3 = (bf16[2,1,64,768]{3,2,1,0:T(8,128)(2,1)S(1)}, bf16[2,1,64,768]{3,2,1,0:T(8,128)(2,1)S(1)}, u32[]{:S(2)}, u32[]{:S(2)}) collective-permute-start(bf16[2,1,64,768]{3,2,1,0:T(8,128)(2,1)S(1)} %row_sum.5), channel_id=1, source_target_pairs={{0,2},{1,5},{2,0},{3,7},{4,6},{5,1},{6,4},{7,3},{8,10},{9,13},{10,... | collective-permute-start | bytes 589832 | tf_op jit(solution)/shard_map/ppermute | solution.py:369
  16.0 4.3 %collective-permute-start.2 = (bf16[2,1,64,768]{3,2,1,0:T(8,128)(2,1)S(1)}, bf16[2,1,64,768]{3,2,1,0:T(8,128)(2,1)S(1)}, u32[]{:S(2)}, u32[]{:S(2)}) collective-permute-start(bf16[2,1,64,768]{3,2,1,0:T(8,128)(2,1)S(1)} %get-tuple-element.44), channel_id=1, source_target_pairs={{0,1},{1,0},{2,3},{3,2},{4,5},{5,4},{6,7},{7,6},{8,9},{9,8},{10,11... | collective-permute-start | bytes 589832 | tf_op jit(solution)/shard_map/ppermute | solution.py:274
  16.8 5.4 %collective-permute-start.7 = (bf16[1,1,64,768]{3,2,1,0:T(8,128)(2,1)S(1)}, bf16[1,1,64,768]{3,2,1,0:T(8,128)(2,1)S(1)}, u32[]{:S(2)}, u32[]{:S(2)}) collective-permute-start(bf16[1,1,64,768]{3,2,1,0:T(8,128)(2,1)S(1)} %row_sum.8), channel_id=1, source_target_pairs={{0,4},{1,9},{2,6},{3,11},{4,0},{5,13},{6,2},{7,15},{8,12},{9,1},{1... | collective-permute-start | bytes 294920 | tf_op jit(solution)/shard_map/ppermute | solution.py:369
  19.5 6.2 %collective-permute-start.6 = (bf16[1,1,64,768]{3,2,1,0:T(8,128)(2,1)S(1)}, bf16[1,1,64,768]{3,2,1,0:T(8,128)(2,1)S(1)}, u32[]{:S(2)}, u32[]{:S(2)}) collective-permute-start(bf16[1,1,64,768]{3,2,1,0:T(8,128)(2,1)S(1)} %row_sum.7), channel_id=1, source_target_pairs={{0,4},{1,9},{2,6},{3,11},{4,0},{5,13},{6,2},{7,15},{8,12},{9,1},{1... | collective-permute-start | bytes 294920 | tf_op jit(solution)/shard_map/ppermute | solution.py:369
  22.3 5.6 %collective-permute-start.8 = (bf16[1,1,64,768]{3,2,1,0:T(8,128)(2,1)S(1)}, bf16[1,1,64,768]{3,2,1,0:T(8,128)(2,1)S(1)}, u32[]{:S(2)}, u32[]{:S(2)}) collective-permute-start(bf16[1,1,64,768]{3,2,1,0:T(8,128)(2,1)S(1)} %row_sum.9), channel_id=1, source_target_pairs={{0,8},{1,3},{2,10},{3,1},{4,12},{5,7},{6,14},{7,5},{8,0},{9,11},{1... | collective-permute-start | bytes 294920 | tf_op jit(solution)/shard_map/ppermute | solution.py:369

commit v7 on v6

--- a/solution.py
+++ b/solution.py
@@ -65,7 +65,7 @@
 def block_in(t, i, over, core):
     first, second, third = 1 - t // 2, i // 2, i % 2
     owner = core if t % 2 else 1 - core
-    return (first + 2 * second + 4 * third + owner * (first + 2 * second - 3 * third)) ^ over
+    return (first + 4 * second + 2 * third + owner * (first - 3 * second + 2 * third)) ^ over
 
 
 def set_words(tiles, pos_ref, word):
@@ -365,7 +365,7 @@
         )(*arrays)
 
     def passed_on(value, stage):
-        bits = (axes[stage], axes[(stage + 1) % 3])
+        bits = (axes[(0, 2, 1)[stage]], axes[(1, 0, 2)[stage]])
         return lax.ppermute(value, "label", [(i, i ^ bits[i % 2]) for i in range(n_label)])
 
     far_got = passed_on(summed_at((first_keep, slice(2, 4)), (first_got, slice(2, 4))), 0)

time: 29 us -> 30.5 us (1.052)
  starting transfers between devices: 11 us -> 12.5 us
    ppermute x5, starting transfers between devices: 7.53 us -> 8.95 us  [passed_on(): lax.ppermute(value, 'label', [(i, i ^ bits[i % 2]) for i in range(n_label)])]
    ppermute x5, waiting for transfers between devices: 4.68 us -> 5.52 us  [passed_on(): lax.ppermute(value, 'label', [(i, i ^ bits[i % 2]) for i in range(n_label)])]
    ppermute x4, waiting for transfers between devices: 1.73 us -> 0.99 us  [swapped(): return lax.ppermute(value, axis, [(i, i ^ bit) for i in range(size)])]
  transfers between devices with their start and end apart: 9 -> 9, of which waited for: 6 -> 6; matrix products, arithmetic and copies ran while one was open for 0% -> 0% of each run, Pallas kernels for 18% -> 17%
where the time goes in v7:
time: 30.5 us; the launch traced here: 30.3 us
  starting transfers between devices  12.5 us (41%)
  Pallas kernels  10.6 us (35%)
  waiting for transfers between devices  6.51 us (21%)
  between operations  0.72 us (2%)
    ppermute x5, starting transfers between devices, passed_on(): lax.ppermute(value, 'label', [(i, i ^ bits[i % 2]) for i in range(n_label)])  8.95 us
    ppermute x5, waiting for transfers between devices, passed_on(): lax.ppermute(value, 'label', [(i, i ^ bits[i % 2]) for i in range(n_label)])  5.52 us
    pallas_call x1, Pallas kernels, on_device(): pl.pallas_call(functools.partial(send_kernel, n_label), out_shape=[shape(...  4.48 us
    ppermute x4, starting transfers between devices, swapped(): return lax.ppermute(value, axis, [(i, i ^ bit) for i in range(size)])  3.51 us
    pallas_call x2, Pallas kernels, tile_rows(): pl.pallas_call(functools.partial(rows_kernel, t), out_shape=[tile_shape,...  2.15 us
    pallas_call x1, Pallas kernels, on_device(): pl.pallas_call(last_rows_kernel, out_shape=[part_shape] * 2 + [row_shape,...  1.71 us
    ppermute x4, waiting for transfers between devices, swapped(): return lax.ppermute(value, axis, [(i, i ^ bit) for i in range(size)])  0.99 us
    pallas_call x1, Pallas kernels, on_device(): pl.pallas_call(keep_kernel, out_shape=shape((half_rows, features), BF16),...  0.98 us
  transfers between devices with their start and end apart: 9, of which 6 were waited for; matrix products, arithmetic and copies ran while one was open for 0% of the time, Pallas kernels for 17%

profile of v7, /device:TPU:0, one launch (start us, length us, event | category | flops | bytes accessed | tf_op | source)
XLA Modules:
  0.0 30.3 jit_solution(4963575129405960440)
XLA Ops:
  0.6 4.5 %send_half.1 = (bf16[1024,768]{1,0:T(8,128)(2,1)S(1)}, bf16[1024,768]{1,0:T(8,128)(2,1)S(1)}, s16[128,1024]{1,0:T(8,128)(2,1)S(1)}, bf16[2,4,8,128]{3,2,1,0:T(8,...) custom-call(bf16[1024,768]{1,0:T(8,128)(2,1)} %embed_hbm.1, ...), custom_call_target="tpu_custom_call" | custom-call | flops 1610612736 | tf_op jit(solution)/shard_map/send_half/pallas_call | solution.py:305
  5.1 3.0 %collective-permute-start.1 = (bf16[512,768]{1,0:T(8,128)(2,1)S(1)}, bf16[512,768]{1,0:T(8,128)(2,1)S(1)}, u32[]{:S(2)}, u32[]{:S(2)}) collective-permute-start(bf16[512,768]{1,0:T(8,128)(2,1)S(1)} %get-tuple-element.42), channel_id=1, source_target_pairs={{0,16},{16,0},{1,17},{17,1},{2,18},{18,2},{3,19},{19,3},{4,20},{20... | collective-permute-start | bytes 2359304 | tf_op jit(solution)/shard_map/ppermute | solution.py:274
  8.1 1.1 %first_rows.1 = (bf16[512,256]{1,0:T(8,128)(2,1)S(1)}, bf16[4,1,64,768]{3,2,1,0:T(8,128)(2,1)S(1)}) custom-call(bf16[1024,768]{1,0:T(8,128)(2,1)S(1)} %get-tuple-element.34.embed, bf16[1024,768]{1,0:T(8,128)(2,1)S(1)} %get-tuple-element.35.w, s16[128,1024]{1,0:T(8,128)(2,1)S(1)} %get-tuple-element.36.word, ...), custom_call_target="tpu_custom_call" | custom-call | tf_op jit(solution)/shard_map/first_rows/pallas_call | solution.py:336
  9.2 0.1 collective-permute-start
  9.3 1.1 %keep_rows.1 = (bf16[512,256]{1,0:T(8,128)(2,1)S(1)}, bf16[4,1,64,768]{3,2,1,0:T(8,128)(2,1)S(1)}) custom-call(bf16[1024,768]{1,0:T(8,128)(2,1)S(1)} %get-tuple-element.34.embed, bf16[1024,768]{1,0:T(8,128)(2,1)S(1)} %get-tuple-element.35.w, s16[128,1024]{1,0:T(8,128)(2,1)S(1)} %get-tuple-element.36.word, bf16[2,4,8,128]{3,2,1,0:T(8,128)(2,1)S(1)} %get-tuple-element.37.mask, ...), custom_call_target="tpu_custom_call" | custom-call | tf_op jit(solution)/shard_map/keep_rows/pallas_call | solution.py:336
  10.4 0.6 %collective-permute-done.refs_1_ = bf16[4,1,64,768]{3,2,1,0:T(8,128)(2,1)S(1)} collective-permute-done((bf16[4,1,64,768]{3,2,1,0:T(8,128)(2,1)S(1)}, bf16[4,1,64,768]{3,2,1,0:T(8,128)(2,1)S(1)}, u32[]{:S(2)}, u32[]{:S(2)}) %collective-permute-start) | collective-permute-done | bytes 393248 | tf_op jit(solution)/shard_map/ppermute | solution.py:274
  11.1 1.6 %collective-permute-start.5 = (bf16[2,1,64,768]{3,2,1,0:T(8,128)(2,1)S(1)}, bf16[2,1,64,768]{3,2,1,0:T(8,128)(2,1)S(1)}, u32[]{:S(2)}, u32[]{:S(2)}) collective-permute-start(bf16[2,1,64,768]{3,2,1,0:T(8,128)(2,1)S(1)} %row_sum.6), channel_id=1, source_target_pairs={{0,2},{1,5},{2,0},{3,7},{4,6},{5,1},{6,4},{7,3},{8,10},{9,13},{10,... | collective-permute-start | bytes 589832 | tf_op jit(solution)/shard_map/ppermute | solution.py:369
  12.6 1.7 %last_rows.1 = (bf16[2,1,64,768]{3,2,1,0:T(8,128)(2,1)S(1)}, bf16[2,1,64,768]{3,2,1,0:T(8,128)(2,1)S(1)}, bf16[4,1,64,768]{3,2,1,0:T(8,128)(2,1)S(1)}, bf16[512,256]{1,0:T(8,128)(2,1)S(1)}, bf16[512,256]{1,0:T(8,128)(2,1)S(1)}) custom-call(bf16[1024,768]{1,0:T(8,128)(2,1)S(1)} %get-tuple-element.34.embed, bf16[1024,768]{1,0:T(8,128)(2,1)S(1)} %get-tuple-element.35.w, ...), custom_call_target="tpu_custom_call" | custom-call | tf_op jit(solution)/shard_map/last_rows/pallas_call | solution.py:375
  14.4 0.1 collective-permute-start.4
  14.5 1.5 %collective-permute-start.3 = (bf16[2,1,64,768]{3,2,1,0:T(8,128)(2,1)S(1)}, bf16[2,1,64,768]{3,2,1,0:T(8,128)(2,1)S(1)}, u32[]{:S(2)}, u32[]{:S(2)}) collective-permute-start(bf16[2,1,64,768]{3,2,1,0:T(8,128)(2,1)S(1)} %row_sum.5), channel_id=1, source_target_pairs={{0,2},{1,5},{2,0},{3,7},{4,6},{5,1},{6,4},{7,3},{8,10},{9,13},{10,... | collective-permute-start | bytes 589832 | tf_op jit(solution)/shard_map/ppermute | solution.py:369
  16.0 0.4 %collective-permute-start.2 = (bf16[2,1,64,768]{3,2,1,0:T(8,128)(2,1)S(1)}, bf16[2,1,64,768]{3,2,1,0:T(8,128)(2,1)S(1)}, u32[]{:S(2)}, u32[]{:S(2)}) collective-permute-start(bf16[2,1,64,768]{3,2,1,0:T(8,128)(2,1)S(1)} %get-tuple-element.44), channel_id=1, source_target_pairs={{0,1},{1,0},{2,3},{3,2},{4,5},{5,4},{6,7},{7,6},{8,9},{9,8},{10,11... | collective-permute-start | bytes 589832 | tf_op jit(solution)/shard_map/ppermute | solution.py:274
  16.3 0.4 %collective-permute-done.5.refs_2_ = bf16[2,1,64,768]{3,2,1,0:T(8,128)(2,1)S(1)} collective-permute-done((bf16[2,1,64,768]{3,2,1,0:T(8,128)(2,1)S(1)}, bf16[2,1,64,768]{3,2,1,0:T(8,128)(2,1)S(1)}, u32[]{:S(2)}, u32[]{:S(2)}) %collective-permute-start.5) | collective-permute-done | bytes 196640 | tf_op jit(solution)/shard_map/ppermute | solution.py:369
  16.8 0.0 collective-permute-done.4.refs_1_
  16.8 2.6 %collective-permute-start.7 = (bf16[1,1,64,768]{3,2,1,0:T(8,128)(2,1)S(1)}, bf16[1,1,64,768]{3,2,1,0:T(8,128)(2,1)S(1)}, u32[]{:S(2)}, u32[]{:S(2)}) collective-permute-start(bf16[1,1,64,768]{3,2,1,0:T(8,128)(2,1)S(1)} %row_sum.8), channel_id=1, source_target_pairs={{0,8},{1,3},{2,10},{3,1},{4,12},{5,7},{6,14},{7,5},{8,0},{9,11},{1... | collective-permute-start | bytes 294920 | tf_op jit(solution)/shard_map/ppermute | solution.py:369
  19.5 1.0 %keep_half.1.kept = bf16[512,768]{1,0:T(8,128)(2,1)S(1)} custom-call(bf16[1024,768]{1,0:T(8,128)(2,1)S(1)} %get-tuple-element.34.embed, bf16[512,256]{1,0:T(8,128)(2,1)S(1)} %get-tuple-element.31.refs_0_, bf16[512,256]{1,0:T(8,128)(2,1)S(1)} %get-tuple-element.32.refs_1_, bf16[512,256]{1,0:T(8,128)(2,1)S(1)} %get-tuple-element.40.refs_2_, ...), custom_call_target="tpu_custom_call" | custom-call | tf_op jit(solution)/shard_map/keep_half/pallas_call | solution.py:404
  20.5 0.4 %collective-permute-start.6 = (bf16[1,1,64,768]{3,2,1,0:T(8,128)(2,1)S(1)}, bf16[1,1,64,768]{3,2,1,0:T(8,128)(2,1)S(1)}, u32[]{:S(2)}, u32[]{:S(2)}) collective-permute-start(bf16[1,1,64,768]{3,2,1,0:T(8,128)(2,1)S(1)} %row_sum.7), channel_id=1, source_target_pairs={{0,8},{1,3},{2,10},{3,1},{4,12},{5,7},{6,14},{7,5},{8,0},{9,11},{1... | collective-permute-start | bytes 294920 | tf_op jit(solution)/shard_map/ppermute | solution.py:369
  20.9 0.3 %collective-permute-done.3.refs_2_ = bf16[2,1,64,768]{3,2,1,0:T(8,128)(2,1)S(1)} collective-permute-done((bf16[2,1,64,768]{3,2,1,0:T(8,128)(2,1)S(1)}, bf16[2,1,64,768]{3,2,1,0:T(8,128)(2,1)S(1)}, u32[]{:S(2)}, u32[]{:S(2)}) %collective-permute-start.3) | collective-permute-done | bytes 196640 | tf_op jit(solution)/shard_map/ppermute | solution.py:369
  21.2 0.0 collective-permute-done.2.refs_1_
  21.2 1.2 %collective-permute-done.7.refs_3_ = bf16[1,1,64,768]{3,2,1,0:T(8,128)(2,1)S(1)} collective-permute-done((bf16[1,1,64,768]{3,2,1,0:T(8,128)(2,1)S(1)}, bf16[1,1,64,768]{3,2,1,0:T(8,128)(2,1)S(1)}, u32[]{:S(2)}, u32[]{:S(2)}) %collective-permute-start.7) | collective-permute-done | bytes 98336 | tf_op jit(solution)/shard_map/ppermute | solution.py:369
  22.4 0.1 row_sum.9
  22.5 2.8 %collective-permute-start.8 = (bf16[1,1,64,768]{3,2,1,0:T(8,128)(2,1)S(1)}, bf16[1,1,64,768]{3,2,1,0:T(8,128)(2,1)S(1)}, u32[]{:S(2)}, u32[]{:S(2)}) collective-permute-start(bf16[1,1,64,768]{3,2,1,0:T(8,128)(2,1)S(1)} %row_sum.9), channel_id=1, source_target_pairs={{0,4},{1,9},{2,6},{3,11},{4,0},{5,13},{6,2},{7,15},{8,12},{9,1},{1... | collective-permute-start | bytes 294920 | tf_op jit(solution)/shard_map/ppermute | solution.py:369
  25.3 0.4 %collective-permute-done.1.got = bf16[512,768]{1,0:T(8,128)(2,1)S(1)} collective-permute-done((bf16[512,768]{1,0:T(8,128)(2,1)S(1)}, bf16[512,768]{1,0:T(8,128)(2,1)S(1)}, u32[]{:S(2)}, u32[]{:S(2)}) %collective-permute-start.1) | collective-permute-done | bytes 786464 | tf_op jit(solution)/shard_map/ppermute | solution.py:274
  25.7 0.1 half_sum.1.summed
  25.8 3.6 %collective-permute-done.6.refs_3_ = bf16[1,1,64,768]{3,2,1,0:T(8,128)(2,1)S(1)} collective-permute-done((bf16[1,1,64,768]{3,2,1,0:T(8,128)(2,1)S(1)}, bf16[1,1,64,768]{3,2,1,0:T(8,128)(2,1)S(1)}, u32[]{:S(2)}, u32[]{:S(2)}) %collective-permute-start.6) | collective-permute-done | bytes 98336 | tf_op jit(solution)/shard_map/ppermute | solution.py:369
  29.3 0.0 collective-permute-done.8.refs_4_
  29.4 0.9 %finish.1 = (bf16[64,768]{1,0:T(8,128)(2,1)}, bf16[512,768]{1,0:T(8,128)(2,1)}) custom-call(bf16[512,768]{1,0:T(8,128)(2,1)S(1)} %keep_half.1.kept, bf16[512,768]{1,0:T(8,128)(2,1)S(1)} %collective-permute-done.1.got, bf16[256,768]{1,0:T(8,128)(2,1)S(1)} %half_sum.1.summed, bf16[4,1,64,768]{3,2,1,0:T(8,128)(2,1)S(1)} %get-tuple-element.43.refs_0_, ...), custom_call_target="tpu_custom_call" | custom-call | tf_op jit(solution)/shard_map/finish/pallas_call | solution.py:436
  (4 shorter events, 0.2 us)
Async XLA Ops:
  5.1 20.5 %collective-permute-start.1 = (bf16[512,768]{1,0:T(8,128)(2,1)S(1)}, bf16[512,768]{1,0:T(8,128)(2,1)S(1)}, u32[]{:S(2)}, u32[]{:S(2)}) collective-permute-start(bf16[512,768]{1,0:T(8,128)(2,1)S(1)} %get-tuple-element.42), channel_id=1, source_target_pairs={{0,16},{16,0},{1,17},{17,1},{2,18},{18,2},{3,19},{19,3},{4,20},{20... | collective-permute-start | bytes 2359304 | tf_op jit(solution)/shard_map/ppermute | solution.py:274
  9.2 1.8 %collective-permute-start = (bf16[4,1,64,768]{3,2,1,0:T(8,128)(2,1)S(1)}, bf16[4,1,64,768]{3,2,1,0:T(8,128)(2,1)S(1)}, u32[]{:S(2)}, u32[]{:S(2)}) collective-permute-start(bf16[4,1,64,768]{3,2,1,0:T(8,128)(2,1)S(1)} %get-tuple-element.33), channel_id=1, source_target_pairs={{0,1},{1,0},{2,3},{3,2},{4,5},{5,4},{6,7},{7,6},{8,9},{9,8},{10,11... | collective-permute-start | bytes 1179656 | tf_op jit(solution)/shard_map/ppermute | solution.py:274
  11.1 5.7 %collective-permute-start.5 = (bf16[2,1,64,768]{3,2,1,0:T(8,128)(2,1)S(1)}, bf16[2,1,64,768]{3,2,1,0:T(8,128)(2,1)S(1)}, u32[]{:S(2)}, u32[]{:S(2)}) collective-permute-start(bf16[2,1,64,768]{3,2,1,0:T(8,128)(2,1)S(1)} %row_sum.6), channel_id=1, source_target_pairs={{0,2},{1,5},{2,0},{3,7},{4,6},{5,1},{6,4},{7,3},{8,10},{9,13},{10,... | collective-permute-start | bytes 589832 | tf_op jit(solution)/shard_map/ppermute | solution.py:369
  14.4 2.4 %collective-permute-start.4 = (bf16[2,1,64,768]{3,2,1,0:T(8,128)(2,1)S(1)}, bf16[2,1,64,768]{3,2,1,0:T(8,128)(2,1)S(1)}, u32[]{:S(2)}, u32[]{:S(2)}) collective-permute-start(bf16[2,1,64,768]{3,2,1,0:T(8,128)(2,1)S(1)} %get-tuple-element.47), channel_id=1, source_target_pairs={{0,1},{1,0},{2,3},{3,2},{4,5},{5,4},{6,7},{7,6},{8,9},{9,8},{10,11... | collective-permute-start | bytes 589832 | tf_op jit(solution)/shard_map/ppermute | solution.py:274
  14.5 6.8 %collective-permute-start.3 = (bf16[2,1,64,768]{3,2,1,0:T(8,128)(2,1)S(1)}, bf16[2,1,64,768]{3,2,1,0:T(8,128)(2,1)S(1)}, u32[]{:S(2)}, u32[]{:S(2)}) collective-permute-start(bf16[2,1,64,768]{3,2,1,0:T(8,128)(2,1)S(1)} %row_sum.5), channel_id=1, source_target_pairs={{0,2},{1,5},{2,0},{3,7},{4,6},{5,1},{6,4},{7,3},{8,10},{9,13},{10,... | collective-permute-start | bytes 589832 | tf_op jit(solution)/shard_map/ppermute | solution.py:369
  16.0 5.3 %collective-permute-start.2 = (bf16[2,1,64,768]{3,2,1,0:T(8,128)(2,1)S(1)}, bf16[2,1,64,768]{3,2,1,0:T(8,128)(2,1)S(1)}, u32[]{:S(2)}, u32[]{:S(2)}) collective-permute-start(bf16[2,1,64,768]{3,2,1,0:T(8,128)(2,1)S(1)} %get-tuple-element.44), channel_id=1, source_target_pairs={{0,1},{1,0},{2,3},{3,2},{4,5},{5,4},{6,7},{7,6},{8,9},{9,8},{10,11... | collective-permute-start | bytes 589832 | tf_op jit(solution)/shard_map/ppermute | solution.py:274
  16.8 5.6 %collective-permute-start.7 = (bf16[1,1,64,768]{3,2,1,0:T(8,128)(2,1)S(1)}, bf16[1,1,64,768]{3,2,1,0:T(8,128)(2,1)S(1)}, u32[]{:S(2)}, u32[]{:S(2)}) collective-permute-start(bf16[1,1,64,768]{3,2,1,0:T(8,128)(2,1)S(1)} %row_sum.8), channel_id=1, source_target_pairs={{0,8},{1,3},{2,10},{3,1},{4,12},{5,7},{6,14},{7,5},{8,0},{9,11},{1... | collective-permute-start | bytes 294920 | tf_op jit(solution)/shard_map/ppermute | solution.py:369
  20.5 8.8 %collective-permute-start.6 = (bf16[1,1,64,768]{3,2,1,0:T(8,128)(2,1)S(1)}, bf16[1,1,64,768]{3,2,1,0:T(8,128)(2,1)S(1)}, u32[]{:S(2)}, u32[]{:S(2)}) collective-permute-start(bf16[1,1,64,768]{3,2,1,0:T(8,128)(2,1)S(1)} %row_sum.7), channel_id=1, source_target_pairs={{0,8},{1,3},{2,10},{3,1},{4,12},{5,7},{6,14},{7,5},{8,0},{9,11},{1... | collective-permute-start | bytes 294920 | tf_op jit(solution)/shard_map/ppermute | solution.py:369
  22.5 6.9 %collective-permute-start.8 = (bf16[1,1,64,768]{3,2,1,0:T(8,128)(2,1)S(1)}, bf16[1,1,64,768]{3,2,1,0:T(8,128)(2,1)S(1)}, u32[]{:S(2)}, u32[]{:S(2)}) collective-permute-start(bf16[1,1,64,768]{3,2,1,0:T(8,128)(2,1)S(1)} %row_sum.9), channel_id=1, source_target_pairs={{0,4},{1,9},{2,6},{3,11},{4,0},{5,13},{6,2},{7,15},{8,12},{9,1},{1... | collective-permute-start | bytes 294920 | tf_op jit(solution)/shard_map/ppermute | solution.py:369

commit v8 on v5

--- a/solution.py
+++ b/solution.py
@@ -125,12 +125,10 @@
                         sems.at[5 + at],
                     )
                 )
-    for copy in (*small, *e_copies[0], *w_copies):
+    for copy in (*small, *e_copies[0], *w_copies, *e_copies[1], *e_copies[2], *e_copies[3]):
         copy.start()
     for copy in small:
         copy.wait()
-    for copy in (*e_copies[1], *e_copies[2], *e_copies[3]):
-        copy.start()
 
     lane = lax.broadcasted_iota(jnp.int32, (BLOCKS, INST_BLOCK), 1)
     low = lane < INST_BLOCK // 2

time: 28 us -> 28 us (level)
  no operation moved by 1% of the time
where the time goes in v8:
time: 28 us; the launch traced here: 27.8 us
  starting transfers between devices  11 us (39%)
  Pallas kernels  9.86 us (35%)
  waiting for transfers between devices  6.24 us (22%)
  between operations  0.73 us (3%)
    ppermute x5, starting transfers between devices, passed_on(): lax.ppermute(value, 'label', [(i, i ^ bits[i % 2]) for i in range(n_label)])  7.53 us
    ppermute x4, waiting for transfers between devices, swapped(): return lax.ppermute(value, axis, [(i, i ^ bit) for i in range(size)])  3.55 us
    ppermute x4, starting transfers between devices, swapped(): return lax.ppermute(value, axis, [(i, i ^ bit) for i in range(size)])  3.45 us
    pallas_call x1, Pallas kernels, on_device(): pl.pallas_call(functools.partial(first_kernel, n_label), out_shape=[shape...  3.18 us
    ppermute x5, waiting for transfers between devices, passed_on(): lax.ppermute(value, 'label', [(i, i ^ bits[i % 2]) for i in range(n_label)])  2.69 us
    pallas_call x1, Pallas kernels, on_device(): pl.pallas_call(last_rows_kernel, out_shape=[part_shape] * 2 + [row_shape,...  1.71 us
    pallas_call x1, Pallas kernels, on_device(): pl.pallas_call(label_kernel, out_shape=[shape((CLUSTER, rows), jnp.int16)...  1.64 us
    pallas_call x1, Pallas kernels, on_device(): pl.pallas_call(keep_rows_kernel, out_shape=[tile_shape, row_shape], in_sp...  1.08 us
  transfers between devices with their start and end apart: 9, of which 4 were waited for; matrix products, arithmetic and copies ran while one was open for 0% of the time, Pallas kernels for 21%

profile of v8, /device:TPU:0, one launch (start us, length us, event | category | flops | bytes accessed | tf_op | source)
XLA Modules:
  0.0 27.8 jit_solution(8948273006760493131)
XLA Ops:
  0.6 3.2 %first_rows.1 = (bf16[1024,768]{1,0:T(8,128)(2,1)S(1)}, bf16[1024,768]{1,0:T(8,128)(2,1)S(1)}, s32[8,1024]{1,0:T(8,128)S(1)}, bf16[2,4,8,128]{3,2,1,0:T(8,128)(2...) custom-call(bf16[1024,768]{1,0:T(8,128)(2,1)} %embed_hbm.1, ...), custom_call_target="tpu_custom_call" | custom-call | flops 1610612736 | tf_op jit(solution)/shard_map/first_rows/pallas_call | solution.py:320
  3.8 0.5 %collective-permute-start = (bf16[4,1,64,768]{3,2,1,0:T(8,128)(2,1)S(1)}, bf16[4,1,64,768]{3,2,1,0:T(8,128)(2,1)S(1)}, u32[]{:S(2)}, u32[]{:S(2)}) collective-permute-start(bf16[4,1,64,768]{3,2,1,0:T(8,128)(2,1)S(1)} %get-tuple-element.29), channel_id=1, source_target_pairs={{0,1},{1,0},{2,3},{3,2},{4,5},{5,4},{6,7},{7,6},{8,9},{9,8},{10,11... | collective-permute-start | bytes 1179656 | tf_op jit(solution)/shard_map/ppermute | solution.py:289
  4.3 1.6 %send_half.1 = (s16[128,1024]{1,0:T(8,128)(2,1)S(1)}, bf16[512,768]{1,0:T(8,128)(2,1)S(1)}, bf16[512,768]{1,0:T(8,128)(2,1)S(1)}) custom-call(bf16[1024,768]{1,0:T(8,128)(2,1)S(1)} %get-tuple-element.37.embed, bf16[1024,768]{1,0:T(8,128)(2,1)S(1)} %get-tuple-element.38.w, s32[8,1024]{1,0:T(8,128)S(1)} %get-tuple-element.31.pos, ...), custom_call_target="tpu_custom_call" | custom-call | tf_op jit(solution)/shard_map/send_half/pallas_call | solution.py:351
  6.0 2.6 %collective-permute-start.1 = (bf16[512,768]{1,0:T(8,128)(2,1)S(1)}, bf16[512,768]{1,0:T(8,128)(2,1)S(1)}, u32[]{:S(2)}, u32[]{:S(2)}) collective-permute-start(bf16[512,768]{1,0:T(8,128)(2,1)S(1)} %get-tuple-element.46), channel_id=1, source_target_pairs={{0,16},{16,0},{1,17},{17,1},{2,18},{18,2},{3,19},{19,3},{4,20},{20... | collective-permute-start | bytes 2359304 | tf_op jit(solution)/shard_map/ppermute | solution.py:289
  8.6 0.0 collective-permute-done.refs_1_
  8.6 1.1 %keep_rows.1 = (bf16[512,256]{1,0:T(8,128)(2,1)S(1)}, bf16[4,1,64,768]{3,2,1,0:T(8,128)(2,1)S(1)}) custom-call(bf16[1024,768]{1,0:T(8,128)(2,1)S(1)} %get-tuple-element.37.embed, bf16[1024,768]{1,0:T(8,128)(2,1)S(1)} %get-tuple-element.38.w, s16[128,1024]{1,0:T(8,128)(2,1)S(1)} %get-tuple-element.39.word, bf16[2,4,8,128]{3,2,1,0:T(8,128)(2,1)S(1)} %get-tuple-element.40.mask, ...), custom_call_target="tpu_custom_call" | custom-call | tf_op jit(solution)/shard_map/keep_rows/pallas_call | solution.py:371
  9.7 1.6 %collective-permute-start.5 = (bf16[2,1,64,768]{3,2,1,0:T(8,128)(2,1)S(1)}, bf16[2,1,64,768]{3,2,1,0:T(8,128)(2,1)S(1)}, u32[]{:S(2)}, u32[]{:S(2)}) collective-permute-start(bf16[2,1,64,768]{3,2,1,0:T(8,128)(2,1)S(1)} %row_sum.6), channel_id=1, source_target_pairs={{0,2},{1,5},{2,0},{3,7},{4,6},{5,1},{6,4},{7,3},{8,10},{9,13},{10,... | collective-permute-start | bytes 589832 | tf_op jit(solution)/shard_map/ppermute | solution.py:399
  11.3 1.7 %last_rows.1 = (bf16[2,1,64,768]{3,2,1,0:T(8,128)(2,1)S(1)}, bf16[2,1,64,768]{3,2,1,0:T(8,128)(2,1)S(1)}, bf16[4,1,64,768]{3,2,1,0:T(8,128)(2,1)S(1)}, bf16[512,256]{1,0:T(8,128)(2,1)S(1)}, bf16[512,256]{1,0:T(8,128)(2,1)S(1)}) custom-call(bf16[1024,768]{1,0:T(8,128)(2,1)S(1)} %get-tuple-element.37.embed, bf16[1024,768]{1,0:T(8,128)(2,1)S(1)} %get-tuple-element.38.w, ...), custom_call_target="tpu_custom_call" | custom-call | flops 1610612736 | tf_op jit(solution)/shard_map/last_rows/pallas_call | solution.py:405
  13.0 0.1 collective-permute-start.4
  13.1 1.6 %collective-permute-start.3 = (bf16[2,1,64,768]{3,2,1,0:T(8,128)(2,1)S(1)}, bf16[2,1,64,768]{3,2,1,0:T(8,128)(2,1)S(1)}, u32[]{:S(2)}, u32[]{:S(2)}) collective-permute-start(bf16[2,1,64,768]{3,2,1,0:T(8,128)(2,1)S(1)} %row_sum.5), channel_id=1, source_target_pairs={{0,2},{1,5},{2,0},{3,7},{4,6},{5,1},{6,4},{7,3},{8,10},{9,13},{10,... | collective-permute-start | bytes 589832 | tf_op jit(solution)/shard_map/ppermute | solution.py:399
  14.7 0.3 %collective-permute-start.2 = (bf16[2,1,64,768]{3,2,1,0:T(8,128)(2,1)S(1)}, bf16[2,1,64,768]{3,2,1,0:T(8,128)(2,1)S(1)}, u32[]{:S(2)}, u32[]{:S(2)}) collective-permute-start(bf16[2,1,64,768]{3,2,1,0:T(8,128)(2,1)S(1)} %get-tuple-element.48), channel_id=1, source_target_pairs={{0,1},{1,0},{2,3},{3,2},{4,5},{5,4},{6,7},{7,6},{8,9},{9,8},{10,11... | collective-permute-start | bytes 589832 | tf_op jit(solution)/shard_map/ppermute | solution.py:289
  15.0 0.4 %collective-permute-done.5.refs_2_ = bf16[2,1,64,768]{3,2,1,0:T(8,128)(2,1)S(1)} collective-permute-done((bf16[2,1,64,768]{3,2,1,0:T(8,128)(2,1)S(1)}, bf16[2,1,64,768]{3,2,1,0:T(8,128)(2,1)S(1)}, u32[]{:S(2)}, u32[]{:S(2)}) %collective-permute-start.5) | collective-permute-done | bytes 196640 | tf_op jit(solution)/shard_map/ppermute | solution.py:399
  15.4 0.0 collective-permute-done.4.refs_1_
  15.5 1.6 %collective-permute-start.7 = (bf16[1,1,64,768]{3,2,1,0:T(8,128)(2,1)S(1)}, bf16[1,1,64,768]{3,2,1,0:T(8,128)(2,1)S(1)}, u32[]{:S(2)}, u32[]{:S(2)}) collective-permute-start(bf16[1,1,64,768]{3,2,1,0:T(8,128)(2,1)S(1)} %row_sum.8), channel_id=1, source_target_pairs={{0,4},{1,9},{2,6},{3,11},{4,0},{5,13},{6,2},{7,15},{8,12},{9,1},{1... | collective-permute-start | bytes 294920 | tf_op jit(solution)/shard_map/ppermute | solution.py:399
  17.1 1.0 %keep_half.1.kept = bf16[512,768]{1,0:T(8,128)(2,1)S(1)} custom-call(bf16[1024,768]{1,0:T(8,128)(2,1)S(1)} %get-tuple-element.37.embed, bf16[512,256]{1,0:T(8,128)(2,1)S(1)} %get-tuple-element.28.refs_0_, bf16[512,256]{1,0:T(8,128)(2,1)S(1)} %get-tuple-element.43.refs_1_, bf16[512,256]{1,0:T(8,128)(2,1)S(1)} %get-tuple-element.44.refs_2_, ...), custom_call_target="tpu_custom_call" | custom-call | tf_op jit(solution)/shard_map/keep_half/pallas_call | solution.py:434
  18.2 0.5 %collective-permute-start.6 = (bf16[1,1,64,768]{3,2,1,0:T(8,128)(2,1)S(1)}, bf16[1,1,64,768]{3,2,1,0:T(8,128)(2,1)S(1)}, u32[]{:S(2)}, u32[]{:S(2)}) collective-permute-start(bf16[1,1,64,768]{3,2,1,0:T(8,128)(2,1)S(1)} %row_sum.7), channel_id=1, source_target_pairs={{0,4},{1,9},{2,6},{3,11},{4,0},{5,13},{6,2},{7,15},{8,12},{9,1},{1... | collective-permute-start | bytes 294920 | tf_op jit(solution)/shard_map/ppermute | solution.py:399
  18.7 0.2 collective-permute-done.3.refs_2_
  18.9 0.0 collective-permute-done.2.refs_1_
  18.9 2.1 %collective-permute-done.7.refs_3_ = bf16[1,1,64,768]{3,2,1,0:T(8,128)(2,1)S(1)} collective-permute-done((bf16[1,1,64,768]{3,2,1,0:T(8,128)(2,1)S(1)}, bf16[1,1,64,768]{3,2,1,0:T(8,128)(2,1)S(1)}, u32[]{:S(2)}, u32[]{:S(2)}) %collective-permute-start.7) | collective-permute-done | bytes 98336 | tf_op jit(solution)/shard_map/ppermute | solution.py:399
  20.9 0.1 row_sum.9
  21.0 2.2 %collective-permute-start.8 = (bf16[1,1,64,768]{3,2,1,0:T(8,128)(2,1)S(1)}, bf16[1,1,64,768]{3,2,1,0:T(8,128)(2,1)S(1)}, u32[]{:S(2)}, u32[]{:S(2)}) collective-permute-start(bf16[1,1,64,768]{3,2,1,0:T(8,128)(2,1)S(1)} %row_sum.9), channel_id=1, source_target_pairs={{0,8},{1,3},{2,10},{3,1},{4,12},{5,7},{6,14},{7,5},{8,0},{9,11},{1... | collective-permute-start | bytes 294920 | tf_op jit(solution)/shard_map/ppermute | solution.py:399
  23.2 3.5 %collective-permute-done.1.got = bf16[512,768]{1,0:T(8,128)(2,1)S(1)} collective-permute-done((bf16[512,768]{1,0:T(8,128)(2,1)S(1)}, bf16[512,768]{1,0:T(8,128)(2,1)S(1)}, u32[]{:S(2)}, u32[]{:S(2)}) %collective-permute-start.1) | collective-permute-done | bytes 786464 | tf_op jit(solution)/shard_map/ppermute | solution.py:289
  26.8 0.1 half_sum.1.summed
  26.8 0.0 collective-permute-done.6.refs_3_
  26.9 0.0 collective-permute-done.8.refs_4_
  26.9 0.9 %finish.1 = (bf16[64,768]{1,0:T(8,128)(2,1)}, bf16[512,768]{1,0:T(8,128)(2,1)}) custom-call(bf16[512,768]{1,0:T(8,128)(2,1)S(1)} %keep_half.1.kept, bf16[512,768]{1,0:T(8,128)(2,1)S(1)} %collective-permute-done.1.got, bf16[256,768]{1,0:T(8,128)(2,1)S(1)} %half_sum.1.summed, bf16[4,1,64,768]{3,2,1,0:T(8,128)(2,1)S(1)} %get-tuple-element.47.refs_0_, ...), custom_call_target="tpu_custom_call" | custom-call | tf_op jit(solution)/shard_map/finish/pallas_call | solution.py:466
  (4 shorter events, 0.2 us)
Async XLA Ops:
  3.8 4.7 %collective-permute-start = (bf16[4,1,64,768]{3,2,1,0:T(8,128)(2,1)S(1)}, bf16[4,1,64,768]{3,2,1,0:T(8,128)(2,1)S(1)}, u32[]{:S(2)}, u32[]{:S(2)}) collective-permute-start(bf16[4,1,64,768]{3,2,1,0:T(8,128)(2,1)S(1)} %get-tuple-element.29), channel_id=1, source_target_pairs={{0,1},{1,0},{2,3},{3,2},{4,5},{5,4},{6,7},{7,6},{8,9},{9,8},{10,11... | collective-permute-start | bytes 1179656 | tf_op jit(solution)/shard_map/ppermute | solution.py:289
  6.0 20.8 %collective-permute-start.1 = (bf16[512,768]{1,0:T(8,128)(2,1)S(1)}, bf16[512,768]{1,0:T(8,128)(2,1)S(1)}, u32[]{:S(2)}, u32[]{:S(2)}) collective-permute-start(bf16[512,768]{1,0:T(8,128)(2,1)S(1)} %get-tuple-element.46), channel_id=1, source_target_pairs={{0,16},{16,0},{1,17},{17,1},{2,18},{18,2},{3,19},{19,3},{4,20},{20... | collective-permute-start | bytes 2359304 | tf_op jit(solution)/shard_map/ppermute | solution.py:289
  9.7 5.7 %collective-permute-start.5 = (bf16[2,1,64,768]{3,2,1,0:T(8,128)(2,1)S(1)}, bf16[2,1,64,768]{3,2,1,0:T(8,128)(2,1)S(1)}, u32[]{:S(2)}, u32[]{:S(2)}) collective-permute-start(bf16[2,1,64,768]{3,2,1,0:T(8,128)(2,1)S(1)} %row_sum.6), channel_id=1, source_target_pairs={{0,2},{1,5},{2,0},{3,7},{4,6},{5,1},{6,4},{7,3},{8,10},{9,13},{10,... | collective-permute-start | bytes 589832 | tf_op jit(solution)/shard_map/ppermute | solution.py:399
  13.0 2.4 %collective-permute-start.4 = (bf16[2,1,64,768]{3,2,1,0:T(8,128)(2,1)S(1)}, bf16[2,1,64,768]{3,2,1,0:T(8,128)(2,1)S(1)}, u32[]{:S(2)}, u32[]{:S(2)}) collective-permute-start(bf16[2,1,64,768]{3,2,1,0:T(8,128)(2,1)S(1)} %get-tuple-element.51), channel_id=1, source_target_pairs={{0,1},{1,0},{2,3},{3,2},{4,5},{5,4},{6,7},{7,6},{8,9},{9,8},{10,11... | collective-permute-start | bytes 589832 | tf_op jit(solution)/shard_map/ppermute | solution.py:289
  13.1 5.7 %collective-permute-start.3 = (bf16[2,1,64,768]{3,2,1,0:T(8,128)(2,1)S(1)}, bf16[2,1,64,768]{3,2,1,0:T(8,128)(2,1)S(1)}, u32[]{:S(2)}, u32[]{:S(2)}) collective-permute-start(bf16[2,1,64,768]{3,2,1,0:T(8,128)(2,1)S(1)} %row_sum.5), channel_id=1, source_target_pairs={{0,2},{1,5},{2,0},{3,7},{4,6},{5,1},{6,4},{7,3},{8,10},{9,13},{10,... | collective-permute-start | bytes 589832 | tf_op jit(solution)/shard_map/ppermute | solution.py:399
  14.7 4.2 %collective-permute-start.2 = (bf16[2,1,64,768]{3,2,1,0:T(8,128)(2,1)S(1)}, bf16[2,1,64,768]{3,2,1,0:T(8,128)(2,1)S(1)}, u32[]{:S(2)}, u32[]{:S(2)}) collective-permute-start(bf16[2,1,64,768]{3,2,1,0:T(8,128)(2,1)S(1)} %get-tuple-element.48), channel_id=1, source_target_pairs={{0,1},{1,0},{2,3},{3,2},{4,5},{5,4},{6,7},{7,6},{8,9},{9,8},{10,11... | collective-permute-start | bytes 589832 | tf_op jit(solution)/shard_map/ppermute | solution.py:289
  15.5 5.4 %collective-permute-start.7 = (bf16[1,1,64,768]{3,2,1,0:T(8,128)(2,1)S(1)}, bf16[1,1,64,768]{3,2,1,0:T(8,128)(2,1)S(1)}, u32[]{:S(2)}, u32[]{:S(2)}) collective-permute-start(bf16[1,1,64,768]{3,2,1,0:T(8,128)(2,1)S(1)} %row_sum.8), channel_id=1, source_target_pairs={{0,4},{1,9},{2,6},{3,11},{4,0},{5,13},{6,2},{7,15},{8,12},{9,1},{1... | collective-permute-start | bytes 294920 | tf_op jit(solution)/shard_map/ppermute | solution.py:399
  18.2 8.7 %collective-permute-start.6 = (bf16[1,1,64,768]{3,2,1,0:T(8,128)(2,1)S(1)}, bf16[1,1,64,768]{3,2,1,0:T(8,128)(2,1)S(1)}, u32[]{:S(2)}, u32[]{:S(2)}) collective-permute-start(bf16[1,1,64,768]{3,2,1,0:T(8,128)(2,1)S(1)} %row_sum.7), channel_id=1, source_target_pairs={{0,4},{1,9},{2,6},{3,11},{4,0},{5,13},{6,2},{7,15},{8,12},{9,1},{1... | collective-permute-start | bytes 294920 | tf_op jit(solution)/shard_map/ppermute | solution.py:399
  21.0 5.9 %collective-permute-start.8 = (bf16[1,1,64,768]{3,2,1,0:T(8,128)(2,1)S(1)}, bf16[1,1,64,768]{3,2,1,0:T(8,128)(2,1)S(1)}, u32[]{:S(2)}, u32[]{:S(2)}) collective-permute-start(bf16[1,1,64,768]{3,2,1,0:T(8,128)(2,1)S(1)} %row_sum.9), channel_id=1, source_target_pairs={{0,8},{1,3},{2,10},{3,1},{4,12},{5,7},{6,14},{7,5},{8,0},{9,11},{1... | collective-permute-start | bytes 294920 | tf_op jit(solution)/shard_map/ppermute | solution.py:399

commit v9 on v8

--- a/solution.py
+++ b/solution.py
@@ -398,8 +398,7 @@
         bits = (axes[stage], axes[(stage + 1) % 3])
         return lax.ppermute(value, "label", [(i, i ^ bits[i % 2]) for i in range(n_label)])
 
-    far_got = passed_on(summed_at((first_keep, slice(2, 4)), (first_got, slice(2, 4))), 0)
-    near_got = passed_on(summed_at((first_keep, slice(0, 2)), (first_got, slice(0, 2))), 0)
+    first_got = passed_on(summed_at((first_keep, slice(0, 4)), (first_got, slice(0, 4))), 0)
 
     part_shape = shape((2, subs, piece, features), BF16)
     *last_send, last_keep, three_slopes_t, four_slopes_t = pl.pallas_call(
@@ -417,10 +416,10 @@
     )(*shared)
 
     last_got = [swapped(part, "label", n_label, 1) for part in last_send]
-    three_got = passed_on(summed_at((last_keep, slice(3, 4)), (last_got[1], slice(1, 2)), (far_got, slice(1, 2))), 1)
-    two_got = passed_on(summed_at((last_keep, slice(2, 3)), (last_got[1], slice(0, 1)), (far_got, slice(0, 1))), 1)
-    row_got = passed_on(summed_at((last_keep, slice(1, 2)), (last_got[0], slice(1, 2)), (near_got, slice(1, 2)), (three_got, slice(0, 1))), 2)
-    row_terms = [last_keep, last_got[0], near_got, two_got, row_got]
+    three_got = passed_on(summed_at((last_keep, slice(3, 4)), (last_got[1], slice(1, 2)), (first_got, slice(3, 4))), 1)
+    two_got = passed_on(summed_at((last_keep, slice(2, 3)), (last_got[1], slice(0, 1)), (first_got, slice(2, 3))), 1)
+    row_got = passed_on(summed_at((last_keep, slice(1, 2)), (last_got[0], slice(1, 2)), (first_got, slice(1, 2)), (three_got, slice(0, 1))), 2)
+    row_terms = [last_keep, last_got[0], first_got, two_got, row_got]
     bit = subs
     while bit > 1:
         row_sum = add(*(term.reshape(-1, subs, piece, features)[0] for term in row_terms[:-1]))

time: 28 us -> 29.4 us (1.050)
  waiting for transfers between devices: 6.24 us -> 8.95 us
  starting transfers between devices: 11 us -> 9.71 us
    ppermute x5 -> x4, waiting for transfers between devices: 2.69 us -> 6.28 us  [passed_on(): lax.ppermute(value, 'label', [(i, i ^ bits[i % 2]) for i in range(n_label)])]
    ppermute x5 -> x4, starting transfers between devices: 7.53 us -> 6.05 us  [passed_on(): lax.ppermute(value, 'label', [(i, i ^ bits[i % 2]) for i in range(n_label)])]
    ppermute x4, waiting for transfers between devices: 3.55 us -> 2.66 us  [swapped(): return lax.ppermute(value, axis, [(i, i ^ bit) for i in range(size)])]
  transfers between devices with their start and end apart: 9 -> 8, of which waited for: 4 -> 5; matrix products, arithmetic and copies ran while one was open for 0% -> 0% of each run, Pallas kernels for 21% -> 20%
where the time goes in v9:
time: 29.4 us; the launch traced here: 29.2 us
  Pallas kernels  9.85 us (34%)
  starting transfers between devices  9.71 us (33%)
  waiting for transfers between devices  8.95 us (30%)
  between operations  0.72 us (2%)
    ppermute x4, waiting for transfers between devices, passed_on(): lax.ppermute(value, 'label', [(i, i ^ bits[i % 2]) for i in range(n_label)])  6.28 us
    ppermute x4, starting transfers between devices, passed_on(): lax.ppermute(value, 'label', [(i, i ^ bits[i % 2]) for i in range(n_label)])  6.05 us
    ppermute x4, starting transfers between devices, swapped(): return lax.ppermute(value, axis, [(i, i ^ bit) for i in range(size)])  3.66 us
    pallas_call x1, Pallas kernels, on_device(): pl.pallas_call(functools.partial(first_kernel, n_label), out_shape=[shape...  3.18 us
    ppermute x4, waiting for transfers between devices, swapped(): return lax.ppermute(value, axis, [(i, i ^ bit) for i in range(size)])  2.66 us
    pallas_call x1, Pallas kernels, on_device(): pl.pallas_call(last_rows_kernel, out_shape=[part_shape] * 2 + [row_shape,...  1.71 us
    pallas_call x1, Pallas kernels, on_device(): pl.pallas_call(label_kernel, out_shape=[shape((CLUSTER, rows), jnp.int16)...  1.64 us
    pallas_call x1, Pallas kernels, on_device(): pl.pallas_call(keep_rows_kernel, out_shape=[tile_shape, row_shape], in_sp...  1.08 us
  transfers between devices with their start and end apart: 8, of which 5 were waited for; matrix products, arithmetic and copies ran while one was open for 0% of the time, Pallas kernels for 20%

profile of v9, /device:TPU:0, one launch (start us, length us, event | category | flops | bytes accessed | tf_op | source)
XLA Modules:
  0.0 29.2 jit_solution(10621230175445465082)
XLA Ops:
  0.6 3.2 %first_rows.1 = (bf16[1024,768]{1,0:T(8,128)(2,1)S(1)}, bf16[1024,768]{1,0:T(8,128)(2,1)S(1)}, s32[8,1024]{1,0:T(8,128)S(1)}, bf16[2,4,8,128]{3,2,1,0:T(8,128)(2...) custom-call(bf16[1024,768]{1,0:T(8,128)(2,1)} %embed_hbm.1, ...), custom_call_target="tpu_custom_call" | custom-call | flops 1610612736 | tf_op jit(solution)/shard_map/first_rows/pallas_call | solution.py:320
  3.8 0.5 %collective-permute-start = (bf16[4,1,64,768]{3,2,1,0:T(8,128)(2,1)S(1)}, bf16[4,1,64,768]{3,2,1,0:T(8,128)(2,1)S(1)}, u32[]{:S(2)}, u32[]{:S(2)}) collective-permute-start(bf16[4,1,64,768]{3,2,1,0:T(8,128)(2,1)S(1)} %get-tuple-element.29), channel_id=1, source_target_pairs={{0,1},{1,0},{2,3},{3,2},{4,5},{5,4},{6,7},{7,6},{8,9},{9,8},{10,11... | collective-permute-start | bytes 1179656 | tf_op jit(solution)/shard_map/ppermute | solution.py:289
  4.3 1.6 %send_half.1 = (s16[128,1024]{1,0:T(8,128)(2,1)S(1)}, bf16[512,768]{1,0:T(8,128)(2,1)S(1)}, bf16[512,768]{1,0:T(8,128)(2,1)S(1)}) custom-call(bf16[1024,768]{1,0:T(8,128)(2,1)S(1)} %get-tuple-element.37.embed, bf16[1024,768]{1,0:T(8,128)(2,1)S(1)} %get-tuple-element.38.w, s32[8,1024]{1,0:T(8,128)S(1)} %get-tuple-element.31.pos, ...), custom_call_target="tpu_custom_call" | custom-call | tf_op jit(solution)/shard_map/send_half/pallas_call | solution.py:351
  6.0 2.6 %collective-permute-start.1 = (bf16[512,768]{1,0:T(8,128)(2,1)S(1)}, bf16[512,768]{1,0:T(8,128)(2,1)S(1)}, u32[]{:S(2)}, u32[]{:S(2)}) collective-permute-start(bf16[512,768]{1,0:T(8,128)(2,1)S(1)} %get-tuple-element.46), channel_id=1, source_target_pairs={{0,16},{16,0},{1,17},{17,1},{2,18},{18,2},{3,19},{19,3},{4,20},{20... | collective-permute-start | bytes 2359304 | tf_op jit(solution)/shard_map/ppermute | solution.py:289
  8.6 0.0 collective-permute-done.refs_1_
  8.6 1.1 %keep_rows.1 = (bf16[512,256]{1,0:T(8,128)(2,1)S(1)}, bf16[4,1,64,768]{3,2,1,0:T(8,128)(2,1)S(1)}) custom-call(bf16[1024,768]{1,0:T(8,128)(2,1)S(1)} %get-tuple-element.37.embed, bf16[1024,768]{1,0:T(8,128)(2,1)S(1)} %get-tuple-element.38.w, s16[128,1024]{1,0:T(8,128)(2,1)S(1)} %get-tuple-element.39.word, bf16[2,4,8,128]{3,2,1,0:T(8,128)(2,1)S(1)} %get-tuple-element.40.mask, ...), custom_call_target="tpu_custom_call" | custom-call | tf_op jit(solution)/shard_map/keep_rows/pallas_call | solution.py:371
  9.6 0.1 row_sum.4
  9.7 1.6 %collective-permute-start.3 = (bf16[4,1,64,768]{3,2,1,0:T(8,128)(2,1)S(1)}, bf16[4,1,64,768]{3,2,1,0:T(8,128)(2,1)S(1)}, u32[]{:S(2)}, u32[]{:S(2)}) collective-permute-start(bf16[4,1,64,768]{3,2,1,0:T(8,128)(2,1)S(1)} %row_sum.4), channel_id=1, source_target_pairs={{0,2},{1,5},{2,0},{3,7},{4,6},{5,1},{6,4},{7,3},{8,10},{9,13},{10,... | collective-permute-start | bytes 1179656 | tf_op jit(solution)/shard_map/ppermute | solution.py:399
  11.3 1.7 %last_rows.1 = (bf16[2,1,64,768]{3,2,1,0:T(8,128)(2,1)S(1)}, bf16[2,1,64,768]{3,2,1,0:T(8,128)(2,1)S(1)}, bf16[4,1,64,768]{3,2,1,0:T(8,128)(2,1)S(1)}, bf16[512,256]{1,0:T(8,128)(2,1)S(1)}, bf16[512,256]{1,0:T(8,128)(2,1)S(1)}) custom-call(bf16[1024,768]{1,0:T(8,128)(2,1)S(1)} %get-tuple-element.37.embed, bf16[1024,768]{1,0:T(8,128)(2,1)S(1)} %get-tuple-element.38.w, ...), custom_call_target="tpu_custom_call" | custom-call | flops 1610612736 | tf_op jit(solution)/shard_map/last_rows/pallas_call | solution.py:404
  13.0 0.1 collective-permute-start.4
  13.1 0.5 %collective-permute-start.2 = (bf16[2,1,64,768]{3,2,1,0:T(8,128)(2,1)S(1)}, bf16[2,1,64,768]{3,2,1,0:T(8,128)(2,1)S(1)}, u32[]{:S(2)}, u32[]{:S(2)}) collective-permute-start(bf16[2,1,64,768]{3,2,1,0:T(8,128)(2,1)S(1)} %get-tuple-element.48), channel_id=1, source_target_pairs={{0,1},{1,0},{2,3},{3,2},{4,5},{5,4},{6,7},{7,6},{8,9},{9,8},{10,11... | collective-permute-start | bytes 589832 | tf_op jit(solution)/shard_map/ppermute | solution.py:289
  13.6 0.9 %collective-permute-done.4.refs_1_ = bf16[2,1,64,768]{3,2,1,0:T(8,128)(2,1)S(1)} collective-permute-done((bf16[2,1,64,768]{3,2,1,0:T(8,128)(2,1)S(1)}, bf16[2,1,64,768]{3,2,1,0:T(8,128)(2,1)S(1)}, u32[]{:S(2)}, u32[]{:S(2)}) %collective-permute-start.4) | collective-permute-done | bytes 196640 | tf_op jit(solution)/shard_map/ppermute | solution.py:289
  14.6 3.0 %collective-permute-done.3.refs_2_ = bf16[4,1,64,768]{3,2,1,0:T(8,128)(2,1)S(1)} collective-permute-done((bf16[4,1,64,768]{3,2,1,0:T(8,128)(2,1)S(1)}, bf16[4,1,64,768]{3,2,1,0:T(8,128)(2,1)S(1)}, u32[]{:S(2)}, u32[]{:S(2)}) %collective-permute-start.3) | collective-permute-done | bytes 393248 | tf_op jit(solution)/shard_map/ppermute | solution.py:399
  17.6 1.6 %collective-permute-start.6 = (bf16[1,1,64,768]{3,2,1,0:T(8,128)(2,1)S(1)}, bf16[1,1,64,768]{3,2,1,0:T(8,128)(2,1)S(1)}, u32[]{:S(2)}, u32[]{:S(2)}) collective-permute-start(bf16[1,1,64,768]{3,2,1,0:T(8,128)(2,1)S(1)} %row_sum.6), channel_id=1, source_target_pairs={{0,4},{1,9},{2,6},{3,11},{4,0},{5,13},{6,2},{7,15},{8,12},{9,1},{1... | collective-permute-start | bytes 294920 | tf_op jit(solution)/shard_map/ppermute | solution.py:399
  19.3 1.0 %keep_half.1.kept = bf16[512,768]{1,0:T(8,128)(2,1)S(1)} custom-call(bf16[1024,768]{1,0:T(8,128)(2,1)S(1)} %get-tuple-element.37.embed, bf16[512,256]{1,0:T(8,128)(2,1)S(1)} %get-tuple-element.28.refs_0_, bf16[512,256]{1,0:T(8,128)(2,1)S(1)} %get-tuple-element.43.refs_1_, bf16[512,256]{1,0:T(8,128)(2,1)S(1)} %get-tuple-element.44.refs_2_, ...), custom_call_target="tpu_custom_call" | custom-call | tf_op jit(solution)/shard_map/keep_half/pallas_call | solution.py:433
  20.3 0.5 %collective-permute-start.5 = (bf16[1,1,64,768]{3,2,1,0:T(8,128)(2,1)S(1)}, bf16[1,1,64,768]{3,2,1,0:T(8,128)(2,1)S(1)}, u32[]{:S(2)}, u32[]{:S(2)}) collective-permute-start(bf16[1,1,64,768]{3,2,1,0:T(8,128)(2,1)S(1)} %row_sum.5), channel_id=1, source_target_pairs={{0,4},{1,9},{2,6},{3,11},{4,0},{5,13},{6,2},{7,15},{8,12},{9,1},{1... | collective-permute-start | bytes 294920 | tf_op jit(solution)/shard_map/ppermute | solution.py:399
  20.8 0.0 collective-permute-done.2.refs_1_
  20.8 1.8 %collective-permute-done.6.refs_3_ = bf16[1,1,64,768]{3,2,1,0:T(8,128)(2,1)S(1)} collective-permute-done((bf16[1,1,64,768]{3,2,1,0:T(8,128)(2,1)S(1)}, bf16[1,1,64,768]{3,2,1,0:T(8,128)(2,1)S(1)}, u32[]{:S(2)}, u32[]{:S(2)}) %collective-permute-start.6) | collective-permute-done | bytes 98336 | tf_op jit(solution)/shard_map/ppermute | solution.py:399
  22.7 0.1 row_sum.7
  22.7 2.3 %collective-permute-start.7 = (bf16[1,1,64,768]{3,2,1,0:T(8,128)(2,1)S(1)}, bf16[1,1,64,768]{3,2,1,0:T(8,128)(2,1)S(1)}, u32[]{:S(2)}, u32[]{:S(2)}) collective-permute-start(bf16[1,1,64,768]{3,2,1,0:T(8,128)(2,1)S(1)} %row_sum.7), channel_id=1, source_target_pairs={{0,8},{1,3},{2,10},{3,1},{4,12},{5,7},{6,14},{7,5},{8,0},{9,11},{1... | collective-permute-start | bytes 294920 | tf_op jit(solution)/shard_map/ppermute | solution.py:399
  25.0 1.7 %collective-permute-done.1.got = bf16[512,768]{1,0:T(8,128)(2,1)S(1)} collective-permute-done((bf16[512,768]{1,0:T(8,128)(2,1)S(1)}, bf16[512,768]{1,0:T(8,128)(2,1)S(1)}, u32[]{:S(2)}, u32[]{:S(2)}) %collective-permute-start.1) | collective-permute-done | bytes 786464 | tf_op jit(solution)/shard_map/ppermute | solution.py:289
  26.8 0.1 half_sum.1.summed
  26.8 0.0 collective-permute-done.5.refs_3_
  26.9 1.4 %collective-permute-done.7.refs_4_ = bf16[1,1,64,768]{3,2,1,0:T(8,128)(2,1)S(1)} collective-permute-done((bf16[1,1,64,768]{3,2,1,0:T(8,128)(2,1)S(1)}, bf16[1,1,64,768]{3,2,1,0:T(8,128)(2,1)S(1)}, u32[]{:S(2)}, u32[]{:S(2)}) %collective-permute-start.7) | collective-permute-done | bytes 98336 | tf_op jit(solution)/shard_map/ppermute | solution.py:399
  28.3 0.9 %finish.1 = (bf16[64,768]{1,0:T(8,128)(2,1)}, bf16[512,768]{1,0:T(8,128)(2,1)}) custom-call(bf16[512,768]{1,0:T(8,128)(2,1)S(1)} %keep_half.1.kept, bf16[512,768]{1,0:T(8,128)(2,1)S(1)} %collective-permute-done.1.got, bf16[256,768]{1,0:T(8,128)(2,1)S(1)} %half_sum.1.summed, bf16[4,1,64,768]{3,2,1,0:T(8,128)(2,1)S(1)} %get-tuple-element.47.refs_0_, ...), custom_call_target="tpu_custom_call" | custom-call | tf_op jit(solution)/shard_map/finish/pallas_call | solution.py:465
  (2 shorter events, 0.1 us)
Async XLA Ops:
  3.8 4.7 %collective-permute-start = (bf16[4,1,64,768]{3,2,1,0:T(8,128)(2,1)S(1)}, bf16[4,1,64,768]{3,2,1,0:T(8,128)(2,1)S(1)}, u32[]{:S(2)}, u32[]{:S(2)}) collective-permute-start(bf16[4,1,64,768]{3,2,1,0:T(8,128)(2,1)S(1)} %get-tuple-element.29), channel_id=1, source_target_pairs={{0,1},{1,0},{2,3},{3,2},{4,5},{5,4},{6,7},{7,6},{8,9},{9,8},{10,11... | collective-permute-start | bytes 1179656 | tf_op jit(solution)/shard_map/ppermute | solution.py:289
  6.0 20.8 %collective-permute-start.1 = (bf16[512,768]{1,0:T(8,128)(2,1)S(1)}, bf16[512,768]{1,0:T(8,128)(2,1)S(1)}, u32[]{:S(2)}, u32[]{:S(2)}) collective-permute-start(bf16[512,768]{1,0:T(8,128)(2,1)S(1)} %get-tuple-element.46), channel_id=1, source_target_pairs={{0,16},{16,0},{1,17},{17,1},{2,18},{18,2},{3,19},{19,3},{4,20},{20... | collective-permute-start | bytes 2359304 | tf_op jit(solution)/shard_map/ppermute | solution.py:289
  9.7 7.8 %collective-permute-start.3 = (bf16[4,1,64,768]{3,2,1,0:T(8,128)(2,1)S(1)}, bf16[4,1,64,768]{3,2,1,0:T(8,128)(2,1)S(1)}, u32[]{:S(2)}, u32[]{:S(2)}) collective-permute-start(bf16[4,1,64,768]{3,2,1,0:T(8,128)(2,1)S(1)} %row_sum.4), channel_id=1, source_target_pairs={{0,2},{1,5},{2,0},{3,7},{4,6},{5,1},{6,4},{7,3},{8,10},{9,13},{10,... | collective-permute-start | bytes 1179656 | tf_op jit(solution)/shard_map/ppermute | solution.py:399
  13.0 1.5 %collective-permute-start.4 = (bf16[2,1,64,768]{3,2,1,0:T(8,128)(2,1)S(1)}, bf16[2,1,64,768]{3,2,1,0:T(8,128)(2,1)S(1)}, u32[]{:S(2)}, u32[]{:S(2)}) collective-permute-start(bf16[2,1,64,768]{3,2,1,0:T(8,128)(2,1)S(1)} %get-tuple-element.51), channel_id=1, source_target_pairs={{0,1},{1,0},{2,3},{3,2},{4,5},{5,4},{6,7},{7,6},{8,9},{9,8},{10,11... | collective-permute-start | bytes 589832 | tf_op jit(solution)/shard_map/ppermute | solution.py:289
  13.1 7.7 %collective-permute-start.2 = (bf16[2,1,64,768]{3,2,1,0:T(8,128)(2,1)S(1)}, bf16[2,1,64,768]{3,2,1,0:T(8,128)(2,1)S(1)}, u32[]{:S(2)}, u32[]{:S(2)}) collective-permute-start(bf16[2,1,64,768]{3,2,1,0:T(8,128)(2,1)S(1)} %get-tuple-element.48), channel_id=1, source_target_pairs={{0,1},{1,0},{2,3},{3,2},{4,5},{5,4},{6,7},{7,6},{8,9},{9,8},{10,11... | collective-permute-start | bytes 589832 | tf_op jit(solution)/shard_map/ppermute | solution.py:289
  17.6 5.0 %collective-permute-start.6 = (bf16[1,1,64,768]{3,2,1,0:T(8,128)(2,1)S(1)}, bf16[1,1,64,768]{3,2,1,0:T(8,128)(2,1)S(1)}, u32[]{:S(2)}, u32[]{:S(2)}) collective-permute-start(bf16[1,1,64,768]{3,2,1,0:T(8,128)(2,1)S(1)} %row_sum.6), channel_id=1, source_target_pairs={{0,4},{1,9},{2,6},{3,11},{4,0},{5,13},{6,2},{7,15},{8,12},{9,1},{1... | collective-permute-start | bytes 294920 | tf_op jit(solution)/shard_map/ppermute | solution.py:399
  20.3 6.5 %collective-permute-start.5 = (bf16[1,1,64,768]{3,2,1,0:T(8,128)(2,1)S(1)}, bf16[1,1,64,768]{3,2,1,0:T(8,128)(2,1)S(1)}, u32[]{:S(2)}, u32[]{:S(2)}) collective-permute-start(bf16[1,1,64,768]{3,2,1,0:T(8,128)(2,1)S(1)} %row_sum.5), channel_id=1, source_target_pairs={{0,4},{1,9},{2,6},{3,11},{4,0},{5,13},{6,2},{7,15},{8,12},{9,1},{1... | collective-permute-start | bytes 294920 | tf_op jit(solution)/shard_map/ppermute | solution.py:399
  22.7 5.6 %collective-permute-start.7 = (bf16[1,1,64,768]{3,2,1,0:T(8,128)(2,1)S(1)}, bf16[1,1,64,768]{3,2,1,0:T(8,128)(2,1)S(1)}, u32[]{:S(2)}, u32[]{:S(2)}) collective-permute-start(bf16[1,1,64,768]{3,2,1,0:T(8,128)(2,1)S(1)} %row_sum.7), channel_id=1, source_target_pairs={{0,8},{1,3},{2,10},{3,1},{4,12},{5,7},{6,14},{7,5},{8,0},{9,11},{1... | collective-permute-start | bytes 294920 | tf_op jit(solution)/shard_map/ppermute | solution.py:399

commit v10 on v8

--- a/solution.py
+++ b/solution.py
@@ -208,15 +208,13 @@
 
     def emit(k, t, c, part):
         slopes_t[c * CLUSTER : (c + 1) * CLUSTER, (t - 1) * TILE : t * TILE] = part
-        if t == tiles - 1 and (c + 1) % (CHUNK // CLUSTER) == 0:
-            rows = slice((c + 1) * CLUSTER - CHUNK, (c + 1) * CLUSTER)
-            label_out[rows] = (
-                jnp.dot(one_slopes_t[rows], embed[:TILE], preferred_element_type=F32)
-                + jnp.dot(slopes_t[rows], embed[TILE:], preferred_element_type=F32)
-            ).astype(BF16)
 
     jobs = [(0, t, h) for t in range(1, tiles) for h in range(half_rows // CHUNK)]
     slope_chunks(jobs, scores, w, embed, bias_full, mask, word, lambda *job: None, emit)
+    label_out[...] = (
+        jnp.dot(one_slopes_t[...], embed[:TILE], preferred_element_type=F32)
+        + jnp.dot(slopes_t[...], embed[TILE:], preferred_element_type=F32)
+    ).astype(BF16)
 
 
 def store_rows(outs, slopes, w):

time: 28 us -> 28.1 us (level)
  no operation moved by 1% of the time
where the time goes in v10:
time: 28.1 us; the launch traced here: 27.9 us
  starting transfers between devices  11 us (39%)
  Pallas kernels  9.98 us (36%)
  waiting for transfers between devices  6.25 us (22%)
  between operations  0.73 us (3%)
    ppermute x5, starting transfers between devices, passed_on(): lax.ppermute(value, 'label', [(i, i ^ bits[i % 2]) for i in range(n_label)])  7.53 us
    ppermute x4, waiting for transfers between devices, swapped(): return lax.ppermute(value, axis, [(i, i ^ bit) for i in range(size)])  3.55 us
    ppermute x4, starting transfers between devices, swapped(): return lax.ppermute(value, axis, [(i, i ^ bit) for i in range(size)])  3.45 us
    pallas_call x1, Pallas kernels, on_device(): pl.pallas_call(functools.partial(first_kernel, n_label), out_shape=[shape...  3.18 us
    ppermute x5, waiting for transfers between devices, passed_on(): lax.ppermute(value, 'label', [(i, i ^ bits[i % 2]) for i in range(n_label)])  2.69 us
    pallas_call x1, Pallas kernels, on_device(): pl.pallas_call(label_kernel, out_shape=[shape((CLUSTER, rows), jnp.int16)...  1.77 us
    pallas_call x1, Pallas kernels, on_device(): pl.pallas_call(last_rows_kernel, out_shape=[part_shape] * 2 + [row_shape,...  1.71 us
    pallas_call x1, Pallas kernels, on_device(): pl.pallas_call(keep_rows_kernel, out_shape=[tile_shape, row_shape], in_sp...  1.08 us
  transfers between devices with their start and end apart: 9, of which 4 were waited for; matrix products, arithmetic and copies ran while one was open for 0% of the time, Pallas kernels for 21%

profile of v10, /device:TPU:0, one launch (start us, length us, event | category | flops | bytes accessed | tf_op | source)
XLA Modules:
  0.0 27.9 jit_solution(13818033288392333661)
XLA Ops:
  0.6 3.2 %first_rows.1 = (bf16[1024,768]{1,0:T(8,128)(2,1)S(1)}, bf16[1024,768]{1,0:T(8,128)(2,1)S(1)}, s32[8,1024]{1,0:T(8,128)S(1)}, bf16[2,4,8,128]{3,2,1,0:T(8,128)(2...) custom-call(bf16[1024,768]{1,0:T(8,128)(2,1)} %embed_hbm.1, ...), custom_call_target="tpu_custom_call" | custom-call | flops 1610612736 | tf_op jit(solution)/shard_map/first_rows/pallas_call | solution.py:318
  3.8 0.5 %collective-permute-start = (bf16[4,1,64,768]{3,2,1,0:T(8,128)(2,1)S(1)}, bf16[4,1,64,768]{3,2,1,0:T(8,128)(2,1)S(1)}, u32[]{:S(2)}, u32[]{:S(2)}) collective-permute-start(bf16[4,1,64,768]{3,2,1,0:T(8,128)(2,1)S(1)} %get-tuple-element.29), channel_id=1, source_target_pairs={{0,1},{1,0},{2,3},{3,2},{4,5},{5,4},{6,7},{7,6},{8,9},{9,8},{10,11... | collective-permute-start | bytes 1179656 | tf_op jit(solution)/shard_map/ppermute | solution.py:287
  4.3 1.8 %send_half.1 = (s16[128,1024]{1,0:T(8,128)(2,1)S(1)}, bf16[512,768]{1,0:T(8,128)(2,1)S(1)}, bf16[512,768]{1,0:T(8,128)(2,1)S(1)}) custom-call(bf16[1024,768]{1,0:T(8,128)(2,1)S(1)} %get-tuple-element.37.embed, bf16[1024,768]{1,0:T(8,128)(2,1)S(1)} %get-tuple-element.38.w, s32[8,1024]{1,0:T(8,128)S(1)} %get-tuple-element.31.pos, ...), custom_call_target="tpu_custom_call" | custom-call | tf_op jit(solution)/shard_map/send_half/pallas_call | solution.py:349
  6.1 2.6 %collective-permute-start.1 = (bf16[512,768]{1,0:T(8,128)(2,1)S(1)}, bf16[512,768]{1,0:T(8,128)(2,1)S(1)}, u32[]{:S(2)}, u32[]{:S(2)}) collective-permute-start(bf16[512,768]{1,0:T(8,128)(2,1)S(1)} %get-tuple-element.46), channel_id=1, source_target_pairs={{0,16},{16,0},{1,17},{17,1},{2,18},{18,2},{3,19},{19,3},{4,20},{20... | collective-permute-start | bytes 2359304 | tf_op jit(solution)/shard_map/ppermute | solution.py:287
  8.7 0.0 collective-permute-done.refs_1_
  8.7 1.1 %keep_rows.1 = (bf16[512,256]{1,0:T(8,128)(2,1)S(1)}, bf16[4,1,64,768]{3,2,1,0:T(8,128)(2,1)S(1)}) custom-call(bf16[1024,768]{1,0:T(8,128)(2,1)S(1)} %get-tuple-element.37.embed, bf16[1024,768]{1,0:T(8,128)(2,1)S(1)} %get-tuple-element.38.w, s16[128,1024]{1,0:T(8,128)(2,1)S(1)} %get-tuple-element.39.word, bf16[2,4,8,128]{3,2,1,0:T(8,128)(2,1)S(1)} %get-tuple-element.40.mask, ...), custom_call_target="tpu_custom_call" | custom-call | tf_op jit(solution)/shard_map/keep_rows/pallas_call | solution.py:369
  9.8 1.6 %collective-permute-start.5 = (bf16[2,1,64,768]{3,2,1,0:T(8,128)(2,1)S(1)}, bf16[2,1,64,768]{3,2,1,0:T(8,128)(2,1)S(1)}, u32[]{:S(2)}, u32[]{:S(2)}) collective-permute-start(bf16[2,1,64,768]{3,2,1,0:T(8,128)(2,1)S(1)} %row_sum.6), channel_id=1, source_target_pairs={{0,2},{1,5},{2,0},{3,7},{4,6},{5,1},{6,4},{7,3},{8,10},{9,13},{10,... | collective-permute-start | bytes 589832 | tf_op jit(solution)/shard_map/ppermute | solution.py:397
  11.4 1.7 %last_rows.1 = (bf16[2,1,64,768]{3,2,1,0:T(8,128)(2,1)S(1)}, bf16[2,1,64,768]{3,2,1,0:T(8,128)(2,1)S(1)}, bf16[4,1,64,768]{3,2,1,0:T(8,128)(2,1)S(1)}, bf16[512,256]{1,0:T(8,128)(2,1)S(1)}, bf16[512,256]{1,0:T(8,128)(2,1)S(1)}) custom-call(bf16[1024,768]{1,0:T(8,128)(2,1)S(1)} %get-tuple-element.37.embed, bf16[1024,768]{1,0:T(8,128)(2,1)S(1)} %get-tuple-element.38.w, ...), custom_call_target="tpu_custom_call" | custom-call | flops 1610612736 | tf_op jit(solution)/shard_map/last_rows/pallas_call | solution.py:403
  13.1 0.1 collective-permute-start.4
  13.3 1.6 %collective-permute-start.3 = (bf16[2,1,64,768]{3,2,1,0:T(8,128)(2,1)S(1)}, bf16[2,1,64,768]{3,2,1,0:T(8,128)(2,1)S(1)}, u32[]{:S(2)}, u32[]{:S(2)}) collective-permute-start(bf16[2,1,64,768]{3,2,1,0:T(8,128)(2,1)S(1)} %row_sum.5), channel_id=1, source_target_pairs={{0,2},{1,5},{2,0},{3,7},{4,6},{5,1},{6,4},{7,3},{8,10},{9,13},{10,... | collective-permute-start | bytes 589832 | tf_op jit(solution)/shard_map/ppermute | solution.py:397
  14.8 0.3 %collective-permute-start.2 = (bf16[2,1,64,768]{3,2,1,0:T(8,128)(2,1)S(1)}, bf16[2,1,64,768]{3,2,1,0:T(8,128)(2,1)S(1)}, u32[]{:S(2)}, u32[]{:S(2)}) collective-permute-start(bf16[2,1,64,768]{3,2,1,0:T(8,128)(2,1)S(1)} %get-tuple-element.48), channel_id=1, source_target_pairs={{0,1},{1,0},{2,3},{3,2},{4,5},{5,4},{6,7},{7,6},{8,9},{9,8},{10,11... | collective-permute-start | bytes 589832 | tf_op jit(solution)/shard_map/ppermute | solution.py:287
  15.1 0.4 %collective-permute-done.5.refs_2_ = bf16[2,1,64,768]{3,2,1,0:T(8,128)(2,1)S(1)} collective-permute-done((bf16[2,1,64,768]{3,2,1,0:T(8,128)(2,1)S(1)}, bf16[2,1,64,768]{3,2,1,0:T(8,128)(2,1)S(1)}, u32[]{:S(2)}, u32[]{:S(2)}) %collective-permute-start.5) | collective-permute-done | bytes 196640 | tf_op jit(solution)/shard_map/ppermute | solution.py:397
  15.6 0.0 collective-permute-done.4.refs_1_
  15.6 1.6 %collective-permute-start.7 = (bf16[1,1,64,768]{3,2,1,0:T(8,128)(2,1)S(1)}, bf16[1,1,64,768]{3,2,1,0:T(8,128)(2,1)S(1)}, u32[]{:S(2)}, u32[]{:S(2)}) collective-permute-start(bf16[1,1,64,768]{3,2,1,0:T(8,128)(2,1)S(1)} %row_sum.8), channel_id=1, source_target_pairs={{0,4},{1,9},{2,6},{3,11},{4,0},{5,13},{6,2},{7,15},{8,12},{9,1},{1... | collective-permute-start | bytes 294920 | tf_op jit(solution)/shard_map/ppermute | solution.py:397
  17.2 1.0 %keep_half.1.kept = bf16[512,768]{1,0:T(8,128)(2,1)S(1)} custom-call(bf16[1024,768]{1,0:T(8,128)(2,1)S(1)} %get-tuple-element.37.embed, bf16[512,256]{1,0:T(8,128)(2,1)S(1)} %get-tuple-element.28.refs_0_, bf16[512,256]{1,0:T(8,128)(2,1)S(1)} %get-tuple-element.43.refs_1_, bf16[512,256]{1,0:T(8,128)(2,1)S(1)} %get-tuple-element.44.refs_2_, ...), custom_call_target="tpu_custom_call" | custom-call | tf_op jit(solution)/shard_map/keep_half/pallas_call | solution.py:432
  18.3 0.5 %collective-permute-start.6 = (bf16[1,1,64,768]{3,2,1,0:T(8,128)(2,1)S(1)}, bf16[1,1,64,768]{3,2,1,0:T(8,128)(2,1)S(1)}, u32[]{:S(2)}, u32[]{:S(2)}) collective-permute-start(bf16[1,1,64,768]{3,2,1,0:T(8,128)(2,1)S(1)} %row_sum.7), channel_id=1, source_target_pairs={{0,4},{1,9},{2,6},{3,11},{4,0},{5,13},{6,2},{7,15},{8,12},{9,1},{1... | collective-permute-start | bytes 294920 | tf_op jit(solution)/shard_map/ppermute | solution.py:397
  18.8 0.2 collective-permute-done.3.refs_2_
  19.0 0.0 collective-permute-done.2.refs_1_
  19.0 2.1 %collective-permute-done.7.refs_3_ = bf16[1,1,64,768]{3,2,1,0:T(8,128)(2,1)S(1)} collective-permute-done((bf16[1,1,64,768]{3,2,1,0:T(8,128)(2,1)S(1)}, bf16[1,1,64,768]{3,2,1,0:T(8,128)(2,1)S(1)}, u32[]{:S(2)}, u32[]{:S(2)}) %collective-permute-start.7) | collective-permute-done | bytes 98336 | tf_op jit(solution)/shard_map/ppermute | solution.py:397
  21.1 0.1 row_sum.9
  21.1 2.2 %collective-permute-start.8 = (bf16[1,1,64,768]{3,2,1,0:T(8,128)(2,1)S(1)}, bf16[1,1,64,768]{3,2,1,0:T(8,128)(2,1)S(1)}, u32[]{:S(2)}, u32[]{:S(2)}) collective-permute-start(bf16[1,1,64,768]{3,2,1,0:T(8,128)(2,1)S(1)} %row_sum.9), channel_id=1, source_target_pairs={{0,8},{1,3},{2,10},{3,1},{4,12},{5,7},{6,14},{7,5},{8,0},{9,11},{1... | collective-permute-start | bytes 294920 | tf_op jit(solution)/shard_map/ppermute | solution.py:397
  23.3 3.5 %collective-permute-done.1.got = bf16[512,768]{1,0:T(8,128)(2,1)S(1)} collective-permute-done((bf16[512,768]{1,0:T(8,128)(2,1)S(1)}, bf16[512,768]{1,0:T(8,128)(2,1)S(1)}, u32[]{:S(2)}, u32[]{:S(2)}) %collective-permute-start.1) | collective-permute-done | bytes 786464 | tf_op jit(solution)/shard_map/ppermute | solution.py:287
  26.9 0.1 half_sum.1.summed
  27.0 0.0 collective-permute-done.6.refs_3_
  27.0 0.0 collective-permute-done.8.refs_4_
  27.0 0.9 %finish.1 = (bf16[64,768]{1,0:T(8,128)(2,1)}, bf16[512,768]{1,0:T(8,128)(2,1)}) custom-call(bf16[512,768]{1,0:T(8,128)(2,1)S(1)} %keep_half.1.kept, bf16[512,768]{1,0:T(8,128)(2,1)S(1)} %collective-permute-done.1.got, bf16[256,768]{1,0:T(8,128)(2,1)S(1)} %half_sum.1.summed, bf16[4,1,64,768]{3,2,1,0:T(8,128)(2,1)S(1)} %get-tuple-element.47.refs_0_, ...), custom_call_target="tpu_custom_call" | custom-call | tf_op jit(solution)/shard_map/finish/pallas_call | solution.py:464
  (4 shorter events, 0.2 us)
Async XLA Ops:
  3.8 4.9 %collective-permute-start = (bf16[4,1,64,768]{3,2,1,0:T(8,128)(2,1)S(1)}, bf16[4,1,64,768]{3,2,1,0:T(8,128)(2,1)S(1)}, u32[]{:S(2)}, u32[]{:S(2)}) collective-permute-start(bf16[4,1,64,768]{3,2,1,0:T(8,128)(2,1)S(1)} %get-tuple-element.29), channel_id=1, source_target_pairs={{0,1},{1,0},{2,3},{3,2},{4,5},{5,4},{6,7},{7,6},{8,9},{9,8},{10,11... | collective-permute-start | bytes 1179656 | tf_op jit(solution)/shard_map/ppermute | solution.py:287
  6.1 20.8 %collective-permute-start.1 = (bf16[512,768]{1,0:T(8,128)(2,1)S(1)}, bf16[512,768]{1,0:T(8,128)(2,1)S(1)}, u32[]{:S(2)}, u32[]{:S(2)}) collective-permute-start(bf16[512,768]{1,0:T(8,128)(2,1)S(1)} %get-tuple-element.46), channel_id=1, source_target_pairs={{0,16},{16,0},{1,17},{17,1},{2,18},{18,2},{3,19},{19,3},{4,20},{20... | collective-permute-start | bytes 2359304 | tf_op jit(solution)/shard_map/ppermute | solution.py:287
  9.8 5.7 %collective-permute-start.5 = (bf16[2,1,64,768]{3,2,1,0:T(8,128)(2,1)S(1)}, bf16[2,1,64,768]{3,2,1,0:T(8,128)(2,1)S(1)}, u32[]{:S(2)}, u32[]{:S(2)}) collective-permute-start(bf16[2,1,64,768]{3,2,1,0:T(8,128)(2,1)S(1)} %row_sum.6), channel_id=1, source_target_pairs={{0,2},{1,5},{2,0},{3,7},{4,6},{5,1},{6,4},{7,3},{8,10},{9,13},{10,... | collective-permute-start | bytes 589832 | tf_op jit(solution)/shard_map/ppermute | solution.py:397
  13.1 2.4 %collective-permute-start.4 = (bf16[2,1,64,768]{3,2,1,0:T(8,128)(2,1)S(1)}, bf16[2,1,64,768]{3,2,1,0:T(8,128)(2,1)S(1)}, u32[]{:S(2)}, u32[]{:S(2)}) collective-permute-start(bf16[2,1,64,768]{3,2,1,0:T(8,128)(2,1)S(1)} %get-tuple-element.51), channel_id=1, source_target_pairs={{0,1},{1,0},{2,3},{3,2},{4,5},{5,4},{6,7},{7,6},{8,9},{9,8},{10,11... | collective-permute-start | bytes 589832 | tf_op jit(solution)/shard_map/ppermute | solution.py:287
  13.3 5.7 %collective-permute-start.3 = (bf16[2,1,64,768]{3,2,1,0:T(8,128)(2,1)S(1)}, bf16[2,1,64,768]{3,2,1,0:T(8,128)(2,1)S(1)}, u32[]{:S(2)}, u32[]{:S(2)}) collective-permute-start(bf16[2,1,64,768]{3,2,1,0:T(8,128)(2,1)S(1)} %row_sum.5), channel_id=1, source_target_pairs={{0,2},{1,5},{2,0},{3,7},{4,6},{5,1},{6,4},{7,3},{8,10},{9,13},{10,... | collective-permute-start | bytes 589832 | tf_op jit(solution)/shard_map/ppermute | solution.py:397
  14.8 4.2 %collective-permute-start.2 = (bf16[2,1,64,768]{3,2,1,0:T(8,128)(2,1)S(1)}, bf16[2,1,64,768]{3,2,1,0:T(8,128)(2,1)S(1)}, u32[]{:S(2)}, u32[]{:S(2)}) collective-permute-start(bf16[2,1,64,768]{3,2,1,0:T(8,128)(2,1)S(1)} %get-tuple-element.48), channel_id=1, source_target_pairs={{0,1},{1,0},{2,3},{3,2},{4,5},{5,4},{6,7},{7,6},{8,9},{9,8},{10,11... | collective-permute-start | bytes 589832 | tf_op jit(solution)/shard_map/ppermute | solution.py:287
  15.6 5.5 %collective-permute-start.7 = (bf16[1,1,64,768]{3,2,1,0:T(8,128)(2,1)S(1)}, bf16[1,1,64,768]{3,2,1,0:T(8,128)(2,1)S(1)}, u32[]{:S(2)}, u32[]{:S(2)}) collective-permute-start(bf16[1,1,64,768]{3,2,1,0:T(8,128)(2,1)S(1)} %row_sum.8), channel_id=1, source_target_pairs={{0,4},{1,9},{2,6},{3,11},{4,0},{5,13},{6,2},{7,15},{8,12},{9,1},{1... | collective-permute-start | bytes 294920 | tf_op jit(solution)/shard_map/ppermute | solution.py:397
  18.3 8.7 %collective-permute-start.6 = (bf16[1,1,64,768]{3,2,1,0:T(8,128)(2,1)S(1)}, bf16[1,1,64,768]{3,2,1,0:T(8,128)(2,1)S(1)}, u32[]{:S(2)}, u32[]{:S(2)}) collective-permute-start(bf16[1,1,64,768]{3,2,1,0:T(8,128)(2,1)S(1)} %row_sum.7), channel_id=1, source_target_pairs={{0,4},{1,9},{2,6},{3,11},{4,0},{5,13},{6,2},{7,15},{8,12},{9,1},{1... | collective-permute-start | bytes 294920 | tf_op jit(solution)/shard_map/ppermute | solution.py:397
  21.1 5.9 %collective-permute-start.8 = (bf16[1,1,64,768]{3,2,1,0:T(8,128)(2,1)S(1)}, bf16[1,1,64,768]{3,2,1,0:T(8,128)(2,1)S(1)}, u32[]{:S(2)}, u32[]{:S(2)}) collective-permute-start(bf16[1,1,64,768]{3,2,1,0:T(8,128)(2,1)S(1)} %row_sum.9), channel_id=1, source_target_pairs={{0,8},{1,3},{2,10},{3,1},{4,12},{5,7},{6,14},{7,5},{8,0},{9,11},{1... | collective-permute-start | bytes 294920 | tf_op jit(solution)/shard_map/ppermute | solution.py:397

commit v11 on v8

--- a/solution.py
+++ b/solution.py
@@ -166,8 +166,7 @@
         for i in range(4):
             group = 8 * (i % 2) + t * 2 + i // 2
             beam[group : group + 1] = beam_raw[pl.ds(block_in(t, i, over, core), 1)]
-    for t in range(tiles):
-        set_positives(t)
+    set_positives(0)
     set_words([0], pos, word)
 
     row = lax.broadcasted_iota(jnp.int32, (2 * clusters, 2 * clusters * INST_BLOCK), 0)
@@ -196,6 +195,8 @@
 
     jobs = [(k, 0, h) for k in range(2) for h in range(half_rows // CHUNK)]
     slope_chunks(jobs, scores, w, embed, bias_full, mask, word, before, emit)
+    for t in range(1, tiles):
+        set_positives(t)
     store_rows([row_out], slopes, w)
     for copy in (*e_copies[1], *e_copies[2], *e_copies[3]):
         copy.wait()

time: 28 us -> 28 us (level)
  no operation moved by 1% of the time
where the time goes in v11:
time: 28 us; the launch traced here: 27.8 us
  starting transfers between devices  11 us (39%)
  Pallas kernels  9.85 us (35%)
  waiting for transfers between devices  6.23 us (22%)
  between operations  0.73 us (3%)
    ppermute x5, starting transfers between devices, passed_on(): lax.ppermute(value, 'label', [(i, i ^ bits[i % 2]) for i in range(n_label)])  7.54 us
    ppermute x4, waiting for transfers between devices, swapped(): return lax.ppermute(value, axis, [(i, i ^ bit) for i in range(size)])  3.54 us
    ppermute x4, starting transfers between devices, swapped(): return lax.ppermute(value, axis, [(i, i ^ bit) for i in range(size)])  3.45 us
    pallas_call x1, Pallas kernels, on_device(): pl.pallas_call(functools.partial(first_kernel, n_label), out_shape=[shape...  3.18 us
    ppermute x5, waiting for transfers between devices, passed_on(): lax.ppermute(value, 'label', [(i, i ^ bits[i % 2]) for i in range(n_label)])  2.69 us
    pallas_call x1, Pallas kernels, on_device(): pl.pallas_call(last_rows_kernel, out_shape=[part_shape] * 2 + [row_shape,...  1.71 us
    pallas_call x1, Pallas kernels, on_device(): pl.pallas_call(label_kernel, out_shape=[shape((CLUSTER, rows), jnp.int16)...  1.64 us
    pallas_call x1, Pallas kernels, on_device(): pl.pallas_call(keep_rows_kernel, out_shape=[tile_shape, row_shape], in_sp...  1.08 us
  transfers between devices with their start and end apart: 9, of which 4 were waited for; matrix products, arithmetic and copies ran while one was open for 0% of the time, Pallas kernels for 21%

profile of v11, /device:TPU:0, one launch (start us, length us, event | category | flops | bytes accessed | tf_op | source)
XLA Modules:
  0.0 27.8 jit_solution(6289939201999922569)
XLA Ops:
  0.6 3.2 %first_rows.1 = (bf16[1024,768]{1,0:T(8,128)(2,1)S(1)}, bf16[1024,768]{1,0:T(8,128)(2,1)S(1)}, s32[8,1024]{1,0:T(8,128)S(1)}, bf16[2,4,8,128]{3,2,1,0:T(8,128)(2...) custom-call(bf16[1024,768]{1,0:T(8,128)(2,1)} %embed_hbm.1, ...), custom_call_target="tpu_custom_call" | custom-call | flops 1610612736 | tf_op jit(solution)/shard_map/first_rows/pallas_call | solution.py:321
  3.8 0.5 %collective-permute-start = (bf16[4,1,64,768]{3,2,1,0:T(8,128)(2,1)S(1)}, bf16[4,1,64,768]{3,2,1,0:T(8,128)(2,1)S(1)}, u32[]{:S(2)}, u32[]{:S(2)}) collective-permute-start(bf16[4,1,64,768]{3,2,1,0:T(8,128)(2,1)S(1)} %get-tuple-element.29), channel_id=1, source_target_pairs={{0,1},{1,0},{2,3},{3,2},{4,5},{5,4},{6,7},{7,6},{8,9},{9,8},{10,11... | collective-permute-start | bytes 1179656 | tf_op jit(solution)/shard_map/ppermute | solution.py:290
  4.3 1.6 %send_half.1 = (s16[128,1024]{1,0:T(8,128)(2,1)S(1)}, bf16[512,768]{1,0:T(8,128)(2,1)S(1)}, bf16[512,768]{1,0:T(8,128)(2,1)S(1)}) custom-call(bf16[1024,768]{1,0:T(8,128)(2,1)S(1)} %get-tuple-element.37.embed, bf16[1024,768]{1,0:T(8,128)(2,1)S(1)} %get-tuple-element.38.w, s32[8,1024]{1,0:T(8,128)S(1)} %get-tuple-element.31.pos, ...), custom_call_target="tpu_custom_call" | custom-call | tf_op jit(solution)/shard_map/send_half/pallas_call | solution.py:352
  6.0 2.6 %collective-permute-start.1 = (bf16[512,768]{1,0:T(8,128)(2,1)S(1)}, bf16[512,768]{1,0:T(8,128)(2,1)S(1)}, u32[]{:S(2)}, u32[]{:S(2)}) collective-permute-start(bf16[512,768]{1,0:T(8,128)(2,1)S(1)} %get-tuple-element.46), channel_id=1, source_target_pairs={{0,16},{16,0},{1,17},{17,1},{2,18},{18,2},{3,19},{19,3},{4,20},{20... | collective-permute-start | bytes 2359304 | tf_op jit(solution)/shard_map/ppermute | solution.py:290
  8.6 0.0 collective-permute-done.refs_1_
  8.6 1.1 %keep_rows.1 = (bf16[512,256]{1,0:T(8,128)(2,1)S(1)}, bf16[4,1,64,768]{3,2,1,0:T(8,128)(2,1)S(1)}) custom-call(bf16[1024,768]{1,0:T(8,128)(2,1)S(1)} %get-tuple-element.37.embed, bf16[1024,768]{1,0:T(8,128)(2,1)S(1)} %get-tuple-element.38.w, s16[128,1024]{1,0:T(8,128)(2,1)S(1)} %get-tuple-element.39.word, bf16[2,4,8,128]{3,2,1,0:T(8,128)(2,1)S(1)} %get-tuple-element.40.mask, ...), custom_call_target="tpu_custom_call" | custom-call | tf_op jit(solution)/shard_map/keep_rows/pallas_call | solution.py:372
  9.7 1.6 %collective-permute-start.5 = (bf16[2,1,64,768]{3,2,1,0:T(8,128)(2,1)S(1)}, bf16[2,1,64,768]{3,2,1,0:T(8,128)(2,1)S(1)}, u32[]{:S(2)}, u32[]{:S(2)}) collective-permute-start(bf16[2,1,64,768]{3,2,1,0:T(8,128)(2,1)S(1)} %row_sum.6), channel_id=1, source_target_pairs={{0,2},{1,5},{2,0},{3,7},{4,6},{5,1},{6,4},{7,3},{8,10},{9,13},{10,... | collective-permute-start | bytes 589832 | tf_op jit(solution)/shard_map/ppermute | solution.py:400
  11.3 1.7 %last_rows.1 = (bf16[2,1,64,768]{3,2,1,0:T(8,128)(2,1)S(1)}, bf16[2,1,64,768]{3,2,1,0:T(8,128)(2,1)S(1)}, bf16[4,1,64,768]{3,2,1,0:T(8,128)(2,1)S(1)}, bf16[512,256]{1,0:T(8,128)(2,1)S(1)}, bf16[512,256]{1,0:T(8,128)(2,1)S(1)}) custom-call(bf16[1024,768]{1,0:T(8,128)(2,1)S(1)} %get-tuple-element.37.embed, bf16[1024,768]{1,0:T(8,128)(2,1)S(1)} %get-tuple-element.38.w, ...), custom_call_target="tpu_custom_call" | custom-call | flops 1610612736 | tf_op jit(solution)/shard_map/last_rows/pallas_call | solution.py:406
  13.0 0.1 collective-permute-start.4
  13.1 1.6 %collective-permute-start.3 = (bf16[2,1,64,768]{3,2,1,0:T(8,128)(2,1)S(1)}, bf16[2,1,64,768]{3,2,1,0:T(8,128)(2,1)S(1)}, u32[]{:S(2)}, u32[]{:S(2)}) collective-permute-start(bf16[2,1,64,768]{3,2,1,0:T(8,128)(2,1)S(1)} %row_sum.5), channel_id=1, source_target_pairs={{0,2},{1,5},{2,0},{3,7},{4,6},{5,1},{6,4},{7,3},{8,10},{9,13},{10,... | collective-permute-start | bytes 589832 | tf_op jit(solution)/shard_map/ppermute | solution.py:400
  14.7 0.3 %collective-permute-start.2 = (bf16[2,1,64,768]{3,2,1,0:T(8,128)(2,1)S(1)}, bf16[2,1,64,768]{3,2,1,0:T(8,128)(2,1)S(1)}, u32[]{:S(2)}, u32[]{:S(2)}) collective-permute-start(bf16[2,1,64,768]{3,2,1,0:T(8,128)(2,1)S(1)} %get-tuple-element.48), channel_id=1, source_target_pairs={{0,1},{1,0},{2,3},{3,2},{4,5},{5,4},{6,7},{7,6},{8,9},{9,8},{10,11... | collective-permute-start | bytes 589832 | tf_op jit(solution)/shard_map/ppermute | solution.py:290
  15.0 0.4 %collective-permute-done.5.refs_2_ = bf16[2,1,64,768]{3,2,1,0:T(8,128)(2,1)S(1)} collective-permute-done((bf16[2,1,64,768]{3,2,1,0:T(8,128)(2,1)S(1)}, bf16[2,1,64,768]{3,2,1,0:T(8,128)(2,1)S(1)}, u32[]{:S(2)}, u32[]{:S(2)}) %collective-permute-start.5) | collective-permute-done | bytes 196640 | tf_op jit(solution)/shard_map/ppermute | solution.py:400
  15.4 0.0 collective-permute-done.4.refs_1_
  15.5 1.6 %collective-permute-start.7 = (bf16[1,1,64,768]{3,2,1,0:T(8,128)(2,1)S(1)}, bf16[1,1,64,768]{3,2,1,0:T(8,128)(2,1)S(1)}, u32[]{:S(2)}, u32[]{:S(2)}) collective-permute-start(bf16[1,1,64,768]{3,2,1,0:T(8,128)(2,1)S(1)} %row_sum.8), channel_id=1, source_target_pairs={{0,4},{1,9},{2,6},{3,11},{4,0},{5,13},{6,2},{7,15},{8,12},{9,1},{1... | collective-permute-start | bytes 294920 | tf_op jit(solution)/shard_map/ppermute | solution.py:400
  17.1 1.0 %keep_half.1.kept = bf16[512,768]{1,0:T(8,128)(2,1)S(1)} custom-call(bf16[1024,768]{1,0:T(8,128)(2,1)S(1)} %get-tuple-element.37.embed, bf16[512,256]{1,0:T(8,128)(2,1)S(1)} %get-tuple-element.28.refs_0_, bf16[512,256]{1,0:T(8,128)(2,1)S(1)} %get-tuple-element.43.refs_1_, bf16[512,256]{1,0:T(8,128)(2,1)S(1)} %get-tuple-element.44.refs_2_, ...), custom_call_target="tpu_custom_call" | custom-call | tf_op jit(solution)/shard_map/keep_half/pallas_call | solution.py:435
  18.2 0.5 %collective-permute-start.6 = (bf16[1,1,64,768]{3,2,1,0:T(8,128)(2,1)S(1)}, bf16[1,1,64,768]{3,2,1,0:T(8,128)(2,1)S(1)}, u32[]{:S(2)}, u32[]{:S(2)}) collective-permute-start(bf16[1,1,64,768]{3,2,1,0:T(8,128)(2,1)S(1)} %row_sum.7), channel_id=1, source_target_pairs={{0,4},{1,9},{2,6},{3,11},{4,0},{5,13},{6,2},{7,15},{8,12},{9,1},{1... | collective-permute-start | bytes 294920 | tf_op jit(solution)/shard_map/ppermute | solution.py:400
  18.7 0.2 collective-permute-done.3.refs_2_
  18.9 0.0 collective-permute-done.2.refs_1_
  18.9 2.0 %collective-permute-done.7.refs_3_ = bf16[1,1,64,768]{3,2,1,0:T(8,128)(2,1)S(1)} collective-permute-done((bf16[1,1,64,768]{3,2,1,0:T(8,128)(2,1)S(1)}, bf16[1,1,64,768]{3,2,1,0:T(8,128)(2,1)S(1)}, u32[]{:S(2)}, u32[]{:S(2)}) %collective-permute-start.7) | collective-permute-done | bytes 98336 | tf_op jit(solution)/shard_map/ppermute | solution.py:400
  20.9 0.1 row_sum.9
  21.0 2.2 %collective-permute-start.8 = (bf16[1,1,64,768]{3,2,1,0:T(8,128)(2,1)S(1)}, bf16[1,1,64,768]{3,2,1,0:T(8,128)(2,1)S(1)}, u32[]{:S(2)}, u32[]{:S(2)}) collective-permute-start(bf16[1,1,64,768]{3,2,1,0:T(8,128)(2,1)S(1)} %row_sum.9), channel_id=1, source_target_pairs={{0,8},{1,3},{2,10},{3,1},{4,12},{5,7},{6,14},{7,5},{8,0},{9,11},{1... | collective-permute-start | bytes 294920 | tf_op jit(solution)/shard_map/ppermute | solution.py:400
  23.2 3.5 %collective-permute-done.1.got = bf16[512,768]{1,0:T(8,128)(2,1)S(1)} collective-permute-done((bf16[512,768]{1,0:T(8,128)(2,1)S(1)}, bf16[512,768]{1,0:T(8,128)(2,1)S(1)}, u32[]{:S(2)}, u32[]{:S(2)}) %collective-permute-start.1) | collective-permute-done | bytes 786464 | tf_op jit(solution)/shard_map/ppermute | solution.py:290
  26.8 0.1 half_sum.1.summed
  26.8 0.0 collective-permute-done.6.refs_3_
  26.9 0.0 collective-permute-done.8.refs_4_
  26.9 0.9 %finish.1 = (bf16[64,768]{1,0:T(8,128)(2,1)}, bf16[512,768]{1,0:T(8,128)(2,1)}) custom-call(bf16[512,768]{1,0:T(8,128)(2,1)S(1)} %keep_half.1.kept, bf16[512,768]{1,0:T(8,128)(2,1)S(1)} %collective-permute-done.1.got, bf16[256,768]{1,0:T(8,128)(2,1)S(1)} %half_sum.1.summed, bf16[4,1,64,768]{3,2,1,0:T(8,128)(2,1)S(1)} %get-tuple-element.47.refs_0_, ...), custom_call_target="tpu_custom_call" | custom-call | tf_op jit(solution)/shard_map/finish/pallas_call | solution.py:467
  (4 shorter events, 0.2 us)
Async XLA Ops:
  3.8 4.7 %collective-permute-start = (bf16[4,1,64,768]{3,2,1,0:T(8,128)(2,1)S(1)}, bf16[4,1,64,768]{3,2,1,0:T(8,128)(2,1)S(1)}, u32[]{:S(2)}, u32[]{:S(2)}) collective-permute-start(bf16[4,1,64,768]{3,2,1,0:T(8,128)(2,1)S(1)} %get-tuple-element.29), channel_id=1, source_target_pairs={{0,1},{1,0},{2,3},{3,2},{4,5},{5,4},{6,7},{7,6},{8,9},{9,8},{10,11... | collective-permute-start | bytes 1179656 | tf_op jit(solution)/shard_map/ppermute | solution.py:290
  6.0 20.8 %collective-permute-start.1 = (bf16[512,768]{1,0:T(8,128)(2,1)S(1)}, bf16[512,768]{1,0:T(8,128)(2,1)S(1)}, u32[]{:S(2)}, u32[]{:S(2)}) collective-permute-start(bf16[512,768]{1,0:T(8,128)(2,1)S(1)} %get-tuple-element.46), channel_id=1, source_target_pairs={{0,16},{16,0},{1,17},{17,1},{2,18},{18,2},{3,19},{19,3},{4,20},{20... | collective-permute-start | bytes 2359304 | tf_op jit(solution)/shard_map/ppermute | solution.py:290
  9.7 5.7 %collective-permute-start.5 = (bf16[2,1,64,768]{3,2,1,0:T(8,128)(2,1)S(1)}, bf16[2,1,64,768]{3,2,1,0:T(8,128)(2,1)S(1)}, u32[]{:S(2)}, u32[]{:S(2)}) collective-permute-start(bf16[2,1,64,768]{3,2,1,0:T(8,128)(2,1)S(1)} %row_sum.6), channel_id=1, source_target_pairs={{0,2},{1,5},{2,0},{3,7},{4,6},{5,1},{6,4},{7,3},{8,10},{9,13},{10,... | collective-permute-start | bytes 589832 | tf_op jit(solution)/shard_map/ppermute | solution.py:400
  13.0 2.4 %collective-permute-start.4 = (bf16[2,1,64,768]{3,2,1,0:T(8,128)(2,1)S(1)}, bf16[2,1,64,768]{3,2,1,0:T(8,128)(2,1)S(1)}, u32[]{:S(2)}, u32[]{:S(2)}) collective-permute-start(bf16[2,1,64,768]{3,2,1,0:T(8,128)(2,1)S(1)} %get-tuple-element.51), channel_id=1, source_target_pairs={{0,1},{1,0},{2,3},{3,2},{4,5},{5,4},{6,7},{7,6},{8,9},{9,8},{10,11... | collective-permute-start | bytes 589832 | tf_op jit(solution)/shard_map/ppermute | solution.py:290
  13.1 5.7 %collective-permute-start.3 = (bf16[2,1,64,768]{3,2,1,0:T(8,128)(2,1)S(1)}, bf16[2,1,64,768]{3,2,1,0:T(8,128)(2,1)S(1)}, u32[]{:S(2)}, u32[]{:S(2)}) collective-permute-start(bf16[2,1,64,768]{3,2,1,0:T(8,128)(2,1)S(1)} %row_sum.5), channel_id=1, source_target_pairs={{0,2},{1,5},{2,0},{3,7},{4,6},{5,1},{6,4},{7,3},{8,10},{9,13},{10,... | collective-permute-start | bytes 589832 | tf_op jit(solution)/shard_map/ppermute | solution.py:400
  14.7 4.2 %collective-permute-start.2 = (bf16[2,1,64,768]{3,2,1,0:T(8,128)(2,1)S(1)}, bf16[2,1,64,768]{3,2,1,0:T(8,128)(2,1)S(1)}, u32[]{:S(2)}, u32[]{:S(2)}) collective-permute-start(bf16[2,1,64,768]{3,2,1,0:T(8,128)(2,1)S(1)} %get-tuple-element.48), channel_id=1, source_target_pairs={{0,1},{1,0},{2,3},{3,2},{4,5},{5,4},{6,7},{7,6},{8,9},{9,8},{10,11... | collective-permute-start | bytes 589832 | tf_op jit(solution)/shard_map/ppermute | solution.py:290
  15.5 5.4 %collective-permute-start.7 = (bf16[1,1,64,768]{3,2,1,0:T(8,128)(2,1)S(1)}, bf16[1,1,64,768]{3,2,1,0:T(8,128)(2,1)S(1)}, u32[]{:S(2)}, u32[]{:S(2)}) collective-permute-start(bf16[1,1,64,768]{3,2,1,0:T(8,128)(2,1)S(1)} %row_sum.8), channel_id=1, source_target_pairs={{0,4},{1,9},{2,6},{3,11},{4,0},{5,13},{6,2},{7,15},{8,12},{9,1},{1... | collective-permute-start | bytes 294920 | tf_op jit(solution)/shard_map/ppermute | solution.py:400
  18.2 8.7 %collective-permute-start.6 = (bf16[1,1,64,768]{3,2,1,0:T(8,128)(2,1)S(1)}, bf16[1,1,64,768]{3,2,1,0:T(8,128)(2,1)S(1)}, u32[]{:S(2)}, u32[]{:S(2)}) collective-permute-start(bf16[1,1,64,768]{3,2,1,0:T(8,128)(2,1)S(1)} %row_sum.7), channel_id=1, source_target_pairs={{0,4},{1,9},{2,6},{3,11},{4,0},{5,13},{6,2},{7,15},{8,12},{9,1},{1... | collective-permute-start | bytes 294920 | tf_op jit(solution)/shard_map/ppermute | solution.py:400
  21.0 5.9 %collective-permute-start.8 = (bf16[1,1,64,768]{3,2,1,0:T(8,128)(2,1)S(1)}, bf16[1,1,64,768]{3,2,1,0:T(8,128)(2,1)S(1)}, u32[]{:S(2)}, u32[]{:S(2)}) collective-permute-start(bf16[1,1,64,768]{3,2,1,0:T(8,128)(2,1)S(1)} %row_sum.9), channel_id=1, source_target_pairs={{0,8},{1,3},{2,10},{3,1},{4,12},{5,7},{6,14},{7,5},{8,0},{9,11},{1... | collective-permute-start | bytes 294920 | tf_op jit(solution)/shard_map/ppermute | solution.py:400
